TPU v7x, 256 devices: a whole 4x4x8 slice. The times are simulated.
256 devices in a mesh: seq: 128 (over x, y, z), head: 2 (over core).
Axes of the slice: x: 4, y: 4, z: 8, core: 2. Of those that a mesh axis runs over, the one named last changes fastest.
Arguments:
- queries: bfloat16 [16384, 4096], P('seq', 'head'), may hold values from -45 to 45
- key_states: bfloat16 [16384, 4096], P('seq', 'head'), may hold values from -6 to 6
- values: bfloat16 [16384, 4096], P('seq', 'head'), may hold values from -6 to 6
- out_grad: bfloat16 [16384, 4096], P('seq', 'head'), may hold values from -6 to 6
- rand_blocks: int32 [256, 32, 3], P(None, 'head'), may hold values from 0 to 255, as said below
Outputs:
- attended: bfloat16 [16384, 4096], P('seq', 'head')
- query_grad: bfloat16 [16384, 4096], P('seq', 'head')
- key_grad: bfloat16 [16384, 4096], P('seq', 'head')
- value_grad: bfloat16 [16384, 4096], P('seq', 'head')
Inputs may be any that keep to these rules, and one draw needn't show every extreme that they name: `rand_blocks`: for every query block i and head the three entries are different blocks; none lies on the seq shard (of 2 blocks) of block 0 or of block 255, nor on the shard of block i. Over the query blocks of one seq shard and the heads of one head shard, the blocks of any one seq shard are named at most 1 times, and some shard's blocks exactly 1 times.
All inputs are finite; a program needn't handle non-finite values.
Results may differ from a plain program's by a relative error of at most 0.028.
Values may be sent and summed in bfloat16 or wider, within the bound.
No kernel may reach another device: no remote copies, remote signals or barrier semaphores. Data moves between devices by JAX's collectives and lax.ppermute only.
A program may use at most 128 MiB of HBM per device.

v0:
```python
import math

import jax
import jax.numpy as jnp
from jax import lax
from jax.sharding import PartitionSpec as P

DH = 128
BLOCK = 64


def with_halo(cells, sides, width):
    for axis, dim in sides:
        count = lax.axis_size(axis)
        ends = count - 1
        head = lax.slice_in_dim(cells, 0, width, axis=dim)
        tail = lax.slice_in_dim(cells, cells.shape[dim] - width, cells.shape[dim], axis=dim)
        cells = jnp.concatenate(
            [
                lax.ppermute(tail, axis, [(i, (i + 1) % count) for i in range(ends)]),
                cells,
                lax.ppermute(head, axis, [((i + 1) % count, i) for i in range(ends)]),
            ],
            axis=dim,
        )
    return cells


def from_root(value, axis, source):
    kept = jnp.where(lax.axis_index(axis) == source, value, 0).astype(value.dtype)
    return lax.psum(kept, axis)


def from_behind(block, axis, distance):
    devices = range(lax.axis_size(axis))
    route = [(i - distance, i) for i in devices if i - distance in devices]
    return lax.ppermute(block, axis, route)


def split_heads(flat_rows, head_count):
    block_count = flat_rows.shape[0] // BLOCK
    return flat_rows.reshape(block_count, BLOCK, head_count, DH).transpose(2, 0, 1, 3)


def merge_heads(arranged):
    head_count, block_count = (arranged.shape[0], arranged.shape[1])
    return arranged.transpose(1, 2, 0, 3).reshape(block_count * BLOCK, head_count * DH)


def plan_routes(rand_blocks, block_count, head_count, shard_count, shard_index):
    request_count = 3 * block_count * head_count
    slot_room = (request_count + shard_count - 4) // (shard_count - 3)
    block_table = rand_blocks.reshape(shard_count, request_count)
    owners = block_table // block_count
    item_codes = (
        block_table % block_count * head_count + jnp.arange(request_count) // 3 % head_count
    )
    mine_owners = lax.dynamic_slice_in_dim(owners, shard_index, 1, 0)[0]
    peer_ids = jnp.arange(shard_count)
    owner_hits = (mine_owners[:, None] == peer_ids[None, :]).astype(jnp.int32)
    slot_rank = jnp.sum(jnp.cumsum(owner_hits, axis=0) * owner_hits, axis=1) - 1
    target = mine_owners * slot_room + slot_rank
    for_me = (owners == shard_index).astype(jnp.int32)
    arrival_rank = jnp.cumsum(for_me, axis=1) - 1
    slot_match = (for_me[:, None, :] == 1) & (
        arrival_rank[:, None, :] == jnp.arange(slot_room)[None, :, None]
    )
    filled = jnp.any(slot_match, axis=2).reshape(-1)
    source = jnp.sum(jnp.where(slot_match, item_codes[:, None, :], 0), axis=2).reshape(-1)
    slot_ids = jnp.arange(shard_count * slot_room)
    back_match = target[None, :] == slot_ids[:, None]
    back_filled = jnp.any(back_match, axis=1)
    back_index = jnp.sum(jnp.where(back_match, jnp.arange(request_count)[None, :], 0), axis=1)
    return (target, source, filled, back_index, back_filled, slot_room)


def block_pairs(key_value, head_count):
    block_count = key_value.shape[1] // BLOCK
    arranged = key_value.reshape(2, block_count, BLOCK, head_count, DH).transpose(1, 3, 0, 2, 4)
    return arranged.reshape(block_count * head_count, 2, BLOCK, DH)


def outgoing_blocks(key_value, head_count, routes, shard_count):
    target, source, filled, back_index, back_filled, slot_room = routes
    item_pairs = block_pairs(key_value, head_count)
    return item_pairs[source].reshape(shard_count, slot_room, 2, BLOCK, DH)


def place_arrived(arrived, key_value, head_count, routes, shard_count):
    target, source, filled, back_index, back_filled, slot_room = routes
    picked = arrived.reshape(shard_count * slot_room, 2, BLOCK, DH)[target]
    block_count = key_value.shape[1] // BLOCK
    picked = picked.reshape(block_count, head_count, 3, 2, BLOCK, DH).transpose(3, 1, 0, 2, 4, 5)
    return picked.reshape(2, head_count, block_count, 3 * BLOCK, DH)


def on_device(queries, key_states, values, out_grad, rand_blocks):
    head_count = queries.shape[1] // DH
    block_count = queries.shape[0] // BLOCK
    shard_count = lax.axis_size("seq")
    shard_index = lax.axis_index("seq")
    score_scale = 1.0 / math.sqrt(DH)
    key_value = jnp.stack([key_states, values])
    routes = plan_routes(rand_blocks, block_count, head_count, shard_count, shard_index)
    padded = with_halo(key_value, (("seq", 1),), BLOCK)
    lined = padded.reshape(2, block_count + 2, BLOCK, head_count, DH).transpose(0, 3, 1, 2, 4)
    window = jnp.concatenate(
        [
            lined[:, :, 0:block_count],
            lined[:, :, 1 : block_count + 1],
            lined[:, :, 2 : block_count + 2],
        ],
        axis=3,
    )
    end_blocks = []
    for root_shard, edge_piece in (
        (0, key_value[:, :BLOCK]),
        (shard_count - 1, key_value[:, -BLOCK:]),
    ):
        end_blocks.append(from_root(edge_piece, "seq", root_shard))
    global_pair = (
        jnp.concatenate(end_blocks, axis=1)
        .reshape(2, 2 * BLOCK, head_count, DH)
        .transpose(0, 2, 1, 3)
    )
    global_pair = jnp.broadcast_to(
        global_pair[:, :, None], (2, head_count, block_count, 2 * BLOCK, DH)
    )
    sending = outgoing_blocks(key_value, head_count, routes, shard_count)
    arrived_first = lax.all_to_all(sending, "seq", split_axis=0, concat_axis=0, tiled=True)
    distant = place_arrived(arrived_first, key_value, head_count, routes, shard_count)
    gathered = jnp.concatenate([window, global_pair, distant], axis=3)
    query_block = shard_index * block_count + jnp.arange(block_count)
    block_total = shard_count * block_count
    always = query_block >= 0
    allowed = jnp.stack(
        [
            query_block >= 1,
            always,
            query_block + 1 < block_total,
            query_block >= 2,
            query_block <= block_total - 3,
            always,
            always,
            always,
        ],
        axis=1,
    )
    allowed = jnp.repeat(allowed, BLOCK, axis=1)
    query_heads = split_heads(queries, head_count)
    scores = (
        jnp.einsum("hlqd,hlkd->hlqk", query_heads, gathered[0], preferred_element_type=jnp.float32)
        * score_scale
    )
    scores = jnp.where(allowed[None, :, None, :], scores, -jnp.inf)
    row_max = jnp.max(scores, axis=-1, keepdims=True)
    log_total = row_max + jnp.log(jnp.sum(jnp.exp(scores - row_max), axis=-1, keepdims=True))
    weights = jnp.exp(scores - log_total)
    weights_low = weights.astype(jnp.bfloat16)
    out_heads = jnp.einsum(
        "hlqk,hlkd->hlqd", weights_low, gathered[1], preferred_element_type=jnp.float32
    ).astype(jnp.bfloat16)
    grad_heads = split_heads(out_grad, head_count)
    row_dot = jnp.sum(grad_heads.astype(jnp.float32) * out_heads.astype(jnp.float32), axis=-1)
    weight_grads = jnp.einsum(
        "hlqd,hlkd->hlqk", grad_heads, gathered[1], preferred_element_type=jnp.float32
    )
    score_grads = (weights * (weight_grads - row_dot[..., None]) * score_scale).astype(jnp.bfloat16)
    query_grad_heads = jnp.einsum(
        "hlqk,hlkd->hlqd", score_grads, gathered[0], preferred_element_type=jnp.float32
    ).astype(jnp.bfloat16)

    def block_terms(low_col, high_col):
        key_part = jnp.einsum(
            "hlqk,hlqd->hlkd",
            score_grads[..., low_col:high_col],
            query_heads,
            preferred_element_type=jnp.float32,
        )
        value_part = jnp.einsum(
            "hlqk,hlqd->hlkd",
            weights_low[..., low_col:high_col],
            grad_heads,
            preferred_element_type=jnp.float32,
        )
        return jnp.stack([key_part, value_part])

    window_span = 3 * BLOCK
    near_terms = block_terms(0, window_span).reshape(2, head_count, block_count, 3, BLOCK, DH)
    grid_pad = ((0, 0), (0, 0), (0, 2), (0, 0), (0, 0))
    mid_pad = ((0, 0), (0, 0), (1, 1), (0, 0), (0, 0))
    high_pad = ((0, 0), (0, 0), (2, 0), (0, 0), (0, 0))
    window_grid = (
        jnp.pad(near_terms[:, :, :, 0], grid_pad)
        + jnp.pad(near_terms[:, :, :, 1], mid_pad)
        + jnp.pad(near_terms[:, :, :, 2], high_pad)
    )
    key_grads = window_grid[:, :, 1 : block_count + 1]
    global_terms = jnp.sum(block_terms(window_span, window_span + 2 * BLOCK), axis=2)
    global_sum = lax.psum(global_terms, "seq")
    first_add = jnp.where(shard_index == 0, global_sum[:, :, :BLOCK], 0.0)
    last_add = jnp.where(shard_index == shard_count - 1, global_sum[:, :, BLOCK:], 0.0)
    key_grads = key_grads.at[:, :, 0].add(first_add).at[:, :, block_count - 1].add(last_add)
    target, source, filled, back_index, back_filled, slot_room = routes
    random_terms = block_terms(window_span + 2 * BLOCK, 8 * BLOCK).astype(jnp.bfloat16)
    random_terms = random_terms.reshape(2, head_count, block_count, 3, BLOCK, DH)
    per_request = random_terms.transpose(2, 1, 3, 0, 4, 5).reshape(
        block_count * head_count * 3, 2, BLOCK, DH
    )
    outgoing = jnp.where(
        back_filled[:, None, None, None], per_request[back_index], jnp.zeros((), jnp.bfloat16)
    )
    outgoing = outgoing.reshape(shard_count, slot_room, 2, BLOCK, DH)
    returned = lax.all_to_all(outgoing, "seq", split_axis=0, concat_axis=0, tiled=True).reshape(
        shard_count * slot_room, 2 * BLOCK * DH
    )
    selector = (
        (source[:, None] == jnp.arange(block_count * head_count)[None, :]) & filled[:, None]
    ).astype(jnp.bfloat16)
    summed = jnp.dot(selector.T, returned, preferred_element_type=jnp.float32)
    summed = summed.reshape(block_count, head_count, 2, BLOCK, DH).transpose(2, 1, 0, 3, 4)
    key_grads = key_grads + summed
    for offset_by, edge_piece in (
        (-1, window_grid[:, :, 0]),
        (1, window_grid[:, :, block_count + 1]),
    ):
        arrived = from_behind(edge_piece.astype(jnp.bfloat16), "seq", offset_by).astype(
            edge_piece.dtype
        )
        target_block = block_count - 1 if offset_by == -1 else 0
        key_grads = key_grads.at[:, :, target_block].add(arrived)
    attended = merge_heads(out_heads)
    query_grad = merge_heads(query_grad_heads)
    key_grad = merge_heads(key_grads[0].astype(jnp.bfloat16))
    value_grad = merge_heads(key_grads[1].astype(jnp.bfloat16))
    return (attended, query_grad, key_grad, value_grad)


def solution(mesh):
    placed = (
        P("seq", "head"),
        P("seq", "head"),
        P("seq", "head"),
        P("seq", "head"),
        P(None, "head", None),
    )
    return jax.shard_map(
        on_device,
        mesh=mesh,
        in_specs=placed,
        out_specs=(P("seq", "head"), P("seq", "head"), P("seq", "head"), P("seq", "head")),
        check_vma=False,
    )
```

profile of v0, /device:TPU:6, one launch (start us, length us, event | category | flops | bytes accessed | tf_op | source)
XLA Modules:
  0.0 598.6 jit_solution(5751157082968911438)
XLA Ops:
  7.2 2.1 copy.64
  9.3 1.6 reshape.580
  10.9 1.6 reshape.579
  14.8 3.0 gather_fusion
  17.9 16.4 %all-to-all-start = ((bf16[128,1,2,64,128]{4,3,2,1,0:T(8,128)(2,1)}), bf16[128,1,2,64,128]{4,3,2,1,0:T(8,128)(2,1)}, u32[]{:S(2)}, u32[]{:S(2)}) async-start(bf16[128,1,2,64,128]{4,3,2,1,0:T(8,128)(2,1)} %bitcast.222), calls=%async_computation | async-start | bytes 8388608 | tf_op jit(solution)/shard_map/all_to_all | solution.py:130
  34.3 1.3 broadcast_select_fusion
  35.6 7.0 %collective-permute-start.1 = (bf16[2,64,2048]{2,1,0:T(8,128)(2,1)S(1)}, bf16[2,64,2048]{2,1,0:T(8,128)(2,1)}, u32[]{:S(2)}, u32[]{:S(2)}) collective-permute-start(bf16[2,64,2048]{2,1,0:T(8,128)(2,1)S(1)} %get-tuple-element.70), channel_id=1, source_target_pairs={{2,0},{4,2},{6,4},{8,6},{10,8},{12,10},{14,12},{16,14},{18,16},{20... | collective-permute-start | bytes 1572872 | tf_op jit(solution)/shard_map/ppermute | solution.py:22
  42.6 2.1 collective-permute-start
  47.0 94.6 %collective-permute-done.1 = bf16[2,64,2048]{2,1,0:T(8,128)(2,1)} collective-permute-done((bf16[2,64,2048]{2,1,0:T(8,128)(2,1)S(1)}, bf16[2,64,2048]{2,1,0:T(8,128)(2,1)}, u32[]{:S(2)}, u32[]{:S(2)}) %collective-permute-start.1) | collective-permute-done | bytes 524320 | tf_op jit(solution)/shard_map/ppermute | solution.py:22
  141.5 3.6 collective-permute-done
  145.1 1.4 pad_maximum_fusion.1
  147.7 1.2 slice_dynamic-update-slice_fusion.2
  149.0 1.3 slice_dynamic-update-slice_fusion.1
  150.2 1.2 slice_dynamic-update-slice_fusion
  151.4 126.6 %all-reduce.9.cloned.1.call-done = (bf16[2,64,2048]{2,1,0:T(8,128)(2,1)}, bf16[2,64,2048]{2,1,0:T(8,128)(2,1)}) async-done(((bf16[2,64,2048]{2,1,0:T(8,128)(2,1)}, bf16[2,64,2048]{2,1,0:T(8,128)(2,1)}), (bf16[2,64,2048]{2,1,0:T(8,128)(2,1)}, bf16[2,64,2048]{2,1,0:T(8,128)(2,1)})) %all-reduce.9.cloned.1.call-update) | async-done | bytes 1048592 | tf_op jit(solution)/shard_map/psum | solution.py:31
  278.0 1.5 bitcast_bitcast_fusion
  279.5 1.8 broadcast_dynamic-update-slice_fusion
  281.4 3.3 gather_fusion.1
  284.7 1.0 copy.75
  285.7 2.5 constant_dynamic-update-slice_fusion
  288.3 3.9 bitcast_reduce_fusion
  292.1 1.3 fusion.6
  294.5 4.5 multiply_reduce_fusion
  299.0 1.3 convolution_convert_fusion
  300.3 3.8 fusion.4
  304.2 1.5 convolution_convert_fusion.1
  306.0 1.0 copy.89
  307.0 3.0 gather_fusion.2
  310.0 4.5 fusion.2
  314.5 11.0 %all-to-all-start.1 = ((bf16[128,1,2,64,128]{4,3,2,1,0:T(8,128)(2,1)}), bf16[128,1,2,64,128]{4,3,2,1,0:T(8,128)(2,1)}, u32[]{:S(2)}, u32[]{:S(2)}) async-start(bf16[128,1,2,64,128]{4,3,2,1,0:T(8,128)(2,1)} %fusion.2), calls=%async_computation.1 | async-start | bytes 8388608 | tf_op jit(solution)/shard_map/all_to_all | solution.py:214
  325.6 1.0 convolution_bitcast_fusion
  326.6 2.2 convolution_bitcast_fusion.1
  329.3 2.5 copy.82
  331.9 3.8 fusion.17
  336.7 0.9 copy.148
  338.0 0.9 copy.147
  339.6 1.8 copy_dynamic-update-slice_fusion.1
  341.4 1.8 copy_dynamic-update-slice_fusion
  344.8 1.9 copy-done
  346.8 1.1 slice_bitcast_fusion.17
  348.0 7.0 %collective-permute-start.2 = (bf16[2,16,64,128]{3,1,2,0:T(8,128)(2,1)}, bf16[2,16,64,128]{3,1,2,0:T(8,128)(2,1)S(1)}, u32[]{:S(2)}, u32[]{:S(2)}) collective-permute-start(bf16[2,16,64,128]{3,1,2,0:T(8,128)(2,1)} %get-tuple-element.66), channel_id=1, source_target_pairs={{2,0},{4,2},{6,4},{8,6},{10,8},{12,10},{14,12},{16,14},{18,16},{20... | collective-permute-start | bytes 1572872 | tf_op jit(solution)/shard_map/ppermute | solution.py:37
  355.0 2.2 collective-permute-start.3
  357.1 217.9 %all-reduce.7.cloned.1.call-done = f32[2,16,128,128]{3,1,2,0:T(8,128)} async-done(((f32[2,16,128,128]{3,1,2,0:T(8,128)}), f32[2,16,128,128]{3,1,2,0:T(8,128)}) %all-reduce.7.cloned.1.call-update) | async-done | bytes 2097168 | tf_op jit(solution)/shard_map/psum | solution.py:200
  575.1 1.7 fusion.27
  576.8 1.5 fusion.24
  578.3 6.6 %copy.90 = bf16[128,1,2,64,128]{0,4,3,2,1:T(8,128)(2,1)} copy(bf16[128,1,2,64,128]{4,3,2,1,0:T(8,128)(2,1)} %all-to-all-done.1) | data formatting | bytes 8388608 | tf_op jit(solution)/shard_map/reshape | solution.py:214
  584.9 3.7 bitcast_add_fusion
  589.4 0.9 copy.146
  (88 shorter events, 12.7 us)
Async XLA Ops:
  7.2 5.5 copy-start.7
  7.2 5.6 copy-start.8
  17.9 263.5 %all-to-all-start = ((bf16[128,1,2,64,128]{4,3,2,1,0:T(8,128)(2,1)}), bf16[128,1,2,64,128]{4,3,2,1,0:T(8,128)(2,1)}, u32[]{:S(2)}, u32[]{:S(2)}) async-start(bf16[128,1,2,64,128]{4,3,2,1,0:T(8,128)(2,1)} %bitcast.222), calls=%async_computation | async-start | bytes 8388608 | tf_op jit(solution)/shard_map/all_to_all | solution.py:130
  34.3 10.5 %copy-start.11 = (bf16[128,2048]{1,0:T(8,128)(2,1)S(1)}, bf16[128,2048]{1,0:T(8,128)(2,1)}, u32[]{:S(2)}) copy-start(bf16[128,2048]{1,0:T(8,128)(2,1)} %param.16) | copy-start | bytes 1572868
  34.3 11.7 %copy-start.12 = (bf16[128,2048]{1,0:T(8,128)(2,1)S(1)}, bf16[128,2048]{1,0:T(8,128)(2,1)}, u32[]{:S(2)}) copy-start(bf16[128,2048]{1,0:T(8,128)(2,1)} %param.13) | copy-start | bytes 1572868
  34.3 243.7 %all-reduce.9.cloned.1.call-start = ((), (), s32[]{:S(2)}) async-start(), calls=%async_computation.3 | async-start | bytes 2097152 | tf_op jit(solution)/shard_map/psum | solution.py:31
  35.6 105.9 %collective-permute-start.1 = (bf16[2,64,2048]{2,1,0:T(8,128)(2,1)S(1)}, bf16[2,64,2048]{2,1,0:T(8,128)(2,1)}, u32[]{:S(2)}, u32[]{:S(2)}) collective-permute-start(bf16[2,64,2048]{2,1,0:T(8,128)(2,1)S(1)} %get-tuple-element.70), channel_id=1, source_target_pairs={{2,0},{4,2},{6,4},{8,6},{10,8},{12,10},{14,12},{16,14},{18,16},{20... | collective-permute-start | bytes 1572872 | tf_op jit(solution)/shard_map/ppermute | solution.py:22
  42.6 102.5 %collective-permute-start = (bf16[2,64,2048]{2,1,0:T(8,128)(2,1)S(1)}, bf16[2,64,2048]{2,1,0:T(8,128)(2,1)}, u32[]{:S(2)}, u32[]{:S(2)}) collective-permute-start(bf16[2,64,2048]{2,1,0:T(8,128)(2,1)S(1)} %get-tuple-element.61), channel_id=1, source_target_pairs={{0,2},{2,4},{4,6},{6,8},{8,10},{10,12},{12,14},{14,16},{16,18},{18... | collective-permute-start | bytes 1572872 | tf_op jit(solution)/shard_map/ppermute | solution.py:20
  285.7 2.6 copy-start.5
  293.4 1.0 copy-start.3
  294.3 6.0 %copy-start.1 = (bf16[16,2,64,512]{3,2,1,0:T(8,128)(2,1)}, bf16[16,2,64,512]{3,2,1,0:T(8,128)(2,1)S(1)}, u32[]{:S(2)}) copy-start(bf16[16,2,64,512]{3,2,1,0:T(8,128)(2,1)S(1)} %fusion.8) | copy-start | bytes 6291460
  304.1 1.8 copy-start.9
  314.5 11.1 %copy-start.2 = (bf16[16,2,64,512]{3,2,1,0:T(8,128)(2,1)S(1)}, bf16[16,2,64,512]{3,2,1,0:T(8,128)(2,1)}, u32[]{:S(2)}) copy-start(bf16[16,2,64,512]{3,2,1,0:T(8,128)(2,1)} %copy-done.1) | copy-start | bytes 6291460
  314.5 11.1 %copy-start.4 = (bf16[16,8,16,128]{3,2,1,0:T(8,128)(2,1)S(1)}, bf16[16,8,16,128]{3,2,1,0:T(8,128)(2,1)}, u32[]{:S(2)}) copy-start(bf16[16,8,16,128]{3,2,1,0:T(8,128)(2,1)} %copy.97) | copy-start | bytes 1572868
  314.5 12.1 %copy-start.6 = (bf16[16,8,16,128]{3,2,1,0:T(8,128)(2,1)S(1)}, bf16[16,8,16,128]{3,2,1,0:T(8,128)(2,1)}, u32[]{:S(2)}) copy-start(bf16[16,8,16,128]{3,2,1,0:T(8,128)(2,1)} %copy.95) | copy-start | bytes 1572868
  314.5 263.8 %all-to-all-start.1 = ((bf16[128,1,2,64,128]{4,3,2,1,0:T(8,128)(2,1)}), bf16[128,1,2,64,128]{4,3,2,1,0:T(8,128)(2,1)}, u32[]{:S(2)}, u32[]{:S(2)}) async-start(bf16[128,1,2,64,128]{4,3,2,1,0:T(8,128)(2,1)} %fusion.2), calls=%async_computation.1 | async-start | bytes 8388608 | tf_op jit(solution)/shard_map/all_to_all | solution.py:214
  325.5 249.6 %all-reduce.7.cloned.1.call-start = ((), (), s32[]{:S(2)}) async-start(), calls=%async_computation.2 | async-start | bytes 4194304 | tf_op jit(solution)/shard_map/psum | solution.py:200
  331.9 3.9 copy-start.10
  331.9 4.5 copy-start.13
  344.8 1.9 copy-start
  348.0 240.7 %collective-permute-start.2 = (bf16[2,16,64,128]{3,1,2,0:T(8,128)(2,1)}, bf16[2,16,64,128]{3,1,2,0:T(8,128)(2,1)S(1)}, u32[]{:S(2)}, u32[]{:S(2)}) collective-permute-start(bf16[2,16,64,128]{3,1,2,0:T(8,128)(2,1)} %get-tuple-element.66), channel_id=1, source_target_pairs={{2,0},{4,2},{6,4},{8,6},{10,8},{12,10},{14,12},{16,14},{18,16},{20... | collective-permute-start | bytes 1572872 | tf_op jit(solution)/shard_map/ppermute | solution.py:37
  355.0 233.9 %collective-permute-start.3 = (bf16[2,16,64,128]{3,1,2,0:T(8,128)(2,1)}, bf16[2,16,64,128]{3,1,2,0:T(8,128)(2,1)S(1)}, u32[]{:S(2)}, u32[]{:S(2)}) collective-permute-start(bf16[2,16,64,128]{3,1,2,0:T(8,128)(2,1)} %get-tuple-element.65), channel_id=1, source_target_pairs={{0,2},{2,4},{4,6},{6,8},{8,10},{10,12},{12,14},{14,16},{16,18},{18... | collective-permute-start | bytes 1572872 | tf_op jit(solution)/shard_map/ppermute | solution.py:37
Sparse Core Ops, SparseCore 0:
  44.8 233.1 all-reduce.8
  332.0 243.0 all-reduce.6
where the time goes:
time: 606 us; the launch traced here: 599 us
  waiting for transfers between devices  443 us (73%)
  local copies, waits for them, and re-layouts  50.6 us (8%)
  starting transfers between devices  45.6 us (8%)
  matrix products  27.1 us (4%)
  other arithmetic  17.3 us (3%)
  between operations  15.1 us (2%)
    psum x1, waiting for transfers between devices, on_device(): global_sum = lax.psum(global_terms, 'seq')  218 us
    psum x1, waiting for transfers between devices, from_root(): return lax.psum(kept, axis)  127 us
    ppermute x1, waiting for transfers between devices, with_halo(): lax.ppermute(head, axis, [((i + 1) % count, i) for i in range(ends)])  94.6 us
    unnamed x43, local copies, waits for them, and re-layouts  17.9 us
    all_to_all x1, starting transfers between devices, on_device(): lax.all_to_all(sending, 'seq', split_axis=0, concat_axis=0, tiled=True)  16.4 us
  transfers between devices with their start and end apart: 8, of which 4 were waited for; matrix products, arithmetic and copies ran while one was open for 8% of the time, Pallas kernels for 0%

commit v1 on v0

v1 whole, which is shorter than its diff:
```python
import math

import jax
import jax.numpy as jnp
from jax import lax
from jax.experimental import pallas as pl
from jax.experimental.pallas import tpu as pltpu
from jax.sharding import PartitionSpec as P

DH = 128
BLOCK = 64
HEADS = 16
SHARDS = 128
LAST = SHARDS - 1
PICKS = 3 * HEADS
NX, NY, NZ = 4, 4, 8
VMEM_BYTES = 48 * 2**20
MASKED = -1e30
SCALE = 1.0 / math.sqrt(DH)
EXP2_SCALE = SCALE * math.log2(math.e)
BF16 = jnp.bfloat16
F32 = jnp.float32

IN_VMEM = pl.BlockSpec(memory_space=pltpu.VMEM)
IN_SMEM = pl.BlockSpec(memory_space=pltpu.SMEM)


def params():
    return pltpu.CompilerParams(vmem_limit_bytes=VMEM_BYTES)


def cost(flops, moved, exps=0):
    return pl.CostEstimate(flops=flops, bytes_accessed=moved, transcendentals=exps)


def lanes(head):
    return pl.ds(pl.multiple_of(head * DH, DH), DH)


def rows(block):
    return pl.ds(pl.multiple_of(block * BLOCK, BLOCK), BLOCK)


def nt(a, b):
    return lax.dot_general(a, b, (((1,), (1,)), ((), ())), preferred_element_type=F32)


def nn(a, b):
    return lax.dot_general(a, b, (((1,), (0,)), ((), ())), preferred_element_type=F32)


def tn(a, b):
    return lax.dot_general(a, b, (((0,), (0,)), ((), ())), preferred_element_type=F32)


def pack_kernel(item_ref, key_ref, value_ref, slots_ref, low_ref, high_ref):
    per_step = slots_ref.shape[0]
    step = pl.program_id(0)

    def one(slot, carry):
        item = item_ref[step * per_step + slot]
        block, head = item >> 4, item & 15
        slots_ref[slot, 0] = key_ref[rows(block), lanes(head)]
        slots_ref[slot, 1] = value_ref[rows(block), lanes(head)]
        return carry

    lax.fori_loop(0, per_step, one, 0, unroll=4)

    @pl.when(step == 0)
    def _():
        low_ref[0] = key_ref[:BLOCK]
        low_ref[1] = value_ref[:BLOCK]
        high_ref[0] = key_ref[BLOCK:]
        high_ref[1] = value_ref[BLOCK:]


def pack(items, key_states, values):
    steps = 8
    edge = jax.ShapeDtypeStruct((2, BLOCK, HEADS * DH), BF16)
    whole = pl.BlockSpec((2 * BLOCK, HEADS * DH), lambda i, items: (0, 0))
    edge_spec = pl.BlockSpec(edge.shape, lambda i, items: (0, 0, 0))
    return pl.pallas_call(
        pack_kernel,
        grid_spec=pltpu.PrefetchScalarGridSpec(
            num_scalar_prefetch=1,
            grid=(steps,),
            in_specs=[whole, whole],
            out_specs=[
                pl.BlockSpec((SHARDS // steps, 2, BLOCK, DH), lambda i, items: (i, 0, 0, 0)),
                edge_spec,
                edge_spec,
            ],
        ),
        out_shape=[jax.ShapeDtypeStruct((SHARDS, 2, BLOCK, DH), BF16), edge, edge],
        compiler_params=params(),
        cost_estimate=cost(0, 6 * 2**20),
        name="pack",
    )(items, key_states, values)


def attend_kernel(
    pick_ref,
    where_ref,
    query_ref,
    grad_ref,
    key_ref,
    value_ref,
    far_ref,
    prev_ref,
    next_ref,
    ends_ref,
    attended_ref,
    query_grad_ref,
    terms_ref,
    own_ref,
    prev_terms_ref,
    next_terms_ref,
    end_terms_ref,
):
    shard, my_x, my_y = where_ref[0], where_ref[1], where_ref[2]
    column = lax.broadcasted_iota(jnp.int32, (1, 4 * BLOCK), 1)
    at_first, at_last = shard == 0, shard == LAST
    no_end = (at_first & (column >= 2 * BLOCK) & (column < 3 * BLOCK)) | (
        at_last & (column >= 3 * BLOCK)
    )
    shared_bias = jnp.where(no_end, MASKED, 0.0)
    bias = [
        jnp.where(at_first & (column < BLOCK), MASKED, 0.0),
        jnp.where(at_last & (column < BLOCK), MASKED, 0.0),
    ]
    halves = [slice(0, BLOCK), slice(BLOCK, 2 * BLOCK)]

    def one(head, carry):
        at = lanes(head)
        head_x, head_y = head >> 2, head & 3
        end = ((my_x - head_x) & 3) * 4 + ((my_y - head_y) & 3)
        end_to = ((head_x - my_x) & 3) * 4 + ((head_y - my_y) & 3)
        query, grad = query_ref[:, at], grad_ref[:, at]
        shared_key = jnp.concatenate([key_ref[:, at], ends_ref[end, 0, 0], ends_ref[end, 1, 0]])
        shared_value = jnp.concatenate(
            [value_ref[:, at], ends_ref[end, 0, 1], ends_ref[end, 1, 1]]
        )
        owners = [
            [pick_ref[b * PICKS + head * 3 + r] >> 1 for r in range(3)] for b in range(2)
        ]
        edges = [prev_ref, next_ref]
        own_key = [
            jnp.concatenate([edges[b][0, :, at]] + [far_ref[o, 0] for o in owners[b]])
            for b in range(2)
        ]
        own_value = [
            jnp.concatenate([edges[b][1, :, at]] + [far_ref[o, 1] for o in owners[b]])
            for b in range(2)
        ]

        def both(of):
            return jnp.concatenate([of(0), of(1)])

        score_a = nt(query, shared_key) + shared_bias
        score_b = both(lambda b: nt(query[halves[b]], own_key[b]) + bias[b])
        top = jnp.max(jnp.maximum(score_a, score_b), axis=1, keepdims=True)
        exp_a = jnp.exp2((score_a - top) * EXP2_SCALE)
        exp_b = jnp.exp2((score_b - top) * EXP2_SCALE)
        inverse = 1.0 / jnp.sum(exp_a + exp_b, axis=1, keepdims=True)
        weight_a, weight_b = exp_a * inverse, exp_b * inverse
        low_a, low_b = weight_a.astype(BF16), weight_b.astype(BF16)
        attended = nn(low_a, shared_value) + both(lambda b: nn(low_b[halves[b]], own_value[b]))
        attended = attended.astype(BF16)
        attended_ref[:, at] = attended
        row_dot = jnp.sum(grad.astype(F32) * attended.astype(F32), axis=1, keepdims=True)
        wgrad_a = nt(grad, shared_value)
        wgrad_b = both(lambda b: nt(grad[halves[b]], own_value[b]))
        sgrad_a = (weight_a * (wgrad_a - row_dot) * SCALE).astype(BF16)
        sgrad_b = (weight_b * (wgrad_b - row_dot) * SCALE).astype(BF16)
        query_grad = nn(sgrad_a, shared_key) + both(lambda b: nn(sgrad_b[halves[b]], own_key[b]))
        query_grad_ref[:, at] = query_grad.astype(BF16)

        for side, left_a, left_b, right in ((0, sgrad_a, sgrad_b, query), (1, low_a, low_b, grad)):
            shared = tn(left_a, right)
            own_ref[side, :, at] = shared[: 2 * BLOCK]
            end_terms_ref[end_to, 0, side] = shared[2 * BLOCK : 3 * BLOCK].astype(BF16)
            end_terms_ref[end_to, 1, side] = shared[3 * BLOCK :].astype(BF16)
            for b, edge_ref in enumerate((prev_terms_ref, next_terms_ref)):
                part = tn(left_b[halves[b]], right[halves[b]]).astype(BF16)
                edge_ref[side, :, at] = part[:BLOCK]
                for r in range(3):
                    terms_ref[owners[b][r], side] = part[(r + 1) * BLOCK : (r + 2) * BLOCK]
        return carry

    lax.fori_loop(0, HEADS, one, 0)


def attend(picks, where, query, grad, key, value, far, prev, following, ends):
    flat = jax.ShapeDtypeStruct((2 * BLOCK, HEADS * DH), BF16)
    edge = jax.ShapeDtypeStruct((2, BLOCK, HEADS * DH), BF16)
    return pl.pallas_call(
        attend_kernel,
        in_specs=[IN_SMEM, IN_SMEM] + [IN_VMEM] * 8,
        out_specs=[IN_VMEM] * 7,
        out_shape=[
            flat,
            flat,
            jax.ShapeDtypeStruct((SHARDS, 2, BLOCK, DH), BF16),
            jax.ShapeDtypeStruct((2, 2 * BLOCK, HEADS * DH), F32),
            edge,
            edge,
            jax.ShapeDtypeStruct((HEADS, 2, 2, BLOCK, DH), BF16),
        ],
        compiler_params=params(),
        cost_estimate=cost(2 * 10**9, 17 * 2**20, 10**6),
        name="attend",
    )(picks, where, query, grad, key, value, far, prev, following, ends)


def gather_kernel(
    item_ref, where_ref, terms_ref, own_ref, low_ref, high_ref, ends_ref, key_ref, value_ref, total_ref
):
    shard, my_x, my_y = where_ref[0], where_ref[1], where_ref[2]
    steps, per_step = pl.num_programs(0), terms_ref.shape[0]
    step = pl.program_id(0)

    @pl.when(step == 0)
    def _():
        total_ref[...] = jnp.zeros_like(total_ref)

    def one(slot, carry):
        item = item_ref[step * per_step + slot]
        for side in range(2):
            total_ref[item, side] += terms_ref[slot, side].astype(F32)
        return carry

    lax.fori_loop(0, per_step, one, 0, unroll=4)

    @pl.when(step == steps - 1)
    def _():
        @pl.when((shard == 0) | (shard == LAST))
        def _():
            block = jnp.where(shard == 0, 0, 1)
            for rel in range(HEADS):
                head = ((my_x + rel // 4) & 3) * 4 + ((my_y + rel % 4) & 3)
                total_ref[block * HEADS + head] += ends_ref[rel]

        for side, out_ref in enumerate((key_ref, value_ref)):
            for block, edge_ref in enumerate((low_ref, high_ref)):
                span = slice(block * BLOCK, (block + 1) * BLOCK)
                for head in range(HEADS):
                    at = slice(head * DH, (head + 1) * DH)
                    total = total_ref[block * HEADS + head, side] + own_ref[side, span, at]
                    total = total + edge_ref[side, :, at].astype(F32)
                    out_ref[span, at] = total.astype(BF16)


def gather(items, where, terms, own, low, high, ends):
    steps = 8
    flat = jax.ShapeDtypeStruct((2 * BLOCK, HEADS * DH), BF16)

    def whole(shape):
        return pl.BlockSpec(shape, lambda i, items, where: (0,) * len(shape))

    return pl.pallas_call(
        gather_kernel,
        grid_spec=pltpu.PrefetchScalarGridSpec(
            num_scalar_prefetch=2,
            grid=(steps,),
            in_specs=[
                pl.BlockSpec((SHARDS // steps, 2, BLOCK, DH), lambda i, items, where: (i, 0, 0, 0)),
                whole(own.shape),
                whole(low.shape),
                whole(high.shape),
                whole(ends.shape),
            ],
            out_specs=[whole(flat.shape), whole(flat.shape)],
            scratch_shapes=[pltpu.VMEM((2 * HEADS + 1, 2, BLOCK, DH), F32)],
        ),
        out_shape=[flat, flat],
        compiler_params=params(),
        cost_estimate=cost(10**6, 9 * 2**20),
        name="gather",
    )(items, where, terms, own, low, high, ends)


def shard_of(x, y, z):
    return (x % NX * NY + y % NY) * NZ + z


def send(value, route):
    return lax.ppermute(value, "seq", route)


def x_shift(by):
    cells = [(x, y, z) for x in range(NX) for y in range(NY) for z in range(NZ)]
    return [(shard_of(x, y, z), shard_of(x + by, y, z)) for x, y, z in cells]


def y_shift(by):
    cells = [(x, y, z) for x in range(NX) for y in range(NY) for z in range(NZ)]
    return [(shard_of(x, y, z), shard_of(x, y + by, z)) for x, y, z in cells]


def z_moves(pairs):
    cells = [(x, y) for x in range(NX) for y in range(NY)]
    return [(shard_of(x, y, a), shard_of(x, y, b)) for x, y in cells for a, b in pairs]


Z_SPREAD = (((0, 4), (7, 3)), ((0, 2), (4, 6), (7, 5), (3, 1)))
Z_SWAP = tuple((z, z ^ 1) for z in range(NZ))
FIRST = (0, 0, 0)
FINAL = (NX - 1, NY - 1, NZ - 1)


def spread_ends(low, high, my_x, my_y, my_z):
    shard = lax.axis_index("seq")
    mine = jnp.where(shard == 0, low, high).reshape(2, BLOCK, NX, NY * DH)
    roots = (FIRST, FINAL)

    def x_piece(by):
        return lax.dynamic_slice_in_dim(mine, (my_x + by) % NX, 1, 2)[:, :, 0]

    held = jnp.where((shard == 0) | (shard == LAST), x_piece(0), jnp.zeros((), BF16))
    arrived = [
        send(x_piece(by), [(shard_of(x, y, z), shard_of(x + by, y, z)) for x, y, z in roots])
        for by in range(1, NX)
    ]
    held = (held + arrived[0] + arrived[1] + arrived[2]).reshape(2, BLOCK, NY, DH)

    def y_piece(by):
        return lax.dynamic_slice_in_dim(held, (my_y + by) % NY, 1, 2)[:, :, 0]

    in_line = ((my_y == 0) & (my_z == 0)) | ((my_y == NY - 1) & (my_z == NZ - 1))
    arrived = [
        send(
            y_piece(by),
            [(shard_of(x, y, z), shard_of(x, y + by, z)) for x in range(NX) for _, y, z in roots],
        )
        for by in range(1, NY)
    ]
    kept = jnp.where(in_line, y_piece(0), jnp.zeros((), BF16))
    held = kept + arrived[0] + arrived[1] + arrived[2]
    for pairs in Z_SPREAD:
        held = held + send(held, z_moves(pairs))
    other = send(held, z_moves(Z_SWAP))
    even = my_z % 2 == 0
    pair = jnp.stack([jnp.where(even, held, other), jnp.where(even, other, held)])
    line = jnp.stack([pair] + [send(pair, y_shift(by)) for by in range(1, NY)])
    plane = jnp.stack([line] + [send(line, x_shift(by)) for by in range(1, NX)])
    return plane.reshape(HEADS, 2, 2, BLOCK, DH)


def collect_ends(terms, my_x, my_y, my_z):
    terms = terms.reshape(NX, NY, 2, 2, BLOCK, DH)
    line = terms[0].astype(F32)
    for by in range(1, NX):
        line = line + send(terms[by], x_shift(by)).astype(F32)
    low_line = line.astype(BF16)
    pair = line[0]
    for by in range(1, NY):
        pair = pair + send(low_line[by], y_shift(by)).astype(F32)
    even = my_z % 2 == 0
    held = jnp.where(even, pair[0], pair[1])
    held = held + send(jnp.where(even, pair[1], pair[0]), z_moves(Z_SWAP))
    for pairs in reversed(Z_SPREAD):
        held = held + send(held, z_moves([(b, a) for a, b in pairs]))
    roots = (FIRST, FINAL)
    line = jnp.stack(
        [held]
        + [
            send(
                held,
                [(shard_of(x, y + by, z), shard_of(x, y, z)) for x in range(NX) for _, y, z in roots],
            )
            for by in range(1, NY)
        ]
    )
    plane = jnp.stack(
        [line]
        + [
            send(line, [(shard_of(x + by, y, z), shard_of(x, y, z)) for x, y, z in roots])
            for by in range(1, NX)
        ]
    )
    return plane.reshape(HEADS, 2, BLOCK, DH)


def on_device(queries, key_states, values, out_grad, rand_blocks):
    shard = lax.axis_index("seq")
    my_x, my_y, my_z = shard // (NY * NZ), shard // NZ % NY, shard % NZ
    where = jnp.stack([shard, my_x, my_y]).astype(jnp.int32)
    wanted = rand_blocks // 2 == shard
    item = rand_blocks % 2 * HEADS + lax.broadcasted_iota(jnp.int32, rand_blocks.shape, 1)
    items = jnp.max(jnp.where(wanted, item, -1), axis=(1, 2))
    items = jnp.max(items.reshape(SHARDS, 2), axis=1)
    picks = lax.dynamic_slice_in_dim(rand_blocks, 2 * shard, 2, 0).reshape(2 * PICKS)

    slots, low, high = pack(jnp.maximum(items, 0), key_states, values)
    far = lax.all_to_all(slots, "seq", split_axis=0, concat_axis=0, tiled=True)
    prev = send(high, [(i, i + 1) for i in range(LAST)])
    following = send(low, [(i + 1, i) for i in range(LAST)])
    ends = spread_ends(low, high, my_x, my_y, my_z)
    attended, query_grad, terms, own, prev_terms, next_terms, end_terms = attend(
        picks, where, queries, out_grad, key_states, values, far, prev, following, ends
    )
    back = lax.all_to_all(terms, "seq", split_axis=0, concat_axis=0, tiled=True)
    from_next = send(prev_terms, [(i + 1, i) for i in range(LAST)])
    from_prev = send(next_terms, [(i, i + 1) for i in range(LAST)])
    end_sums = collect_ends(end_terms, my_x, my_y, my_z)
    key_grad, value_grad = gather(
        jnp.where(items < 0, 2 * HEADS, items), where, back, own, from_prev, from_next, end_sums
    )
    return (attended, query_grad, key_grad, value_grad)


def solution(mesh):
    placed = P("seq", "head")
    return jax.shard_map(
        on_device,
        mesh=mesh,
        in_specs=(placed, placed, placed, placed, P(None, "head", None)),
        out_specs=(placed, placed, placed, placed),
        check_vma=False,
    )
```

time: 606 us -> 340 us (0.56)
  waiting for transfers between devices: 443 us -> 192 us
  starting transfers between devices: 45.6 us -> 94.1 us
  local copies, waits for them, and re-layouts: 50.6 us -> 10.5 us
  Pallas kernels: 0 us -> 32.2 us
  matrix products: 27.1 us -> 0 us
  between operations: 15.1 us -> 1.48 us
  other arithmetic: 17.3 us -> 5.9 us
    psum x2 -> x0, waiting for transfers between devices: 345 us -> none  [the longest x1 218 us: on_device(): global_sum = lax.psum(global_terms, 'seq')]
    ppermute x4 -> x34, waiting for transfers between devices: 98.2 us -> 192 us  [send(): return lax.ppermute(value, 'seq', route)]
    ppermute x4 -> x34, starting transfers between devices: 18.2 us -> 64.9 us  [send(): return lax.ppermute(value, 'seq', route)]
    pallas_call x0 -> x3, Pallas kernels: none -> 32.2 us  [the longest x1 20.4 us: attend(): pl.pallas_call(attend_kernel, in_specs=[IN_SMEM, IN_SMEM] + [IN_VMEM] * 8...]
    dot_general x11 -> x0, matrix products: 27.1 us -> none  [the longest x1 4.52 us: on_device(): jnp.einsum('hlqk,hlkd->hlqd', weights_low, gathered[1], preferred_element...]
    reshape x6 -> x4, local copies, waits for them, and re-layouts: 10.6 us -> 0.66 us  [the longest x1 0.38 us: spread_ends(): mine = jnp.where(shard == 0, low, high).reshape(2, BLOCK, NX, NY * DH)]
    unnamed x43 -> x44, local copies, waits for them, and re-layouts: 17.9 us -> 8.45 us
    gather x3 -> x0, local copies, waits for them, and re-layouts: 9.43 us -> none  [the longest x1 3.34 us: place_arrived(): picked = arrived.reshape(shard_count * slot_room, 2, BLOCK, DH)[target]]
  transfers between devices with their start and end apart: 8 -> 36, of which waited for: 4 -> 20; matrix products, arithmetic and copies ran while one was open for 8% -> 2% of each run, Pallas kernels for 0% -> 0%
where the time goes in v1:
time: 340 us; the launch traced here: 337 us
  waiting for transfers between devices  192 us (56%)
  starting transfers between devices  94.1 us (28%)
  Pallas kernels  32.2 us (9%)
  local copies, waits for them, and re-layouts  10.5 us (3%)
  other arithmetic  5.9 us (2%)
    ppermute x34, waiting for transfers between devices, send(): return lax.ppermute(value, 'seq', route)  192 us
    ppermute x34, starting transfers between devices, send(): return lax.ppermute(value, 'seq', route)  64.9 us
    pallas_call x1, Pallas kernels, attend(): pl.pallas_call(attend_kernel, in_specs=[IN_SMEM, IN_SMEM] + [IN_VMEM] * 8...  20.4 us
    all_to_all x1, starting transfers between devices, on_device(): far = lax.all_to_all(slots, 'seq', split_axis=0, concat_axis=0, tiled=True)  16.4 us
    all_to_all x1, starting transfers between devices, on_device(): back = lax.all_to_all(terms, 'seq', split_axis=0, concat_axis=0, tiled=True)  12.8 us
    unnamed x44, local copies, waits for them, and re-layouts  8.45 us
    pallas_call x1, Pallas kernels, gather(): pl.pallas_call(gather_kernel, grid_spec=pltpu.PrefetchScalarGridSpec(num_...  6.97 us
  transfers between devices with their start and end apart: 36, of which 20 were waited for; matrix products, arithmetic and copies ran while one was open for 2% of the time, Pallas kernels for 0%

profile of v1, /device:TPU:6, one launch (start us, length us, event | category | flops | bytes accessed | tf_op | source)
XLA Modules:
  0.0 336.6 jit_solution(8898288897560332786)
XLA Ops:
  3.9 4.9 %pack.1 = (bf16[128,2,64,128]{3,2,1,0:T(8,128)(2,1)}, bf16[2,64,2048]{2,1,0:T(8,128)(2,1)S(1)}, bf16[2,64,2048]{2,1,0:T(8,128)(2,1)}) custom-call(s32[128]{0:T(128)S(1)} %get-tuple-element.53.item_ref, bf16[128,2048]{1,0:T(8,128)(2,1)S(1)} %copy-done.1, bf16[128,2048]{1,0:T(8,128)(2,1)S(1)} %copy-done.3), custom_call_target="tpu_custom_call" | custom-call | bytes 6291456 | tf_op jit(solution)/shard_map/pack/pallas_call | solution.py:82
  8.8 16.4 %all-to-all-start = ((bf16[128,2,64,128]{3,2,1,0:T(8,128)(2,1)}), bf16[128,2,64,128]{3,2,1,0:T(8,128)(2,1)}, u32[]{:S(2)}, u32[]{:S(2)}) async-start(bf16[128,2,64,128]{3,2,1,0:T(8,128)(2,1)} %get-tuple-element.16), calls=%async_computation | async-start | bytes 8388608 | tf_op jit(solution)/shard_map/all_to_all | solution.py:395
  25.3 1.1 broadcast_select_fusion
  26.8 1.1 constant_dynamic-slice_fusion.6
  28.0 1.3 collective-permute-start.4
  30.8 8.6 %collective-permute-done.4 = bf16[2,64,512]{2,1,0:T(8,128)(2,1)S(1)} collective-permute-done((bf16[2,64,512]{2,1,0:T(8,128)(2,1)S(1)}, bf16[2,64,512]{2,1,0:T(8,128)(2,1)S(1)}, u32[]{:S(2)}, u32[]{:S(2)}) %collective-permute-start.4) | collective-permute-done | bytes 131104 | tf_op jit(solution)/shard_map/ppermute | solution.py:287
  39.8 1.3 collective-permute-start.5
  41.1 1.3 collective-permute-start.6
  42.4 1.3 collective-permute-start.7
  45.3 1.3 collective-permute-start.8
  46.6 67.7 %collective-permute-done.8 = bf16[2,64,128]{2,1,0:T(8,128)(2,1)S(1)} collective-permute-done((bf16[2,64,128]{2,1,0:T(8,128)(2,1)S(1)}, bf16[2,64,128]{2,1,0:T(8,128)(2,1)S(1)}, u32[]{:S(2)}, u32[]{:S(2)}) %collective-permute-start.8) | collective-permute-done | bytes 32800 | tf_op jit(solution)/shard_map/ppermute | solution.py:287
  114.3 1.3 collective-permute-start.9
  115.6 1.6 collective-permute-done.9
  117.2 7.2 %collective-permute-start.10 = (bf16[2,64,128]{2,1,0:T(8,128)(2,1)S(1)}, bf16[2,64,128]{2,1,0:T(8,128)(2,1)S(1)}, u32[]{:S(2)}, u32[]{:S(2)}) collective-permute-start(bf16[2,64,128]{2,1,0:T(8,128)(2,1)S(1)} %add.178), channel_id=1, source_target_pairs={{0,2},{2,0},{4,6},{6,4},{8,10},{10,8},{12,14},{14,12},{16,18},{18,... | collective-permute-start | bytes 98312 | tf_op jit(solution)/shard_map/ppermute | solution.py:287
  124.3 1.9 collective-permute-done.10
  126.3 3.4 %collective-permute-start.12 = (bf16[2,2,64,128]{3,2,1,0:T(8,128)(2,1)S(1)}, bf16[2,2,64,128]{3,2,1,0:T(8,128)(2,1)S(1)}, u32[]{:S(2)}, u32[]{:S(2)}) collective-permute-start(bf16[2,2,64,128]{3,2,1,0:T(8,128)(2,1)S(1)} %get-tuple-element.49), channel_id=1, source_target_pairs={{0,32},{2,34},{4,36},{6,38},{8,40},{10,42},{12,44},{14,46},{16,48}... | collective-permute-start | bytes 196616 | tf_op jit(solution)/shard_map/ppermute | solution.py:287
  130.3 2.6 collective-permute-start.13
  132.9 3.9 %collective-permute-start = (bf16[2,64,2048]{2,1,0:T(8,128)(2,1)}, bf16[2,64,2048]{2,1,0:T(8,128)(2,1)S(1)}, u32[]{:S(2)}, u32[]{:S(2)}) collective-permute-start(bf16[2,64,2048]{2,1,0:T(8,128)(2,1)} %get-tuple-element.17), channel_id=1, source_target_pairs={{0,2},{2,4},{4,6},{6,8},{8,10},{10,12},{12,14},{14,16},{16,18},{18... | collective-permute-start | bytes 1572872 | tf_op jit(solution)/shard_map/ppermute | solution.py:287
  136.8 6.1 %collective-permute-start.1 = (bf16[2,64,2048]{2,1,0:T(8,128)(2,1)}, bf16[2,64,2048]{2,1,0:T(8,128)(2,1)S(1)}, u32[]{:S(2)}, u32[]{:S(2)}) collective-permute-start(bf16[2,64,2048]{2,1,0:T(8,128)(2,1)} %copy-done.13), channel_id=1, source_target_pairs={{2,0},{4,2},{6,4},{8,6},{10,8},{12,10},{14,12},{16,14},{18,16},{20... | collective-permute-start | bytes 1572872 | tf_op jit(solution)/shard_map/ppermute | solution.py:287
  144.8 2.3 collective-permute-start.14
  147.5 5.4 %collective-permute-done.15 = bf16[4,2,2,64,128]{4,3,2,1,0:T(8,128)(2,1)} collective-permute-done((bf16[4,2,2,64,128]{4,3,2,1,0:T(8,128)(2,1)}, bf16[4,2,2,64,128]{4,3,2,1,0:T(8,128)(2,1)}, u32[]{:S(2)}, u32[]{:S(2)}) %collective-permute-start.15) | collective-permute-done | bytes 262176 | tf_op jit(solution)/shard_map/ppermute | solution.py:287
  153.0 2.6 collective-permute-done.16
  155.6 2.2 pad_maximum_fusion
  157.9 20.4 %attend.1 = (bf16[128,2048]{1,0:T(8,128)(2,1)}, bf16[128,2048]{1,0:T(8,128)(2,1)}, bf16[128,2,64,128]{3,2,1,0:T(8,128)(2,1)}, f32[2,128,2048]{2,1,0:T(8,128)}, b...) custom-call(s32[96]{0:T(128)S(1)} %reshape.45.pick_ref, ...), custom_call_target="tpu_custom_call" | custom-call | flops 2000000000 | bytes 17825792 | tf_op jit(solution)/shard_map/attend/pallas_call | solution.py:196
  180.8 12.8 %all-to-all-start.1 = ((bf16[128,2,64,128]{3,2,1,0:T(8,128)(2,1)}), bf16[128,2,64,128]{3,2,1,0:T(8,128)(2,1)}, u32[]{:S(2)}, u32[]{:S(2)}) async-start(bf16[128,2,64,128]{3,2,1,0:T(8,128)(2,1)} %get-tuple-element.21), calls=%async_computation.1 | async-start | bytes 8388608 | tf_op jit(solution)/shard_map/all_to_all | solution.py:402
  194.3 1.6 collective-permute-start.21
  196.9 18.0 %collective-permute-done.19 = bf16[4,2,2,64,128]{4,3,2,1,0:T(8,128)(2,1)S(1)} collective-permute-done((bf16[4,2,2,64,128]{4,3,2,1,0:T(8,128)(2,1)S(1)}, bf16[4,2,2,64,128]{4,3,2,1,0:T(8,128)(2,1)S(1)}, u32[]{:S(2)}, u32[]{:S(2)}) %collective-permute-start.19) | collective-permute-done | bytes 262176 | tf_op jit(solution)/shard_map/ppermute | solution.py:287
  214.9 1.6 collective-permute-done.21
  216.5 7.7 %collective-permute-done.20 = bf16[4,2,2,64,128]{4,3,2,1,0:T(8,128)(2,1)S(1)} collective-permute-done((bf16[4,2,2,64,128]{4,3,2,1,0:T(8,128)(2,1)S(1)}, bf16[4,2,2,64,128]{4,3,2,1,0:T(8,128)(2,1)S(1)}, u32[]{:S(2)}, u32[]{:S(2)}) %collective-permute-start.20) | collective-permute-done | bytes 262176 | tf_op jit(solution)/shard_map/ppermute | solution.py:287
  224.4 1.9 collective-permute-start.22
  226.3 1.4 collective-permute-start.24
  228.7 2.7 collective-permute-done.22
  232.1 2.7 collective-permute-done.23
  234.8 2.0 collective-permute-start.25
  236.9 48.5 %collective-permute-done.25 = f32[2,64,128]{2,1,0:T(8,128)S(1)} collective-permute-done((f32[2,64,128]{2,1,0:T(8,128)S(1)}, f32[2,64,128]{2,1,0:T(8,128)S(1)}, u32[]{:S(2)}, u32[]{:S(2)}) %collective-permute-start.25) | collective-permute-done | bytes 65568 | tf_op jit(solution)/shard_map/ppermute | solution.py:287
  285.4 1.3 collective-permute-start.26
  286.7 5.8 %collective-permute-done.26 = f32[2,64,128]{2,1,0:T(8,128)S(1)} collective-permute-done((f32[2,64,128]{2,1,0:T(8,128)S(1)}, f32[2,64,128]{2,1,0:T(8,128)S(1)}, u32[]{:S(2)}, u32[]{:S(2)}) %collective-permute-start.26) | collective-permute-done | bytes 65568 | tf_op jit(solution)/shard_map/ppermute | solution.py:287
  292.5 1.3 collective-permute-start.27
  293.8 8.9 %collective-permute-done.27 = f32[2,64,128]{2,1,0:T(8,128)S(1)} collective-permute-done((f32[2,64,128]{2,1,0:T(8,128)S(1)}, f32[2,64,128]{2,1,0:T(8,128)S(1)}, u32[]{:S(2)}, u32[]{:S(2)}) %collective-permute-start.27) | collective-permute-done | bytes 65568 | tf_op jit(solution)/shard_map/ppermute | solution.py:287
  302.7 1.3 collective-permute-start.30
  304.0 1.3 collective-permute-start.29
  305.3 1.3 collective-permute-start.28
  306.6 1.9 collective-permute-start.17
  308.5 8.1 %collective-permute-start.18 = (bf16[2,64,2048]{2,1,0:T(8,128)(2,1)S(1)}, bf16[2,64,2048]{2,1,0:T(8,128)(2,1)S(1)}, u32[]{:S(2)}, u32[]{:S(2)}) collective-permute-start(bf16[2,64,2048]{2,1,0:T(8,128)(2,1)S(1)} %copy-done.15), channel_id=1, source_target_pairs={{2,0},{4,2},{6,4},{8,6},{10,8},{12,10},{14,12},{16,14},{18,16},{20... | collective-permute-start | bytes 1572872 | tf_op jit(solution)/shard_map/ppermute | solution.py:287
  318.1 1.3 collective-permute-start.33
  319.4 6.4 %collective-permute-done.33 = f32[4,2,64,128]{3,2,1,0:T(8,128)S(1)} collective-permute-done((f32[4,2,64,128]{3,2,1,0:T(8,128)S(1)}, f32[4,2,64,128]{3,2,1,0:T(8,128)S(1)}, u32[]{:S(2)}, u32[]{:S(2)}) %collective-permute-start.33) | collective-permute-done | bytes 262176 | tf_op jit(solution)/shard_map/ppermute | solution.py:287
  327.5 1.0 copy-done.10
  329.6 7.0 %gather.1 = (bf16[128,2048]{1,0:T(8,128)(2,1)}, bf16[128,2048]{1,0:T(8,128)(2,1)}) custom-call(s32[128]{0:T(128)S(1)} %get-tuple-element.52.item_ref, s32[3]{0:T(128)S(1)} %pad_add_fusion.where_ref, bf16[128,2,64,128]{3,2,1,0:T(8,128)(2,1)} %all-to-all-done.1.terms_ref, f32[2,128,2048]{2,1,0:T(8,128)S(1)} %copy-done, bf16[2,64,2048]{2,1,0:T(8,128)(2,1)S(1)} %copy-done.10, ...), custom_call_target="tpu_custom_call" | custom-call | flops 1000000 | bytes 9437184 | tf_op jit(solution)/shard_map/gather/pallas_call | solution.py:260
  (102 shorter events, 20.2 us)
Async XLA Ops:
  1.8 1.0 copy-start.1
  8.8 16.5 %copy-start.13 = (bf16[2,64,2048]{2,1,0:T(8,128)(2,1)}, bf16[2,64,2048]{2,1,0:T(8,128)(2,1)S(1)}, u32[]{:S(2)}) copy-start(bf16[2,64,2048]{2,1,0:T(8,128)(2,1)S(1)} %get-tuple-element.18) | copy-start | bytes 1572868
  8.8 149.1 %all-to-all-start = ((bf16[128,2,64,128]{3,2,1,0:T(8,128)(2,1)}), bf16[128,2,64,128]{3,2,1,0:T(8,128)(2,1)}, u32[]{:S(2)}, u32[]{:S(2)}) async-start(bf16[128,2,64,128]{3,2,1,0:T(8,128)(2,1)} %get-tuple-element.16), calls=%async_computation | async-start | bytes 8388608 | tf_op jit(solution)/shard_map/all_to_all | solution.py:395
  26.4 120.7 %copy-start.18 = (s32[256,16,3]{0,1,2:T(8,128)S(1)}, s32[256,16,3]{0,1,2:T(8,128)}, u32[]{:S(2)}) copy-start(s32[256,16,3]{0,1,2:T(8,128)} %param.9) | copy-start | bytes 147460
  26.8 131.1 %copy-start.2 = (bf16[128,2048]{1,0:T(8,128)(2,1)S(1)}, bf16[128,2048]{1,0:T(8,128)(2,1)}, u32[]{:S(2)}) copy-start(bf16[128,2048]{1,0:T(8,128)(2,1)} %key_ref.3) | copy-start | bytes 1572868
  26.8 131.1 %copy-start.4 = (bf16[128,2048]{1,0:T(8,128)(2,1)S(1)}, bf16[128,2048]{1,0:T(8,128)(2,1)}, u32[]{:S(2)}) copy-start(bf16[128,2048]{1,0:T(8,128)(2,1)} %value_ref.3) | copy-start | bytes 1572868
  26.8 131.1 %copy-start.7 = (bf16[128,2048]{1,0:T(8,128)(2,1)S(1)}, bf16[128,2048]{1,0:T(8,128)(2,1)}, u32[]{:S(2)}) copy-start(bf16[128,2048]{1,0:T(8,128)(2,1)} %query_ref.1) | copy-start | bytes 1572868
  26.8 131.1 %copy-start.8 = (bf16[128,2048]{1,0:T(8,128)(2,1)S(1)}, bf16[128,2048]{1,0:T(8,128)(2,1)}, u32[]{:S(2)}) copy-start(bf16[128,2048]{1,0:T(8,128)(2,1)} %grad_ref.1) | copy-start | bytes 1572868
  28.0 11.4 %collective-permute-start.4 = (bf16[2,64,512]{2,1,0:T(8,128)(2,1)S(1)}, bf16[2,64,512]{2,1,0:T(8,128)(2,1)S(1)}, u32[]{:S(2)}, u32[]{:S(2)}) collective-permute-start(bf16[2,64,512]{2,1,0:T(8,128)(2,1)S(1)} %bitcast.84), channel_id=1, source_target_pairs={{0,192},{254,190},{1,193},{255,191}} | collective-permute-start | bytes 393224 | tf_op jit(solution)/shard_map/ppermute | solution.py:287
  29.3 10.1 %collective-permute-start.2 = (bf16[2,64,512]{2,1,0:T(8,128)(2,1)S(1)}, bf16[2,64,512]{2,1,0:T(8,128)(2,1)S(1)}, u32[]{:S(2)}, u32[]{:S(2)}) collective-permute-start(bf16[2,64,512]{2,1,0:T(8,128)(2,1)S(1)} %bitcast.85), channel_id=1, source_target_pairs={{0,64},{254,62},{1,65},{255,63}} | collective-permute-start | bytes 393224 | tf_op jit(solution)/shard_map/ppermute | solution.py:287
  30.0 9.4 %collective-permute-start.3 = (bf16[2,64,512]{2,1,0:T(8,128)(2,1)S(1)}, bf16[2,64,512]{2,1,0:T(8,128)(2,1)S(1)}, u32[]{:S(2)}, u32[]{:S(2)}) collective-permute-start(bf16[2,64,512]{2,1,0:T(8,128)(2,1)S(1)} %bitcast.86), channel_id=1, source_target_pairs={{0,128},{254,126},{1,129},{255,127}} | collective-permute-start | bytes 393224 | tf_op jit(solution)/shard_map/ppermute | solution.py:287
  39.8 4.0 %collective-permute-start.5 = (bf16[2,64,128]{2,1,0:T(8,128)(2,1)S(1)}, bf16[2,64,128]{2,1,0:T(8,128)(2,1)S(1)}, u32[]{:S(2)}, u32[]{:S(2)}) collective-permute-start(bf16[2,64,128]{2,1,0:T(8,128)(2,1)S(1)} %bitcast.95), channel_id=1, source_target_pairs={{0,16},{62,14},{64,80},{126,78},{128,144},{190,142},{192,208},{254... | collective-permute-start | bytes 98312 | tf_op jit(solution)/shard_map/ppermute | solution.py:287
  41.1 3.7 %collective-permute-start.6 = (bf16[2,64,128]{2,1,0:T(8,128)(2,1)S(1)}, bf16[2,64,128]{2,1,0:T(8,128)(2,1)S(1)}, u32[]{:S(2)}, u32[]{:S(2)}) collective-permute-start(bf16[2,64,128]{2,1,0:T(8,128)(2,1)S(1)} %bitcast.94), channel_id=1, source_target_pairs={{0,32},{62,30},{64,96},{126,94},{128,160},{190,158},{192,224},{254... | collective-permute-start | bytes 98312 | tf_op jit(solution)/shard_map/ppermute | solution.py:287
  42.4 2.9 collective-permute-start.7
  45.3 69.0 %collective-permute-start.8 = (bf16[2,64,128]{2,1,0:T(8,128)(2,1)S(1)}, bf16[2,64,128]{2,1,0:T(8,128)(2,1)S(1)}, u32[]{:S(2)}, u32[]{:S(2)}) collective-permute-start(bf16[2,64,128]{2,1,0:T(8,128)(2,1)S(1)} %fusion.15), channel_id=1, source_target_pairs={{0,8},{14,6},{16,24},{30,22},{32,40},{46,38},{48,56},{62,54},{64,7... | collective-permute-start | bytes 98312 | tf_op jit(solution)/shard_map/ppermute | solution.py:287
  114.3 2.9 collective-permute-start.9
  117.2 9.0 %collective-permute-start.10 = (bf16[2,64,128]{2,1,0:T(8,128)(2,1)S(1)}, bf16[2,64,128]{2,1,0:T(8,128)(2,1)S(1)}, u32[]{:S(2)}, u32[]{:S(2)}) collective-permute-start(bf16[2,64,128]{2,1,0:T(8,128)(2,1)S(1)} %add.178), channel_id=1, source_target_pairs={{0,2},{2,0},{4,6},{6,4},{8,10},{10,8},{12,14},{14,12},{16,18},{18,... | collective-permute-start | bytes 98312 | tf_op jit(solution)/shard_map/ppermute | solution.py:287
  126.3 16.7 %collective-permute-start.12 = (bf16[2,2,64,128]{3,2,1,0:T(8,128)(2,1)S(1)}, bf16[2,2,64,128]{3,2,1,0:T(8,128)(2,1)S(1)}, u32[]{:S(2)}, u32[]{:S(2)}) collective-permute-start(bf16[2,2,64,128]{3,2,1,0:T(8,128)(2,1)S(1)} %get-tuple-element.49), channel_id=1, source_target_pairs={{0,32},{2,34},{4,36},{6,38},{8,40},{10,42},{12,44},{14,46},{16,48}... | collective-permute-start | bytes 196616 | tf_op jit(solution)/shard_map/ppermute | solution.py:287
  129.7 13.3 %collective-permute-start.11 = (bf16[2,2,64,128]{3,2,1,0:T(8,128)(2,1)S(1)}, bf16[2,2,64,128]{3,2,1,0:T(8,128)(2,1)S(1)}, u32[]{:S(2)}, u32[]{:S(2)}) collective-permute-start(bf16[2,2,64,128]{3,2,1,0:T(8,128)(2,1)S(1)} %get-tuple-element.49), channel_id=1, source_target_pairs={{0,16},{2,18},{4,20},{6,22},{8,24},{10,26},{12,28},{14,30},{16,32}... | collective-permute-start | bytes 196616 | tf_op jit(solution)/shard_map/ppermute | solution.py:287
  130.3 12.7 %collective-permute-start.13 = (bf16[2,2,64,128]{3,2,1,0:T(8,128)(2,1)S(1)}, bf16[2,2,64,128]{3,2,1,0:T(8,128)(2,1)S(1)}, u32[]{:S(2)}, u32[]{:S(2)}) collective-permute-start(bf16[2,2,64,128]{3,2,1,0:T(8,128)(2,1)S(1)} %get-tuple-element.49), channel_id=1, source_target_pairs={{0,48},{2,50},{4,52},{6,54},{8,56},{10,58},{12,60},{14,62},{16,0},... | collective-permute-start | bytes 196616 | tf_op jit(solution)/shard_map/ppermute | solution.py:287
  132.9 24.9 %collective-permute-start = (bf16[2,64,2048]{2,1,0:T(8,128)(2,1)}, bf16[2,64,2048]{2,1,0:T(8,128)(2,1)S(1)}, u32[]{:S(2)}, u32[]{:S(2)}) collective-permute-start(bf16[2,64,2048]{2,1,0:T(8,128)(2,1)} %get-tuple-element.17), channel_id=1, source_target_pairs={{0,2},{2,4},{4,6},{6,8},{8,10},{10,12},{12,14},{14,16},{16,18},{18... | collective-permute-start | bytes 1572872 | tf_op jit(solution)/shard_map/ppermute | solution.py:287
  136.8 21.0 %collective-permute-start.1 = (bf16[2,64,2048]{2,1,0:T(8,128)(2,1)}, bf16[2,64,2048]{2,1,0:T(8,128)(2,1)S(1)}, u32[]{:S(2)}, u32[]{:S(2)}) collective-permute-start(bf16[2,64,2048]{2,1,0:T(8,128)(2,1)} %copy-done.13), channel_id=1, source_target_pairs={{2,0},{4,2},{6,4},{8,6},{10,8},{12,10},{14,12},{16,14},{18,16},{20... | collective-permute-start | bytes 1572872 | tf_op jit(solution)/shard_map/ppermute | solution.py:287
  143.7 9.1 %collective-permute-start.15 = (bf16[4,2,2,64,128]{4,3,2,1,0:T(8,128)(2,1)}, bf16[4,2,2,64,128]{4,3,2,1,0:T(8,128)(2,1)}, u32[]{:S(2)}, u32[]{:S(2)}) collective-permute-start(bf16[4,2,2,64,128]{4,3,2,1,0:T(8,128)(2,1)} %get-tuple-element.43), channel_id=1, source_target_pairs={{0,128},{2,130},{4,132},{6,134},{8,136},{10,138},{12,140},{14,142}... | collective-permute-start | bytes 786440 | tf_op jit(solution)/shard_map/ppermute | solution.py:287
  144.8 8.2 %collective-permute-start.14 = (bf16[4,2,2,64,128]{4,3,2,1,0:T(8,128)(2,1)}, bf16[4,2,2,64,128]{4,3,2,1,0:T(8,128)(2,1)}, u32[]{:S(2)}, u32[]{:S(2)}) collective-permute-start(bf16[4,2,2,64,128]{4,3,2,1,0:T(8,128)(2,1)} %get-tuple-element.43), channel_id=1, source_target_pairs={{0,64},{2,66},{4,68},{6,70},{8,72},{10,74},{12,76},{14,78},{16,80}... | collective-permute-start | bytes 786440 | tf_op jit(solution)/shard_map/ppermute | solution.py:287
  147.1 8.6 %collective-permute-start.16 = (bf16[4,2,2,64,128]{4,3,2,1,0:T(8,128)(2,1)}, bf16[4,2,2,64,128]{4,3,2,1,0:T(8,128)(2,1)}, u32[]{:S(2)}, u32[]{:S(2)}) collective-permute-start(bf16[4,2,2,64,128]{4,3,2,1,0:T(8,128)(2,1)} %get-tuple-element.43), channel_id=1, source_target_pairs={{0,192},{2,194},{4,196},{6,198},{8,200},{10,202},{12,204},{14,206}... | collective-permute-start | bytes 786440 | tf_op jit(solution)/shard_map/ppermute | solution.py:287
  180.8 12.9 %copy-start.6 = (bf16[16,2,2,64,128]{4,3,2,1,0:T(8,128)(2,1)S(1)}, bf16[16,2,2,64,128]{4,3,2,1,0:T(8,128)(2,1)}, u32[]{:S(2)}) copy-start(bf16[16,2,2,64,128]{4,3,2,1,0:T(8,128)(2,1)} %copy-done.5) | copy-start | bytes 3145732
  180.8 146.7 %all-to-all-start.1 = ((bf16[128,2,64,128]{3,2,1,0:T(8,128)(2,1)}), bf16[128,2,64,128]{3,2,1,0:T(8,128)(2,1)}, u32[]{:S(2)}, u32[]{:S(2)}) async-start(bf16[128,2,64,128]{3,2,1,0:T(8,128)(2,1)} %get-tuple-element.21), calls=%async_computation.1 | async-start | bytes 8388608 | tf_op jit(solution)/shard_map/all_to_all | solution.py:402
  193.7 112.9 %copy-start.17 = (bf16[2,64,2048]{2,1,0:T(8,128)(2,1)S(1)}, bf16[2,64,2048]{2,1,0:T(8,128)(2,1)}, u32[]{:S(2)}) copy-start(bf16[2,64,2048]{2,1,0:T(8,128)(2,1)} %copy-done.16) | copy-start | bytes 1572868
  193.7 114.8 %copy-start.15 = (bf16[2,64,2048]{2,1,0:T(8,128)(2,1)S(1)}, bf16[2,64,2048]{2,1,0:T(8,128)(2,1)}, u32[]{:S(2)}) copy-start(bf16[2,64,2048]{2,1,0:T(8,128)(2,1)} %copy-done.14) | copy-start | bytes 1572868
  193.7 133.9 %copy-start = (f32[2,128,2048]{2,1,0:T(8,128)S(1)}, f32[2,128,2048]{2,1,0:T(8,128)}, u32[]{:S(2)}) copy-start(f32[2,128,2048]{2,1,0:T(8,128)} %get-tuple-element.22.own_ref) | copy-start | bytes 6291460
  193.8 21.1 %collective-permute-start.19 = (bf16[4,2,2,64,128]{4,3,2,1,0:T(8,128)(2,1)S(1)}, bf16[4,2,2,64,128]{4,3,2,1,0:T(8,128)(2,1)S(1)}, u32[]{:S(2)}, u32[]{:S(2)}) collective-permute-start(bf16[4,2,2,64,128]{4,3,2,1,0:T(8,128)(2,1)S(1)} %get-tuple-element.30), channel_id=1, source_target_pairs={{0,64},{2,66},{4,68},{6,70},{8,72},{10,74},{12,76},{14,78},{16,80}... | collective-permute-start | bytes 786440 | tf_op jit(solution)/shard_map/ppermute | solution.py:287
  194.3 22.2 %collective-permute-start.21 = (bf16[4,2,2,64,128]{4,3,2,1,0:T(8,128)(2,1)S(1)}, bf16[4,2,2,64,128]{4,3,2,1,0:T(8,128)(2,1)S(1)}, u32[]{:S(2)}, u32[]{:S(2)}) collective-permute-start(bf16[4,2,2,64,128]{4,3,2,1,0:T(8,128)(2,1)S(1)} %get-tuple-element.31), channel_id=1, source_target_pairs={{0,192},{2,194},{4,196},{6,198},{8,200},{10,202},{12,204},{14,206}... | collective-permute-start | bytes 786440 | tf_op jit(solution)/shard_map/ppermute | solution.py:287
  195.9 28.3 %collective-permute-start.20 = (bf16[4,2,2,64,128]{4,3,2,1,0:T(8,128)(2,1)S(1)}, bf16[4,2,2,64,128]{4,3,2,1,0:T(8,128)(2,1)S(1)}, u32[]{:S(2)}, u32[]{:S(2)}) collective-permute-start(bf16[4,2,2,64,128]{4,3,2,1,0:T(8,128)(2,1)S(1)} %get-tuple-element.32), channel_id=1, source_target_pairs={{0,128},{2,130},{4,132},{6,134},{8,136},{10,138},{12,140},{14,142}... | collective-permute-start | bytes 786440 | tf_op jit(solution)/shard_map/ppermute | solution.py:287
  224.4 7.0 %collective-permute-start.22 = (bf16[2,2,64,128]{3,2,1,0:T(8,128)(2,1)S(1)}, bf16[2,2,64,128]{3,2,1,0:T(8,128)(2,1)S(1)}, u32[]{:S(2)}, u32[]{:S(2)}) collective-permute-start(bf16[2,2,64,128]{3,2,1,0:T(8,128)(2,1)S(1)} %get-tuple-element.39), channel_id=1, source_target_pairs={{0,16},{2,18},{4,20},{6,22},{8,24},{10,26},{12,28},{14,30},{16,32}... | collective-permute-start | bytes 196616 | tf_op jit(solution)/shard_map/ppermute | solution.py:287
  226.3 5.8 %collective-permute-start.24 = (bf16[2,2,64,128]{3,2,1,0:T(8,128)(2,1)S(1)}, bf16[2,2,64,128]{3,2,1,0:T(8,128)(2,1)S(1)}, u32[]{:S(2)}, u32[]{:S(2)}) collective-permute-start(bf16[2,2,64,128]{3,2,1,0:T(8,128)(2,1)S(1)} %get-tuple-element.40), channel_id=1, source_target_pairs={{0,48},{2,50},{4,52},{6,54},{8,56},{10,58},{12,60},{14,62},{16,0},... | collective-permute-start | bytes 196616 | tf_op jit(solution)/shard_map/ppermute | solution.py:287
  227.7 7.1 %collective-permute-start.23 = (bf16[2,2,64,128]{3,2,1,0:T(8,128)(2,1)S(1)}, bf16[2,2,64,128]{3,2,1,0:T(8,128)(2,1)S(1)}, u32[]{:S(2)}, u32[]{:S(2)}) collective-permute-start(bf16[2,2,64,128]{3,2,1,0:T(8,128)(2,1)S(1)} %get-tuple-element.41), channel_id=1, source_target_pairs={{0,32},{2,34},{4,36},{6,38},{8,40},{10,42},{12,44},{14,46},{16,48}... | collective-permute-start | bytes 196616 | tf_op jit(solution)/shard_map/ppermute | solution.py:287
  234.8 50.5 %collective-permute-start.25 = (f32[2,64,128]{2,1,0:T(8,128)S(1)}, f32[2,64,128]{2,1,0:T(8,128)S(1)}, u32[]{:S(2)}, u32[]{:S(2)}) collective-permute-start(f32[2,64,128]{2,1,0:T(8,128)S(1)} %select_bitcast_fusion), channel_id=1, source_target_pairs={{0,2},{2,0},{4,6},{6,4},{8,10},{10,8},{12,14},{14,12},{16,18},{18,... | collective-permute-start | bytes 196616 | tf_op jit(solution)/shard_map/ppermute | solution.py:287
  285.4 7.1 %collective-permute-start.26 = (f32[2,64,128]{2,1,0:T(8,128)S(1)}, f32[2,64,128]{2,1,0:T(8,128)S(1)}, u32[]{:S(2)}, u32[]{:S(2)}) collective-permute-start(f32[2,64,128]{2,1,0:T(8,128)S(1)} %bitcast_add_fusion), channel_id=1, source_target_pairs={{4,0},{12,8},{10,14},{2,6},{20,16},{28,24},{26,30},{18,22},{36,32}... | collective-permute-start | bytes 196616 | tf_op jit(solution)/shard_map/ppermute | solution.py:287
  292.5 10.2 %collective-permute-start.27 = (f32[2,64,128]{2,1,0:T(8,128)S(1)}, f32[2,64,128]{2,1,0:T(8,128)S(1)}, u32[]{:S(2)}, u32[]{:S(2)}) collective-permute-start(f32[2,64,128]{2,1,0:T(8,128)S(1)} %add.186), channel_id=1, source_target_pairs={{8,0},{6,14},{24,16},{22,30},{40,32},{38,46},{56,48},{54,62},{72,6... | collective-permute-start | bytes 196616 | tf_op jit(solution)/shard_map/ppermute | solution.py:287
  302.7 14.0 %collective-permute-start.30 = (f32[2,64,128]{2,1,0:T(8,128)S(1)}, f32[2,64,128]{2,1,0:T(8,128)S(1)}, u32[]{:S(2)}, u32[]{:S(2)}) collective-permute-start(f32[2,64,128]{2,1,0:T(8,128)S(1)} %add.187), channel_id=1, source_target_pairs={{48,0},{46,62},{112,64},{110,126},{176,128},{174,190},{240,192},{2... | collective-permute-start | bytes 196616 | tf_op jit(solution)/shard_map/ppermute | solution.py:287
  304.0 12.7 %collective-permute-start.29 = (f32[2,64,128]{2,1,0:T(8,128)S(1)}, f32[2,64,128]{2,1,0:T(8,128)S(1)}, u32[]{:S(2)}, u32[]{:S(2)}) collective-permute-start(f32[2,64,128]{2,1,0:T(8,128)S(1)} %add.187), channel_id=1, source_target_pairs={{32,0},{30,62},{96,64},{94,126},{160,128},{158,190},{224,192},{222... | collective-permute-start | bytes 196616 | tf_op jit(solution)/shard_map/ppermute | solution.py:287
  305.3 11.4 %collective-permute-start.28 = (f32[2,64,128]{2,1,0:T(8,128)S(1)}, f32[2,64,128]{2,1,0:T(8,128)S(1)}, u32[]{:S(2)}, u32[]{:S(2)}) collective-permute-start(f32[2,64,128]{2,1,0:T(8,128)S(1)} %add.187), channel_id=1, source_target_pairs={{16,0},{14,62},{80,64},{78,126},{144,128},{142,190},{208,192},{206... | collective-permute-start | bytes 196616 | tf_op jit(solution)/shard_map/ppermute | solution.py:287
  306.6 19.4 %collective-permute-start.17 = (bf16[2,64,2048]{2,1,0:T(8,128)(2,1)S(1)}, bf16[2,64,2048]{2,1,0:T(8,128)(2,1)S(1)}, u32[]{:S(2)}, u32[]{:S(2)}) collective-permute-start(bf16[2,64,2048]{2,1,0:T(8,128)(2,1)S(1)} %copy-done.17), channel_id=1, source_target_pairs={{0,2},{2,4},{4,6},{6,8},{8,10},{10,12},{12,14},{14,16},{16,18},{18... | collective-permute-start | bytes 1572872 | tf_op jit(solution)/shard_map/ppermute | solution.py:287
  308.5 18.2 %collective-permute-start.18 = (bf16[2,64,2048]{2,1,0:T(8,128)(2,1)S(1)}, bf16[2,64,2048]{2,1,0:T(8,128)(2,1)S(1)}, u32[]{:S(2)}, u32[]{:S(2)}) collective-permute-start(bf16[2,64,2048]{2,1,0:T(8,128)(2,1)S(1)} %copy-done.15), channel_id=1, source_target_pairs={{2,0},{4,2},{6,4},{8,6},{10,8},{12,10},{14,12},{16,14},{18,16},{20... | collective-permute-start | bytes 1572872 | tf_op jit(solution)/shard_map/ppermute | solution.py:287
  316.7 2.7 collective-permute-start.32
  317.4 2.0 collective-permute-start.31
  318.1 7.8 %collective-permute-start.33 = (f32[4,2,64,128]{3,2,1,0:T(8,128)S(1)}, f32[4,2,64,128]{3,2,1,0:T(8,128)S(1)}, u32[]{:S(2)}, u32[]{:S(2)}) collective-permute-start(f32[4,2,64,128]{3,2,1,0:T(8,128)S(1)} %get-tuple-element.38), channel_id=1, source_target_pairs={{192,0},{190,254},{193,1},{191,255}} | collective-permute-start | bytes 786440 | tf_op jit(solution)/shard_map/ppermute | solution.py:287
  327.5 1.0 copy-start.10
  (7 other events, 6.2 us)

commit v2 on v1

--- a/solution.py
+++ b/solution.py
@@ -187,7 +187,7 @@
                     terms_ref[owners[b][r], side] = part[(r + 1) * BLOCK : (r + 2) * BLOCK]
         return carry
 
-    lax.fori_loop(0, HEADS, one, 0)
+    lax.fori_loop(0, HEADS, one, 0, unroll=4)
 
 
 def attend(picks, where, query, grad, key, value, far, prev, following, ends):
@@ -213,9 +213,8 @@
 
 
 def gather_kernel(
-    item_ref, where_ref, terms_ref, own_ref, low_ref, high_ref, ends_ref, key_ref, value_ref, total_ref
+    item_ref, terms_ref, own_ref, low_ref, high_ref, key_ref, value_ref, total_ref
 ):
-    shard, my_x, my_y = where_ref[0], where_ref[1], where_ref[2]
     steps, per_step = pl.num_programs(0), terms_ref.shape[0]
     step = pl.program_id(0)
 
@@ -233,13 +232,6 @@
 
     @pl.when(step == steps - 1)
     def _():
-        @pl.when((shard == 0) | (shard == LAST))
-        def _():
-            block = jnp.where(shard == 0, 0, 1)
-            for rel in range(HEADS):
-                head = ((my_x + rel // 4) & 3) * 4 + ((my_y + rel % 4) & 3)
-                total_ref[block * HEADS + head] += ends_ref[rel]
-
         for side, out_ref in enumerate((key_ref, value_ref)):
             for block, edge_ref in enumerate((low_ref, high_ref)):
                 span = slice(block * BLOCK, (block + 1) * BLOCK)
@@ -250,24 +242,23 @@
                     out_ref[span, at] = total.astype(BF16)
 
 
-def gather(items, where, terms, own, low, high, ends):
+def gather(items, terms, own, low, high):
     steps = 8
     flat = jax.ShapeDtypeStruct((2 * BLOCK, HEADS * DH), BF16)
 
     def whole(shape):
-        return pl.BlockSpec(shape, lambda i, items, where: (0,) * len(shape))
+        return pl.BlockSpec(shape, lambda i, items: (0,) * len(shape))
 
     return pl.pallas_call(
         gather_kernel,
         grid_spec=pltpu.PrefetchScalarGridSpec(
-            num_scalar_prefetch=2,
+            num_scalar_prefetch=1,
             grid=(steps,),
             in_specs=[
-                pl.BlockSpec((SHARDS // steps, 2, BLOCK, DH), lambda i, items, where: (i, 0, 0, 0)),
+                pl.BlockSpec((SHARDS // steps, 2, BLOCK, DH), lambda i, items: (i, 0, 0, 0)),
                 whole(own.shape),
                 whole(low.shape),
                 whole(high.shape),
-                whole(ends.shape),
             ],
             out_specs=[whole(flat.shape), whole(flat.shape)],
             scratch_shapes=[pltpu.VMEM((2 * HEADS + 1, 2, BLOCK, DH), F32)],
@@ -276,7 +267,7 @@
         compiler_params=params(),
         cost_estimate=cost(10**6, 9 * 2**20),
         name="gather",
-    )(items, where, terms, own, low, high, ends)
+    )(items, terms, own, low, high)
 
 
 def shard_of(x, y, z):
@@ -297,56 +288,13 @@
     return [(shard_of(x, y, z), shard_of(x, y + by, z)) for x, y, z in cells]
 
 
-def z_moves(pairs):
-    cells = [(x, y) for x in range(NX) for y in range(NY)]
-    return [(shard_of(x, y, a), shard_of(x, y, b)) for x, y in cells for a, b in pairs]
-
-
-Z_SPREAD = (((0, 4), (7, 3)), ((0, 2), (4, 6), (7, 5), (3, 1)))
-Z_SWAP = tuple((z, z ^ 1) for z in range(NZ))
-FIRST = (0, 0, 0)
-FINAL = (NX - 1, NY - 1, NZ - 1)
-
-
-def spread_ends(low, high, my_x, my_y, my_z):
-    shard = lax.axis_index("seq")
-    mine = jnp.where(shard == 0, low, high).reshape(2, BLOCK, NX, NY * DH)
-    roots = (FIRST, FINAL)
-
-    def x_piece(by):
-        return lax.dynamic_slice_in_dim(mine, (my_x + by) % NX, 1, 2)[:, :, 0]
-
-    held = jnp.where((shard == 0) | (shard == LAST), x_piece(0), jnp.zeros((), BF16))
-    arrived = [
-        send(x_piece(by), [(shard_of(x, y, z), shard_of(x + by, y, z)) for x, y, z in roots])
-        for by in range(1, NX)
-    ]
-    held = (held + arrived[0] + arrived[1] + arrived[2]).reshape(2, BLOCK, NY, DH)
-
-    def y_piece(by):
-        return lax.dynamic_slice_in_dim(held, (my_y + by) % NY, 1, 2)[:, :, 0]
-
-    in_line = ((my_y == 0) & (my_z == 0)) | ((my_y == NY - 1) & (my_z == NZ - 1))
-    arrived = [
-        send(
-            y_piece(by),
-            [(shard_of(x, y, z), shard_of(x, y + by, z)) for x in range(NX) for _, y, z in roots],
-        )
-        for by in range(1, NY)
-    ]
-    kept = jnp.where(in_line, y_piece(0), jnp.zeros((), BF16))
-    held = kept + arrived[0] + arrived[1] + arrived[2]
-    for pairs in Z_SPREAD:
-        held = held + send(held, z_moves(pairs))
-    other = send(held, z_moves(Z_SWAP))
-    even = my_z % 2 == 0
-    pair = jnp.stack([jnp.where(even, held, other), jnp.where(even, other, held)])
+def spread_ends(pair):
     line = jnp.stack([pair] + [send(pair, y_shift(by)) for by in range(1, NY)])
     plane = jnp.stack([line] + [send(line, x_shift(by)) for by in range(1, NX)])
     return plane.reshape(HEADS, 2, 2, BLOCK, DH)
 
 
-def collect_ends(terms, my_x, my_y, my_z):
+def sum_ends(terms):
     terms = terms.reshape(NX, NY, 2, 2, BLOCK, DH)
     line = terms[0].astype(F32)
     for by in range(1, NX):
@@ -355,56 +303,36 @@
     pair = line[0]
     for by in range(1, NY):
         pair = pair + send(low_line[by], y_shift(by)).astype(F32)
-    even = my_z % 2 == 0
-    held = jnp.where(even, pair[0], pair[1])
-    held = held + send(jnp.where(even, pair[1], pair[0]), z_moves(Z_SWAP))
-    for pairs in reversed(Z_SPREAD):
-        held = held + send(held, z_moves([(b, a) for a, b in pairs]))
-    roots = (FIRST, FINAL)
-    line = jnp.stack(
-        [held]
-        + [
-            send(
-                held,
-                [(shard_of(x, y + by, z), shard_of(x, y, z)) for x in range(NX) for _, y, z in roots],
-            )
-            for by in range(1, NY)
-        ]
-    )
-    plane = jnp.stack(
-        [line]
-        + [
-            send(line, [(shard_of(x + by, y, z), shard_of(x, y, z)) for x, y, z in roots])
-            for by in range(1, NX)
-        ]
-    )
-    return plane.reshape(HEADS, 2, BLOCK, DH)
+    return pair.astype(BF16)
 
 
 def on_device(queries, key_states, values, out_grad, rand_blocks):
     shard = lax.axis_index("seq")
-    my_x, my_y, my_z = shard // (NY * NZ), shard // NZ % NY, shard % NZ
-    where = jnp.stack([shard, my_x, my_y]).astype(jnp.int32)
+    where = jnp.stack([shard, shard // (NY * NZ), shard // NZ % NY]).astype(jnp.int32)
     wanted = rand_blocks // 2 == shard
     item = rand_blocks % 2 * HEADS + lax.broadcasted_iota(jnp.int32, rand_blocks.shape, 1)
     items = jnp.max(jnp.where(wanted, item, -1), axis=(1, 2))
     items = jnp.max(items.reshape(SHARDS, 2), axis=1)
+    cell = jnp.arange(SHARDS, dtype=jnp.int32) // NZ
+    items = jnp.where(shard == 0, cell, jnp.where(shard == LAST, HEADS + cell, items))
     picks = lax.dynamic_slice_in_dim(rand_blocks, 2 * shard, 2, 0).reshape(2 * PICKS)
 
     slots, low, high = pack(jnp.maximum(items, 0), key_states, values)
     far = lax.all_to_all(slots, "seq", split_axis=0, concat_axis=0, tiled=True)
     prev = send(high, [(i, i + 1) for i in range(LAST)])
     following = send(low, [(i + 1, i) for i in range(LAST)])
-    ends = spread_ends(low, high, my_x, my_y, my_z)
+    far, prev, following = lax.optimization_barrier((far, prev, following))
+    ends = spread_ends(jnp.stack([far[0], far[LAST]]))
     attended, query_grad, terms, own, prev_terms, next_terms, end_terms = attend(
         picks, where, queries, out_grad, key_states, values, far, prev, following, ends
     )
+    end_pair = sum_ends(end_terms)
+    terms = terms.at[0].set(end_pair[0]).at[LAST].set(end_pair[1])
     back = lax.all_to_all(terms, "seq", split_axis=0, concat_axis=0, tiled=True)
     from_next = send(prev_terms, [(i + 1, i) for i in range(LAST)])
     from_prev = send(next_terms, [(i, i + 1) for i in range(LAST)])
-    end_sums = collect_ends(end_terms, my_x, my_y, my_z)
     key_grad, value_grad = gather(
-        jnp.where(items < 0, 2 * HEADS, items), where, back, own, from_prev, from_next, end_sums
+        jnp.where(items < 0, 2 * HEADS, items), back, own, from_prev, from_next
     )
     return (attended, query_grad, key_grad, value_grad)
 

time: 340 us -> 319 us (0.938)
  starting transfers between devices: 94.1 us -> 63.1 us
  waiting for transfers between devices: 192 us -> 214 us
  local copies, waits for them, and re-layouts: 10.5 us -> 5.51 us
    ppermute x34 -> x16, starting transfers between devices: 64.9 us -> 35.5 us  [send(): return lax.ppermute(value, 'seq', route)]
    ppermute x34 -> x16, waiting for transfers between devices: 192 us -> 214 us  [send(): return lax.ppermute(value, 'seq', route)]
    unnamed x44 -> x20, local copies, waits for them, and re-layouts: 8.45 us -> 2.9 us
  transfers between devices with their start and end apart: 36 -> 18, of which waited for: 20 -> 11; matrix products, arithmetic and copies ran while one was open for 2% -> 0% of each run, Pallas kernels for 0% -> 0%
where the time goes in v2:
time: 319 us; the launch traced here: 318 us
  waiting for transfers between devices  214 us (67%)
  starting transfers between devices  63.1 us (20%)
  Pallas kernels  30.1 us (9%)
  local copies, waits for them, and re-layouts  5.51 us (2%)
  other arithmetic  4.26 us (1%)
    ppermute x16, waiting for transfers between devices, send(): return lax.ppermute(value, 'seq', route)  214 us
    ppermute x16, starting transfers between devices, send(): return lax.ppermute(value, 'seq', route)  35.5 us
    pallas_call x1, Pallas kernels, attend(): pl.pallas_call(attend_kernel, in_specs=[IN_SMEM, IN_SMEM] + [IN_VMEM] * 8...  18.3 us
    all_to_all x1, starting transfers between devices, on_device(): far = lax.all_to_all(slots, 'seq', split_axis=0, concat_axis=0, tiled=True)  16.5 us
    all_to_all x1, starting transfers between devices, on_device(): back = lax.all_to_all(terms, 'seq', split_axis=0, concat_axis=0, tiled=True)  11.1 us
    pallas_call x1, Pallas kernels, gather(): pl.pallas_call(gather_kernel, grid_spec=pltpu.PrefetchScalarGridSpec(num_...  6.96 us
  transfers between devices with their start and end apart: 18, of which 11 were waited for; matrix products, arithmetic and copies ran while one was open for 0% of the time, Pallas kernels for 0%

profile of v2, /device:TPU:6, one launch (start us, length us, event | category | flops | bytes accessed | tf_op | source)
XLA Modules:
  0.0 318.2 jit_solution(17562800758408581482)
XLA Ops:
  0.6 0.9 fusion.8
  1.5 0.1 reshape.95
  1.7 0.1 reduce_max.19
  1.8 1.0 copy-done
  2.8 1.0 copy-done.2
  3.9 4.9 %pack.1 = (bf16[128,2,64,128]{3,2,1,0:T(8,128)(2,1)}, bf16[2,64,2048]{2,1,0:T(8,128)(2,1)S(1)}, bf16[2,64,2048]{2,1,0:T(8,128)(2,1)}) custom-call(s32[128]{0:T(128)S(1)} %broadcast_maximum_fusion.item_ref, bf16[128,2048]{1,0:T(8,128)(2,1)S(1)} %copy-done, bf16[128,2048]{1,0:T(8,128)(2,1)S(1)} %copy-done.2), custom_call_target="tpu_custom_call" | custom-call | bytes 6291456 | tf_op jit(solution)/shard_map/pack/pallas_call | solution.py:82
  8.8 0.8 copy-done.8
  9.6 16.5 %all-to-all-start = ((bf16[128,2,64,128]{3,2,1,0:T(8,128)(2,1)}), bf16[128,2,64,128]{3,2,1,0:T(8,128)(2,1)}, u32[]{:S(2)}, u32[]{:S(2)}) async-start(bf16[128,2,64,128]{3,2,1,0:T(8,128)(2,1)} %get-tuple-element.43), calls=%async_computation | async-start | bytes 8388608 | tf_op jit(solution)/shard_map/all_to_all | solution.py:321
  26.1 3.4 %collective-permute-start = (bf16[2,64,2048]{2,1,0:T(8,128)(2,1)}, bf16[2,64,2048]{2,1,0:T(8,128)(2,1)S(1)}, u32[]{:S(2)}, u32[]{:S(2)}) collective-permute-start(bf16[2,64,2048]{2,1,0:T(8,128)(2,1)} %get-tuple-element.44), channel_id=1, source_target_pairs={{0,2},{2,4},{4,6},{6,8},{8,10},{10,12},{12,14},{14,16},{16,18},{18... | collective-permute-start | bytes 1572872 | tf_op jit(solution)/shard_map/ppermute | solution.py:278
  29.5 6.7 %collective-permute-start.1 = (bf16[2,64,2048]{2,1,0:T(8,128)(2,1)}, bf16[2,64,2048]{2,1,0:T(8,128)(2,1)S(1)}, u32[]{:S(2)}, u32[]{:S(2)}) collective-permute-start(bf16[2,64,2048]{2,1,0:T(8,128)(2,1)} %copy-done.8), channel_id=1, source_target_pairs={{2,0},{4,2},{6,4},{8,6},{10,8},{12,10},{14,12},{16,14},{18,16},{20... | collective-permute-start | bytes 1572872 | tf_op jit(solution)/shard_map/ppermute | solution.py:278
  36.2 95.1 %collective-permute-done.prev_ref = bf16[2,64,2048]{2,1,0:T(8,128)(2,1)S(1)} collective-permute-done((bf16[2,64,2048]{2,1,0:T(8,128)(2,1)}, bf16[2,64,2048]{2,1,0:T(8,128)(2,1)S(1)}, u32[]{:S(2)}, u32[]{:S(2)}) %collective-permute-start) | collective-permute-done | bytes 524320 | tf_op jit(solution)/shard_map/ppermute | solution.py:278
  131.3 0.8 fusion.14
  132.1 0.8 collective-permute-start.3
  132.9 0.9 collective-permute-start.2
  133.8 2.3 collective-permute-start.4
  136.1 1.9 collective-permute-done.3
  138.0 0.7 collective-permute-done.2
  138.7 0.7 fusion.12
  139.4 1.2 collective-permute-start.6
  140.6 1.9 collective-permute-start.5
  142.5 0.2 collective-permute-start.7
  142.6 0.1 constant_dynamic-slice_fusion
  142.7 0.2 copy.10
  142.9 0.1 reshape.94.pick_ref
  143.0 0.1 pad_add_fusion.where_ref
  143.1 6.8 %collective-permute-done.6 = bf16[4,2,2,64,128]{4,3,2,1,0:T(8,128)(2,1)} collective-permute-done((bf16[4,2,2,64,128]{4,3,2,1,0:T(8,128)(2,1)}, bf16[4,2,2,64,128]{4,3,2,1,0:T(8,128)(2,1)}, u32[]{:S(2)}, u32[]{:S(2)}) %collective-permute-start.6) | collective-permute-done | bytes 262176 | tf_op jit(solution)/shard_map/ppermute | solution.py:278
  149.9 0.4 collective-permute-done.5
  150.3 2.3 collective-permute-done.7
  152.6 2.2 pad_maximum_fusion
  154.9 18.3 %attend.1 = (bf16[128,2048]{1,0:T(8,128)(2,1)}, bf16[128,2048]{1,0:T(8,128)(2,1)}, bf16[128,2,64,128]{3,2,1,0:T(8,128)(2,1)}, f32[2,128,2048]{2,1,0:T(8,128)}, b...) custom-call(s32[96]{0:T(128)S(1)} %reshape.94.pick_ref, ...), custom_call_target="tpu_custom_call" | custom-call | flops 2000000000 | bytes 17825792 | tf_op jit(solution)/shard_map/attend/pallas_call | solution.py:196
  173.2 0.6 collective-permute-start.8
  173.9 1.5 collective-permute-start.10
  175.3 1.1 collective-permute-start.9
  176.4 5.9 %collective-permute-done.8 = bf16[4,2,2,64,128]{4,3,2,1,0:T(8,128)(2,1)S(1)} collective-permute-done((bf16[4,2,2,64,128]{4,3,2,1,0:T(8,128)(2,1)S(1)}, bf16[4,2,2,64,128]{4,3,2,1,0:T(8,128)(2,1)S(1)}, u32[]{:S(2)}, u32[]{:S(2)}) %collective-permute-start.8) | collective-permute-done | bytes 262176 | tf_op jit(solution)/shard_map/ppermute | solution.py:278
  182.3 4.7 %collective-permute-done.10 = bf16[4,2,2,64,128]{4,3,2,1,0:T(8,128)(2,1)S(1)} collective-permute-done((bf16[4,2,2,64,128]{4,3,2,1,0:T(8,128)(2,1)S(1)}, bf16[4,2,2,64,128]{4,3,2,1,0:T(8,128)(2,1)S(1)}, u32[]{:S(2)}, u32[]{:S(2)}) %collective-permute-start.10) | collective-permute-done | bytes 262176 | tf_op jit(solution)/shard_map/ppermute | solution.py:278
  187.1 0.2 fusion.13
  187.3 1.9 collective-permute-start.11
  189.2 1.6 collective-permute-start.13
  190.9 1.4 collective-permute-start.12
  192.2 1.5 collective-permute-done.11
  193.7 2.9 collective-permute-done.12
  196.7 0.6 slice_dynamic-update-slice_fusion.1
  197.3 0.6 slice_dynamic-update-slice_fusion
  197.9 11.1 %all-to-all-start.1 = ((bf16[128,2,64,128]{3,2,1,0:T(8,128)(2,1)}), bf16[128,2,64,128]{3,2,1,0:T(8,128)(2,1)}, u32[]{:S(2)}, u32[]{:S(2)}) async-start(bf16[128,2,64,128]{3,2,1,0:T(8,128)(2,1)} %slice_dynamic-update-slice_fusion), calls=%async_computation.1 | async-start | bytes 8388608 | tf_op jit(solution)/shard_map/all_to_all | solution.py:331
  209.0 3.4 %collective-permute-start.14 = (bf16[2,64,2048]{2,1,0:T(8,128)(2,1)}, bf16[2,64,2048]{2,1,0:T(8,128)(2,1)S(1)}, u32[]{:S(2)}, u32[]{:S(2)}) collective-permute-start(bf16[2,64,2048]{2,1,0:T(8,128)(2,1)} %get-tuple-element.54), channel_id=1, source_target_pairs={{0,2},{2,4},{4,6},{6,8},{8,10},{10,12},{12,14},{14,16},{16,18},{18... | collective-permute-start | bytes 1572872 | tf_op jit(solution)/shard_map/ppermute | solution.py:278
  212.4 6.7 %collective-permute-start.15 = (bf16[2,64,2048]{2,1,0:T(8,128)(2,1)}, bf16[2,64,2048]{2,1,0:T(8,128)(2,1)S(1)}, u32[]{:S(2)}, u32[]{:S(2)}) collective-permute-start(bf16[2,64,2048]{2,1,0:T(8,128)(2,1)} %copy-done.7), channel_id=1, source_target_pairs={{2,0},{4,2},{6,4},{8,6},{10,8},{12,10},{14,12},{16,14},{18,16},{20... | collective-permute-start | bytes 1572872 | tf_op jit(solution)/shard_map/ppermute | solution.py:278
  219.1 92.1 %collective-permute-done.14.low_ref = bf16[2,64,2048]{2,1,0:T(8,128)(2,1)S(1)} collective-permute-done((bf16[2,64,2048]{2,1,0:T(8,128)(2,1)}, bf16[2,64,2048]{2,1,0:T(8,128)(2,1)S(1)}, u32[]{:S(2)}, u32[]{:S(2)}) %collective-permute-start.14) | collective-permute-done | bytes 524320 | tf_op jit(solution)/shard_map/ppermute | solution.py:278
  311.2 7.0 %gather.1 = (bf16[128,2048]{1,0:T(8,128)(2,1)}, bf16[128,2048]{1,0:T(8,128)(2,1)}) custom-call(s32[128]{0:T(128)S(1)} %get-tuple-element.60.item_ref, bf16[128,2,64,128]{3,2,1,0:T(8,128)(2,1)} %all-to-all-done.1.terms_ref, f32[2,128,2048]{2,1,0:T(8,128)S(1)} %copy-done.4, bf16[2,64,2048]{2,1,0:T(8,128)(2,1)S(1)} %collective-permute-done.14.low_ref, ...), custom_call_target="tpu_custom_call" | custom-call | flops 1000000 | bytes 9437184 | tf_op jit(solution)/shard_map/gather/pallas_call | solution.py:252
  (30 shorter events, 0.2 us)
Async XLA Ops:
  1.8 1.0 copy-start
  2.8 1.0 copy-start.2
  8.8 0.8 copy-start.8
  9.6 133.1 %copy-start.9 = (s32[256,16,3]{0,1,2:T(8,128)S(1)}, s32[256,16,3]{0,1,2:T(8,128)}, u32[]{:S(2)}) copy-start(s32[256,16,3]{0,1,2:T(8,128)} %param.13) | copy-start | bytes 147460
  9.6 145.3 %copy-start.1 = (bf16[128,2048]{1,0:T(8,128)(2,1)S(1)}, bf16[128,2048]{1,0:T(8,128)(2,1)}, u32[]{:S(2)}) copy-start(bf16[128,2048]{1,0:T(8,128)(2,1)} %key_ref.3) | copy-start | bytes 1572868
  9.6 145.3 %copy-start.3 = (bf16[128,2048]{1,0:T(8,128)(2,1)S(1)}, bf16[128,2048]{1,0:T(8,128)(2,1)}, u32[]{:S(2)}) copy-start(bf16[128,2048]{1,0:T(8,128)(2,1)} %value_ref.3) | copy-start | bytes 1572868
  9.6 145.3 %copy-start.5 = (bf16[128,2048]{1,0:T(8,128)(2,1)S(1)}, bf16[128,2048]{1,0:T(8,128)(2,1)}, u32[]{:S(2)}) copy-start(bf16[128,2048]{1,0:T(8,128)(2,1)} %query_ref.1) | copy-start | bytes 1572868
  9.6 145.3 %copy-start.6 = (bf16[128,2048]{1,0:T(8,128)(2,1)S(1)}, bf16[128,2048]{1,0:T(8,128)(2,1)}, u32[]{:S(2)}) copy-start(bf16[128,2048]{1,0:T(8,128)(2,1)} %grad_ref.1) | copy-start | bytes 1572868
  9.6 121.7 %all-to-all-start = ((bf16[128,2,64,128]{3,2,1,0:T(8,128)(2,1)}), bf16[128,2,64,128]{3,2,1,0:T(8,128)(2,1)}, u32[]{:S(2)}, u32[]{:S(2)}) async-start(bf16[128,2,64,128]{3,2,1,0:T(8,128)(2,1)} %get-tuple-element.43), calls=%async_computation | async-start | bytes 8388608 | tf_op jit(solution)/shard_map/all_to_all | solution.py:321
  26.1 105.2 %collective-permute-start = (bf16[2,64,2048]{2,1,0:T(8,128)(2,1)}, bf16[2,64,2048]{2,1,0:T(8,128)(2,1)S(1)}, u32[]{:S(2)}, u32[]{:S(2)}) collective-permute-start(bf16[2,64,2048]{2,1,0:T(8,128)(2,1)} %get-tuple-element.44), channel_id=1, source_target_pairs={{0,2},{2,4},{4,6},{6,8},{8,10},{10,12},{12,14},{14,16},{16,18},{18... | collective-permute-start | bytes 1572872 | tf_op jit(solution)/shard_map/ppermute | solution.py:278
  29.5 101.8 %collective-permute-start.1 = (bf16[2,64,2048]{2,1,0:T(8,128)(2,1)}, bf16[2,64,2048]{2,1,0:T(8,128)(2,1)S(1)}, u32[]{:S(2)}, u32[]{:S(2)}) collective-permute-start(bf16[2,64,2048]{2,1,0:T(8,128)(2,1)} %copy-done.8), channel_id=1, source_target_pairs={{2,0},{4,2},{6,4},{8,6},{10,8},{12,10},{14,12},{16,14},{18,16},{20... | collective-permute-start | bytes 1572872 | tf_op jit(solution)/shard_map/ppermute | solution.py:278
  132.1 5.9 %collective-permute-start.3 = (bf16[2,2,64,128]{3,2,1,0:T(8,128)(2,1)S(1)}, bf16[2,2,64,128]{3,2,1,0:T(8,128)(2,1)S(1)}, u32[]{:S(2)}, u32[]{:S(2)}) collective-permute-start(bf16[2,2,64,128]{3,2,1,0:T(8,128)(2,1)S(1)} %get-tuple-element.73), channel_id=1, source_target_pairs={{0,32},{2,34},{4,36},{6,38},{8,40},{10,42},{12,44},{14,46},{16,48}... | collective-permute-start | bytes 196616 | tf_op jit(solution)/shard_map/ppermute | solution.py:278
  132.9 5.8 %collective-permute-start.2 = (bf16[2,2,64,128]{3,2,1,0:T(8,128)(2,1)S(1)}, bf16[2,2,64,128]{3,2,1,0:T(8,128)(2,1)S(1)}, u32[]{:S(2)}, u32[]{:S(2)}) collective-permute-start(bf16[2,2,64,128]{3,2,1,0:T(8,128)(2,1)S(1)} %get-tuple-element.73), channel_id=1, source_target_pairs={{0,16},{2,18},{4,20},{6,22},{8,24},{10,26},{12,28},{14,30},{16,32}... | collective-permute-start | bytes 196616 | tf_op jit(solution)/shard_map/ppermute | solution.py:278
  133.8 4.9 %collective-permute-start.4 = (bf16[2,2,64,128]{3,2,1,0:T(8,128)(2,1)S(1)}, bf16[2,2,64,128]{3,2,1,0:T(8,128)(2,1)S(1)}, u32[]{:S(2)}, u32[]{:S(2)}) collective-permute-start(bf16[2,2,64,128]{3,2,1,0:T(8,128)(2,1)S(1)} %get-tuple-element.73), channel_id=1, source_target_pairs={{0,48},{2,50},{4,52},{6,54},{8,56},{10,58},{12,60},{14,62},{16,0},... | collective-permute-start | bytes 196616 | tf_op jit(solution)/shard_map/ppermute | solution.py:278
  139.4 10.5 %collective-permute-start.6 = (bf16[4,2,2,64,128]{4,3,2,1,0:T(8,128)(2,1)}, bf16[4,2,2,64,128]{4,3,2,1,0:T(8,128)(2,1)}, u32[]{:S(2)}, u32[]{:S(2)}) collective-permute-start(bf16[4,2,2,64,128]{4,3,2,1,0:T(8,128)(2,1)} %get-tuple-element.71), channel_id=1, source_target_pairs={{0,128},{2,130},{4,132},{6,134},{8,136},{10,138},{12,140},{14,142}... | collective-permute-start | bytes 786440 | tf_op jit(solution)/shard_map/ppermute | solution.py:278
  140.6 9.7 %collective-permute-start.5 = (bf16[4,2,2,64,128]{4,3,2,1,0:T(8,128)(2,1)}, bf16[4,2,2,64,128]{4,3,2,1,0:T(8,128)(2,1)}, u32[]{:S(2)}, u32[]{:S(2)}) collective-permute-start(bf16[4,2,2,64,128]{4,3,2,1,0:T(8,128)(2,1)} %get-tuple-element.71), channel_id=1, source_target_pairs={{0,64},{2,66},{4,68},{6,70},{8,72},{10,74},{12,76},{14,78},{16,80}... | collective-permute-start | bytes 786440 | tf_op jit(solution)/shard_map/ppermute | solution.py:278
  142.5 10.1 %collective-permute-start.7 = (bf16[4,2,2,64,128]{4,3,2,1,0:T(8,128)(2,1)}, bf16[4,2,2,64,128]{4,3,2,1,0:T(8,128)(2,1)}, u32[]{:S(2)}, u32[]{:S(2)}) collective-permute-start(bf16[4,2,2,64,128]{4,3,2,1,0:T(8,128)(2,1)} %get-tuple-element.71), channel_id=1, source_target_pairs={{0,192},{2,194},{4,196},{6,198},{8,200},{10,202},{12,204},{14,206}... | collective-permute-start | bytes 786440 | tf_op jit(solution)/shard_map/ppermute | solution.py:278
  173.2 24.1 %copy-start.7 = (bf16[2,64,2048]{2,1,0:T(8,128)(2,1)}, bf16[2,64,2048]{2,1,0:T(8,128)(2,1)S(1)}, u32[]{:S(2)}) copy-start(bf16[2,64,2048]{2,1,0:T(8,128)(2,1)S(1)} %get-tuple-element.55) | copy-start | bytes 1572868
  173.2 9.1 %collective-permute-start.8 = (bf16[4,2,2,64,128]{4,3,2,1,0:T(8,128)(2,1)S(1)}, bf16[4,2,2,64,128]{4,3,2,1,0:T(8,128)(2,1)S(1)}, u32[]{:S(2)}, u32[]{:S(2)}) collective-permute-start(bf16[4,2,2,64,128]{4,3,2,1,0:T(8,128)(2,1)S(1)} %get-tuple-element.64), channel_id=1, source_target_pairs={{0,64},{2,66},{4,68},{6,70},{8,72},{10,74},{12,76},{14,78},{16,80}... | collective-permute-start | bytes 786440 | tf_op jit(solution)/shard_map/ppermute | solution.py:278
  173.9 13.2 %collective-permute-start.10 = (bf16[4,2,2,64,128]{4,3,2,1,0:T(8,128)(2,1)S(1)}, bf16[4,2,2,64,128]{4,3,2,1,0:T(8,128)(2,1)S(1)}, u32[]{:S(2)}, u32[]{:S(2)}) collective-permute-start(bf16[4,2,2,64,128]{4,3,2,1,0:T(8,128)(2,1)S(1)} %get-tuple-element.65), channel_id=1, source_target_pairs={{0,192},{2,194},{4,196},{6,198},{8,200},{10,202},{12,204},{14,206}... | collective-permute-start | bytes 786440 | tf_op jit(solution)/shard_map/ppermute | solution.py:278
  175.3 11.7 %collective-permute-start.9 = (bf16[4,2,2,64,128]{4,3,2,1,0:T(8,128)(2,1)S(1)}, bf16[4,2,2,64,128]{4,3,2,1,0:T(8,128)(2,1)S(1)}, u32[]{:S(2)}, u32[]{:S(2)}) collective-permute-start(bf16[4,2,2,64,128]{4,3,2,1,0:T(8,128)(2,1)S(1)} %get-tuple-element.66), channel_id=1, source_target_pairs={{0,128},{2,130},{4,132},{6,134},{8,136},{10,138},{12,140},{14,142}... | collective-permute-start | bytes 786440 | tf_op jit(solution)/shard_map/ppermute | solution.py:278
  187.3 6.4 %collective-permute-start.11 = (bf16[2,2,64,128]{3,2,1,0:T(8,128)(2,1)S(1)}, bf16[2,2,64,128]{3,2,1,0:T(8,128)(2,1)S(1)}, u32[]{:S(2)}, u32[]{:S(2)}) collective-permute-start(bf16[2,2,64,128]{3,2,1,0:T(8,128)(2,1)S(1)} %get-tuple-element.67), channel_id=1, source_target_pairs={{0,16},{2,18},{4,20},{6,22},{8,24},{10,26},{12,28},{14,30},{16,32}... | collective-permute-start | bytes 196616 | tf_op jit(solution)/shard_map/ppermute | solution.py:278
  189.2 4.5 %collective-permute-start.13 = (bf16[2,2,64,128]{3,2,1,0:T(8,128)(2,1)S(1)}, bf16[2,2,64,128]{3,2,1,0:T(8,128)(2,1)S(1)}, u32[]{:S(2)}, u32[]{:S(2)}) collective-permute-start(bf16[2,2,64,128]{3,2,1,0:T(8,128)(2,1)S(1)} %get-tuple-element.68), channel_id=1, source_target_pairs={{0,48},{2,50},{4,52},{6,54},{8,56},{10,58},{12,60},{14,62},{16,0},... | collective-permute-start | bytes 196616 | tf_op jit(solution)/shard_map/ppermute | solution.py:278
  190.9 5.8 %collective-permute-start.12 = (bf16[2,2,64,128]{3,2,1,0:T(8,128)(2,1)S(1)}, bf16[2,2,64,128]{3,2,1,0:T(8,128)(2,1)S(1)}, u32[]{:S(2)}, u32[]{:S(2)}) collective-permute-start(bf16[2,2,64,128]{3,2,1,0:T(8,128)(2,1)S(1)} %get-tuple-element.69), channel_id=1, source_target_pairs={{0,32},{2,34},{4,36},{6,38},{8,40},{10,42},{12,44},{14,46},{16,48}... | collective-permute-start | bytes 196616 | tf_op jit(solution)/shard_map/ppermute | solution.py:278
  197.9 113.3 %copy-start.4 = (f32[2,128,2048]{2,1,0:T(8,128)S(1)}, f32[2,128,2048]{2,1,0:T(8,128)}, u32[]{:S(2)}) copy-start(f32[2,128,2048]{2,1,0:T(8,128)} %get-tuple-element.53.own_ref) | copy-start | bytes 6291460
  197.9 113.3 %all-to-all-start.1 = ((bf16[128,2,64,128]{3,2,1,0:T(8,128)(2,1)}), bf16[128,2,64,128]{3,2,1,0:T(8,128)(2,1)}, u32[]{:S(2)}, u32[]{:S(2)}) async-start(bf16[128,2,64,128]{3,2,1,0:T(8,128)(2,1)} %slice_dynamic-update-slice_fusion), calls=%async_computation.1 | async-start | bytes 8388608 | tf_op jit(solution)/shard_map/all_to_all | solution.py:331
  209.0 102.2 %collective-permute-start.14 = (bf16[2,64,2048]{2,1,0:T(8,128)(2,1)}, bf16[2,64,2048]{2,1,0:T(8,128)(2,1)S(1)}, u32[]{:S(2)}, u32[]{:S(2)}) collective-permute-start(bf16[2,64,2048]{2,1,0:T(8,128)(2,1)} %get-tuple-element.54), channel_id=1, source_target_pairs={{0,2},{2,4},{4,6},{6,8},{8,10},{10,12},{12,14},{14,16},{16,18},{18... | collective-permute-start | bytes 1572872 | tf_op jit(solution)/shard_map/ppermute | solution.py:278
  212.4 98.8 %collective-permute-start.15 = (bf16[2,64,2048]{2,1,0:T(8,128)(2,1)}, bf16[2,64,2048]{2,1,0:T(8,128)(2,1)S(1)}, u32[]{:S(2)}, u32[]{:S(2)}) collective-permute-start(bf16[2,64,2048]{2,1,0:T(8,128)(2,1)} %copy-done.7), channel_id=1, source_target_pairs={{2,0},{4,2},{6,4},{8,6},{10,8},{12,10},{14,12},{16,14},{18,16},{20... | collective-permute-start | bytes 1572872 | tf_op jit(solution)/shard_map/ppermute | solution.py:278

commit v3 on v2

v3 whole, which is shorter than its diff:
```python
import math

import jax
import jax.numpy as jnp
from jax import lax
from jax.experimental import pallas as pl
from jax.experimental.pallas import tpu as pltpu
from jax.sharding import PartitionSpec as P

DH = 128
BLOCK = 64
HEADS = 16
SHARDS = 128
LAST = SHARDS - 1
PICKS = 3 * HEADS
NX, NY, NZ = 4, 4, 8
VMEM_BYTES = 32 * 2**20
MASKED = -1e30
SCALE = 1.0 / math.sqrt(DH)
EXP2_SCALE = SCALE * math.log2(math.e)
BF16 = jnp.bfloat16
F32 = jnp.float32

IN_VMEM = pl.BlockSpec(memory_space=pltpu.VMEM)
IN_SMEM = pl.BlockSpec(memory_space=pltpu.SMEM)


def params():
    return pltpu.CompilerParams(vmem_limit_bytes=VMEM_BYTES)


def cost(flops, moved, exps=0):
    return pl.CostEstimate(flops=flops, bytes_accessed=moved, transcendentals=exps)


def lanes(head):
    return pl.ds(pl.multiple_of(head * DH, DH), DH)


def rows(block):
    return pl.ds(pl.multiple_of(block * BLOCK, BLOCK), BLOCK)


def nt(a, b):
    return lax.dot_general(a, b, (((1,), (1,)), ((), ())), preferred_element_type=F32)


def nn(a, b):
    return lax.dot_general(a, b, (((1,), (0,)), ((), ())), preferred_element_type=F32)


def tn(a, b):
    return lax.dot_general(a, b, (((0,), (0,)), ((), ())), preferred_element_type=F32)


def pack_kernel(item_ref, key_ref, value_ref, slots_ref, sem):
    def moves(slot):
        item = item_ref[slot]
        block, head = item >> 4, item & 15
        return [
            pltpu.make_async_copy(
                ref.at[rows(block), lanes(head)], slots_ref.at[slot, side], sem.at[side]
            )
            for side, ref in enumerate((key_ref, value_ref))
        ]

    def start(slot, carry):
        for move in moves(slot):
            move.start()
        return carry

    lax.fori_loop(0, SHARDS, start, 0, unroll=8)
    for side in range(2):
        whole = slots_ref.at[:, side]
        pltpu.make_async_copy(whole, whole, sem.at[side]).wait()


def pack(items, key_states, values):
    return pl.pallas_call(
        pack_kernel,
        in_specs=[IN_SMEM, IN_VMEM, IN_VMEM],
        out_specs=pl.BlockSpec(memory_space=pl.ANY),
        out_shape=jax.ShapeDtypeStruct((SHARDS, 2, BLOCK, DH), BF16),
        scratch_shapes=[pltpu.SemaphoreType.DMA((2,))],
        compiler_params=params(),
        cost_estimate=cost(0, 6 * 2**20),
        name="pack",
    )(items, key_states, values)


HALVES = (slice(0, BLOCK), slice(BLOCK, 2 * BLOCK))
NEAR = 6 * BLOCK


def struct(shape, dtype=F32):
    return jax.ShapeDtypeStruct(shape, dtype)


def both(of):
    return jnp.concatenate([of(0), of(1)])


def owners_of(pick_ref, head):
    return [[pick_ref[b * PICKS + head * 3 + r] >> 1 for r in range(3)] for b in range(2)]


def near_blocks(side, at, edges, far_ref, owners):
    return [
        jnp.concatenate([edges[b][side, :, at]] + [far_ref[o, side] for o in owners[b]])
        for b in range(2)
    ]


def near_kernel(
    pick_ref,
    where_ref,
    query_ref,
    grad_ref,
    key_ref,
    value_ref,
    far_ref,
    prev_ref,
    next_ref,
    exp_ref,
    wgrad_ref,
    part_ref,
    top_ref,
    sum_ref,
):
    shard = where_ref[0]
    column = lax.broadcasted_iota(jnp.int32, (1, 4 * BLOCK), 1)
    bias = [
        jnp.where((shard == end) & (column < BLOCK), MASKED, 0.0) for end in (0, LAST)
    ]
    edges = (prev_ref, next_ref)

    def one(head, carry):
        at = lanes(head)
        query, grad = query_ref[:, at], grad_ref[:, at]
        key, value = key_ref[:, at], value_ref[:, at]
        owners = owners_of(pick_ref, head)
        keys = near_blocks(0, at, edges, far_ref, owners)
        values = near_blocks(1, at, edges, far_ref, owners)
        score_a = nt(query, key)
        score_b = both(lambda b: nt(query[HALVES[b]], keys[b]) + bias[b])
        score = jnp.concatenate([score_a, score_b], axis=1)
        top = jnp.max(score, axis=1, keepdims=True)
        exps = jnp.exp2((score - top) * EXP2_SCALE)
        top_ref[head] = top
        sum_ref[head] = jnp.sum(exps, axis=1, keepdims=True)
        exp_ref[head] = exps
        low = exps.astype(BF16)
        low_a, low_b = low[:, : 2 * BLOCK], low[:, 2 * BLOCK :]
        part_ref[head] = nn(low_a, value) + both(lambda b: nn(low_b[HALVES[b]], values[b]))
        wgrad_ref[head, :, : 2 * BLOCK] = nt(grad, value)
        for b in range(2):
            wgrad_ref[head, HALVES[b], 2 * BLOCK :] = nt(grad[HALVES[b]], values[b])
        return carry

    lax.fori_loop(0, HEADS, one, 0, unroll=4)


def near(picks, where, query, grad, key, value, far, prev, following):
    wide = struct((HEADS, 2 * BLOCK, NEAR))
    stat = struct((HEADS, 2 * BLOCK, 1))
    return pl.pallas_call(
        near_kernel,
        in_specs=[IN_SMEM, IN_SMEM] + [IN_VMEM] * 7,
        out_specs=[IN_VMEM] * 5,
        out_shape=[wide, wide, struct((HEADS, 2 * BLOCK, DH)), stat, stat],
        compiler_params=params(),
        cost_estimate=cost(6 * 10**8, 16 * 2**20, 10**6),
        name="near",
    )(picks, where, query, grad, key, value, far, prev, following)


def ends_kernel(
    where_ref,
    query_ref,
    grad_ref,
    part_ref,
    top_ref,
    sum_ref,
    ends0_ref,
    ends1_ref,
    ends2_ref,
    ends3_ref,
    attended_ref,
    query_part_ref,
    factor_ref,
    dot_ref,
    terms0_ref,
    terms1_ref,
    terms2_ref,
    terms3_ref,
):
    shard, my_x, my_y = where_ref[0], where_ref[1], where_ref[2]
    column = lax.broadcasted_iota(jnp.int32, (1, 2 * BLOCK), 1)
    no_end = ((shard == 0) & (column < BLOCK)) | ((shard == LAST) & (column >= BLOCK))
    bias = jnp.where(no_end, MASKED, 0.0)
    ends_refs = (ends0_ref, ends1_ref, ends2_ref, ends3_ref)
    terms_refs = (terms0_ref, terms1_ref, terms2_ref, terms3_ref)

    def one(ends_ref, terms_ref, head_x, y):
        head = head_x * 4 + ((my_y - y) & 3)
        to_y = (4 - y) & 3
        at = lanes(head)
        query, grad = query_ref[:, at], grad_ref[:, at]
        key = jnp.concatenate([ends_ref[y, 0, 0], ends_ref[y, 1, 0]])
        value = jnp.concatenate([ends_ref[y, 0, 1], ends_ref[y, 1, 1]])
        score = nt(query, key) + bias
        top = jnp.maximum(top_ref[head], jnp.max(score, axis=1, keepdims=True))
        exps = jnp.exp2((score - top) * EXP2_SCALE)
        shrink = jnp.exp2((top_ref[head] - top) * EXP2_SCALE)
        inverse = 1.0 / (sum_ref[head] * shrink + jnp.sum(exps, axis=1, keepdims=True))
        factor = shrink * inverse
        weight = exps * inverse
        low = weight.astype(BF16)
        attended = (part_ref[head] * factor + nn(low, value)).astype(BF16)
        attended_ref[:, at] = attended
        row_dot = jnp.sum(grad.astype(F32) * attended.astype(F32), axis=1, keepdims=True)
        sgrad = (weight * (nt(grad, value) - row_dot) * SCALE).astype(BF16)
        factor_ref[head] = factor
        dot_ref[head] = row_dot
        query_part_ref[head] = nn(sgrad, key)
        for side, left, right in ((0, sgrad, query), (1, low, grad)):
            terms = tn(left, right).astype(BF16)
            terms_ref[to_y, 0, side] = terms[:BLOCK]
            terms_ref[to_y, 1, side] = terms[BLOCK:]

    for x in range(NX):
        for y in range(NY):
            one(ends_refs[x], terms_refs[-x % NX], (my_x - x) & 3, y)


def ends(where, query, grad, part, top, total, lines):
    stat = struct((HEADS, 2 * BLOCK, 1))
    line = struct((NY, 2, 2, BLOCK, DH), BF16)
    return pl.pallas_call(
        ends_kernel,
        in_specs=[IN_SMEM] + [IN_VMEM] * 9,
        out_specs=[IN_VMEM] * 8,
        out_shape=[struct((2 * BLOCK, HEADS * DH), BF16), struct((HEADS, 2 * BLOCK, DH)), stat, stat]
        + [line] * NX,
        compiler_params=params(),
        cost_estimate=cost(4 * 10**8, 8 * 2**20, 3 * 10**5),
        name="ends",
    )(where, query, grad, part, top, total, *lines)


def rest_kernel(
    pick_ref,
    query_ref,
    grad_ref,
    key_ref,
    far_ref,
    prev_ref,
    next_ref,
    exp_ref,
    wgrad_ref,
    query_part_ref,
    factor_ref,
    dot_ref,
    query_grad_ref,
    terms_ref,
    own_ref,
    prev_terms_ref,
    next_terms_ref,
):
    edges = (prev_ref, next_ref)
    no_rows = jnp.zeros((BLOCK, DH), BF16)

    def split(block_rows):
        return jnp.concatenate(
            [
                jnp.concatenate([block_rows[HALVES[0]], no_rows], axis=1),
                jnp.concatenate([no_rows, block_rows[HALVES[1]]], axis=1),
            ]
        )

    def one(head, carry):
        at = lanes(head)
        query, grad = query_ref[:, at], grad_ref[:, at]
        owners = owners_of(pick_ref, head)
        keys = near_blocks(0, at, edges, far_ref, owners)
        weight = exp_ref[head] * factor_ref[head]
        low = weight.astype(BF16)
        sgrad = (weight * (wgrad_ref[head] - dot_ref[head]) * SCALE).astype(BF16)
        sgrad_b = sgrad[:, 2 * BLOCK :]
        query_grad = query_part_ref[head] + nn(sgrad[:, : 2 * BLOCK], key_ref[:, at])
        query_grad = query_grad + both(lambda b: nn(sgrad_b[HALVES[b]], keys[b]))
        query_grad_ref[:, at] = query_grad.astype(BF16)
        for side, left, right in ((0, sgrad, query), (1, low, grad)):
            own_ref[side, :, at] = tn(left[:, : 2 * BLOCK], right)
            parts = tn(left[:, 2 * BLOCK :], split(right)).astype(BF16)
            for b, edge_ref in enumerate((prev_terms_ref, next_terms_ref)):
                part = parts[:, b * DH : (b + 1) * DH]
                edge_ref[side, :, at] = part[:BLOCK]
                for r in range(3):
                    terms_ref[owners[b][r], side] = part[(r + 1) * BLOCK : (r + 2) * BLOCK]
        return carry

    lax.fori_loop(0, HEADS, one, 0, unroll=4)


def rest(picks, query, grad, key, far, prev, following, exps, wgrads, query_part, factor, dots):
    edge = struct((2, BLOCK, HEADS * DH), BF16)
    return pl.pallas_call(
        rest_kernel,
        in_specs=[IN_SMEM] + [IN_VMEM] * 11,
        out_specs=[IN_VMEM] * 5,
        out_shape=[
            struct((2 * BLOCK, HEADS * DH), BF16),
            struct((SHARDS, 2, BLOCK, DH), BF16),
            struct((2, 2 * BLOCK, HEADS * DH)),
            edge,
            edge,
        ],
        compiler_params=params(),
        cost_estimate=cost(8 * 10**8, 20 * 2**20),
        name="rest",
    )(picks, query, grad, key, far, prev, following, exps, wgrads, query_part, factor, dots)


def gather_kernel(
    order_ref, begin_ref, terms_ref, own_ref, low_ref, high_ref, key_ref, value_ref
):
    edges = (low_ref, high_ref)
    outs = (key_ref, value_ref)
    for block in range(2):
        for head in range(HEADS):
            item = block * HEADS + head
            at = slice(head * DH, (head + 1) * DH)

            def add(place, totals):
                slot = order_ref[place]
                return tuple(totals[side] + terms_ref[slot, side].astype(F32) for side in range(2))

            totals = tuple(
                own_ref[side, HALVES[block], at] + edges[block][side, :, at].astype(F32)
                for side in range(2)
            )
            totals = lax.fori_loop(begin_ref[item], begin_ref[item + 1], add, totals)
            for side in range(2):
                outs[side][HALVES[block], at] = totals[side].astype(BF16)


def gather(order, begins, terms, own, low, high):
    flat = struct((2 * BLOCK, HEADS * DH), BF16)
    return pl.pallas_call(
        gather_kernel,
        in_specs=[IN_SMEM, IN_SMEM] + [IN_VMEM] * 4,
        out_specs=[IN_VMEM] * 2,
        out_shape=[flat, flat],
        compiler_params=params(),
        cost_estimate=cost(10**6, 9 * 2**20),
        name="gather",
    )(order, begins, terms, own, low, high)


def shard_of(x, y, z):
    return (x % NX * NY + y % NY) * NZ + z


def send(value, route):
    return lax.ppermute(value, "seq", route)


def x_shift(by):
    cells = [(x, y, z) for x in range(NX) for y in range(NY) for z in range(NZ)]
    return [(shard_of(x, y, z), shard_of(x + by, y, z)) for x, y, z in cells]


def y_shift(by):
    cells = [(x, y, z) for x in range(NX) for y in range(NY) for z in range(NZ)]
    return [(shard_of(x, y, z), shard_of(x, y + by, z)) for x, y, z in cells]


def spread_ends(pair):
    line = jnp.stack([pair] + [send(pair, y_shift(by)) for by in range(1, NY)])
    return [line] + [send(line, x_shift(by)) for by in range(1, NX)]


def sum_ends(lines):
    line = lines[0].astype(F32)
    for by in range(1, NX):
        line = line + send(lines[by], x_shift(by)).astype(F32)
    low_line = line.astype(BF16)
    pair = line[0]
    for by in range(1, NY):
        pair = pair + send(low_line[by], y_shift(by)).astype(F32)
    return pair.astype(BF16)


def on_device(queries, key_states, values, out_grad, rand_blocks):
    shard = lax.axis_index("seq")
    where = jnp.stack([shard, shard // (NY * NZ), shard // NZ % NY]).astype(jnp.int32)
    wanted = rand_blocks // 2 == shard
    item = rand_blocks % 2 * HEADS + lax.broadcasted_iota(jnp.int32, rand_blocks.shape, 1)
    items = jnp.max(jnp.where(wanted, item, -1), axis=(1, 2))
    items = jnp.max(items.reshape(SHARDS, 2), axis=1)
    cell = jnp.arange(SHARDS, dtype=jnp.int32) // NZ
    items = jnp.where(shard == 0, cell, jnp.where(shard == LAST, HEADS + cell, items))
    picks = lax.dynamic_slice_in_dim(rand_blocks, 2 * shard, 2, 0).reshape(2 * PICKS)

    named = jnp.where(items < 0, 2 * HEADS, items)
    place = jnp.arange(SHARDS, dtype=jnp.int32)
    before = (named[None, :] < named[:, None]) | (
        (named[None, :] == named[:, None]) & (place[None, :] < place[:, None])
    )
    rank = jnp.sum(before.astype(jnp.int32), axis=1)
    order = jnp.sum(jnp.where(rank[None, :] == place[:, None], place[None, :], 0), axis=1)
    kinds = jnp.arange(2 * HEADS + 1, dtype=jnp.int32)
    begins = jnp.sum((named[None, :] < kinds[:, None]).astype(jnp.int32), axis=1)

    low = jnp.stack([key_states[:BLOCK], values[:BLOCK]])
    high = jnp.stack([key_states[BLOCK:], values[BLOCK:]])
    up, down = [(i, i + 1) for i in range(LAST)], [(i + 1, i) for i in range(LAST)]
    prev, following = send(high, up), send(low, down)
    slots = pack(jnp.maximum(items, 0), key_states, values)
    slots, prev, following = lax.optimization_barrier((slots, prev, following))
    far = lax.all_to_all(slots, "seq", split_axis=0, concat_axis=0, tiled=True)
    lines = spread_ends(jnp.stack([far[0], far[LAST]]))
    exps, wgrads, part, top, total = near(
        picks, where, queries, out_grad, key_states, values, far, prev, following
    )
    attended, query_part, factor, dots, *end_terms = ends(
        where, queries, out_grad, part, top, total, lines
    )
    end_pair = sum_ends(end_terms)
    query_grad, terms, own, prev_terms, next_terms = rest(
        picks, queries, out_grad, key_states, far, prev, following,
        exps, wgrads, query_part, factor, dots,
    )
    terms = terms.at[0].set(end_pair[0]).at[LAST].set(end_pair[1])
    back = lax.all_to_all(terms, "seq", split_axis=0, concat_axis=0, tiled=True)
    from_next, from_prev = send(prev_terms, down), send(next_terms, up)
    key_grad, value_grad = gather(order, begins, back, own, from_prev, from_next)
    return (attended, query_grad, key_grad, value_grad)


def solution(mesh):
    placed = P("seq", "head")
    return jax.shard_map(
        on_device,
        mesh=mesh,
        in_specs=(placed, placed, placed, placed, P(None, "head", None)),
        out_specs=(placed, placed, placed, placed),
        check_vma=False,
    )
```

time: 319 us -> 320 us (level)
  blocking collectives: 0 us -> 108 us
  waiting for transfers between devices: 214 us -> 112 us
  starting transfers between devices: 63.1 us -> 49.4 us
  Pallas kernels: 30.1 us -> 35.6 us
  local copies, waits for them, and re-layouts: 5.51 us -> 10.1 us
    all_to_all x0 -> x1, blocking collectives: none -> 108 us  [on_device(): far = lax.all_to_all(slots, 'seq', split_axis=0, concat_axis=0, tiled=True)]
    ppermute x16, waiting for transfers between devices: 214 us -> 112 us  [send(): return lax.ppermute(value, 'seq', route)]
    all_to_all x1 -> x0, starting transfers between devices: 16.5 us -> none  [on_device(): far = lax.all_to_all(slots, 'seq', split_axis=0, concat_axis=0, tiled=True)]
    pallas_call x3 -> x5, Pallas kernels: 30.1 us -> 35.6 us  [the longest x1 13.5 us: ends(): pl.pallas_call(ends_kernel, in_specs=[IN_SMEM] + [IN_VMEM] * 9, out_specs...]
    unnamed x20 -> x26, local copies, waits for them, and re-layouts: 2.9 us -> 6.98 us
  transfers between devices with their start and end apart: 18 -> 17, of which waited for: 11 -> 10; matrix products, arithmetic and copies ran while one was open for 0% -> 1% of each run, Pallas kernels for 0% -> 5%
where the time goes in v3:
time: 320 us
  waiting for transfers between devices  112 us (35%)
  blocking collectives  108 us (34%)
  starting transfers between devices  49.4 us (15%)
  Pallas kernels  35.6 us (11%)
  local copies, waits for them, and re-layouts  10.1 us (3%)
  other arithmetic  3.52 us (1%)
    ppermute x16, waiting for transfers between devices, send(): return lax.ppermute(value, 'seq', route)  112 us
    all_to_all x1, blocking collectives, on_device(): far = lax.all_to_all(slots, 'seq', split_axis=0, concat_axis=0, tiled=True)  108 us
    ppermute x16, starting transfers between devices, send(): return lax.ppermute(value, 'seq', route)  36.6 us
    pallas_call x1, Pallas kernels, ends(): pl.pallas_call(ends_kernel, in_specs=[IN_SMEM] + [IN_VMEM] * 9, out_specs...  13.5 us
    all_to_all x1, starting transfers between devices, on_device(): back = lax.all_to_all(terms, 'seq', split_axis=0, concat_axis=0, tiled=True)  12.7 us
    pallas_call x1, Pallas kernels, rest(): pl.pallas_call(rest_kernel, in_specs=[IN_SMEM] + [IN_VMEM] * 11, out_spec...  7.97 us
    unnamed x26, local copies, waits for them, and re-layouts  6.98 us
    pallas_call x1, Pallas kernels, near(): pl.pallas_call(near_kernel, in_specs=[IN_SMEM, IN_SMEM] + [IN_VMEM] * 7,...  6.49 us
  transfers between devices with their start and end apart: 17, of which 10 were waited for; matrix products, arithmetic and copies ran while one was open for 1% of the time, Pallas kernels for 5%

profile of v3, /device:TPU:6, one launch (start us, length us, event | category | flops | bytes accessed | tf_op | source)
XLA Modules:
  0.0 319.8 jit_solution(16877759860762440450)
XLA Ops:
  0.7 1.4 slice_bitcast_fusion
  2.0 0.8 pad_maximum_fusion
  2.9 3.8 %collective-permute-start = (bf16[2,64,2048]{2,1,0:T(8,128)(2,1)}, bf16[2,64,2048]{2,1,0:T(8,128)(2,1)S(1)}, u32[]{:S(2)}, u32[]{:S(2)}) collective-permute-start(bf16[2,64,2048]{2,1,0:T(8,128)(2,1)} %pad_maximum_fusion), channel_id=1, source_target_pairs={{0,2},{2,4},{4,6},{6,8},{8,10},{10,12},{12,14},{14,16},{16,18},{18... | collective-permute-start | bytes 1572872 | tf_op jit(solution)/shard_map/ppermute | solution.py:366
  6.7 0.8 pad_maximum_fusion.1
  7.5 8.6 %collective-permute-start.1 = (bf16[2,64,2048]{2,1,0:T(8,128)(2,1)}, bf16[2,64,2048]{2,1,0:T(8,128)(2,1)S(1)}, u32[]{:S(2)}, u32[]{:S(2)}) collective-permute-start(bf16[2,64,2048]{2,1,0:T(8,128)(2,1)} %pad_maximum_fusion.1), channel_id=1, source_target_pairs={{2,0},{4,2},{6,4},{8,6},{10,8},{12,10},{14,12},{16,14},{18,16},{20... | collective-permute-start | bytes 1572872 | tf_op jit(solution)/shard_map/ppermute | solution.py:366
  16.2 0.1 reshape.124
  16.3 0.1 reduce_max.19
  16.5 2.9 pack.1
  19.4 6.1 %collective-permute-done.prev_ref = bf16[2,64,2048]{2,1,0:T(8,128)(2,1)S(1)} collective-permute-done((bf16[2,64,2048]{2,1,0:T(8,128)(2,1)}, bf16[2,64,2048]{2,1,0:T(8,128)(2,1)S(1)}, u32[]{:S(2)}, u32[]{:S(2)}) %collective-permute-start) | collective-permute-done | bytes 524320 | tf_op jit(solution)/shard_map/ppermute | solution.py:366
  25.5 2.1 collective-permute-done.1.next_ref
  27.6 108.4 %all_to_all.10.far_ref = bf16[128,2,64,128]{3,2,1,0:T(8,128)(2,1)S(1)} all-to-all(bf16[128,2,64,128]{3,2,1,0:T(8,128)(2,1)S(1)} %pack.1), channel_id=1, replica_groups=mesh['seq'=128,'head'=2] {'seq'}, dimensions={0} | all-to-all | bytes 8388608 | tf_op jit(solution)/shard_map/all_to_all | solution.py:422
  136.0 1.9 copy-done
  138.0 0.8 collective-permute-start.4
  138.8 1.3 collective-permute-start.2
  140.1 0.7 collective-permute-start.3
  140.7 1.6 collective-permute-done.4
  142.3 1.9 collective-permute-done.2
  144.2 1.6 collective-permute-done.3
  145.8 0.6 copy-done.12
  146.5 0.9 pad_maximum_fusion.2.ends0_ref
  147.4 2.7 collective-permute-start.5
  150.1 1.0 collective-permute-start.7
  151.1 0.2 copy.11
  151.5 2.2 copy-done.1
  153.7 6.5 %near.1 = (f32[16,128,384]{2,1,0:T(8,128)S(1)}, f32[16,128,384]{2,1,0:T(8,128)S(1)}, f32[16,128,128]{2,1,0:T(8,128)S(1)}, f32[16,128,1]{2,1,0:T(8,128)S(1)}, f32[16,128,1]{2,1,0:T(8,128)S(1)}) custom-call(s32[96]{0:T(128)S(1)} %reshape.123.pick_ref, s32[3]{0:T(128)S(1)} %pad_add_fusion.where_ref, bf16[128,2048]{1,0:T(8,128)(2,1)S(1)} %copy-done.3, ...), custom_call_target="tpu_custom_call" | custom-call | flops 600000000 | bytes 16777216 | tf_op jit(solution)/shard_map/near/pallas_call | solution.py:166
  160.2 0.3 collective-permute-done.7.ends3_ref
  160.6 13.5 %ends.1 = (bf16[128,2048]{1,0:T(8,128)(2,1)}, f32[16,128,128]{2,1,0:T(8,128)S(1)}, f32[16,128,1]{2,1,0:T(8,128)S(1)}, f32[16,128,1]{2,1,0:T(8,128)S(1)}, bf16[4,...) custom-call(s32[3]{0:T(128)S(1)} %pad_add_fusion.where_ref, ...), custom_call_target="tpu_custom_call" | custom-call | flops 400000000 | bytes 8388608 | tf_op jit(solution)/shard_map/ends/pallas_call | solution.py:239
  174.0 2.2 collective-permute-start.10
  176.3 1.0 collective-permute-start.8
  177.3 1.1 collective-permute-start.9
  178.3 3.3 %collective-permute-done.10 = bf16[4,2,2,64,128]{4,3,2,1,0:T(8,128)(2,1)S(1)} collective-permute-done((bf16[4,2,2,64,128]{4,3,2,1,0:T(8,128)(2,1)S(1)}, bf16[4,2,2,64,128]{4,3,2,1,0:T(8,128)(2,1)S(1)}, u32[]{:S(2)}, u32[]{:S(2)}) %collective-permute-start.10) | collective-permute-done | bytes 262176 | tf_op jit(solution)/shard_map/ppermute | solution.py:366
  181.6 1.0 collective-permute-done.8
  182.6 2.5 collective-permute-done.9
  185.1 0.2 fusion.14
  185.4 3.0 collective-permute-start.12
  188.5 0.4 collective-permute-start.13
  188.8 8.0 %rest.1 = (bf16[128,2048]{1,0:T(8,128)(2,1)}, bf16[128,2,64,128]{3,2,1,0:T(8,128)(2,1)}, f32[2,128,2048]{2,1,0:T(8,128)S(1)}, bf16[2,64,2048]{2,1,0:T(8,128)(2,1)S(1)}, bf16[2,64,2048]{2,1,0:T(8,128)(2,1)}) custom-call(s32[96]{0:T(128)S(1)} %reshape.123.pick_ref, bf16[128,2048]{1,0:T(8,128)(2,1)S(1)} %copy-done.3, bf16[128,2048]{1,0:T(8,128)(2,1)S(1)} %copy-done.4, ...), custom_call_target="tpu_custom_call" | custom-call | flops 800000000 | bytes 20971520 | tf_op jit(solution)/shard_map/rest/pallas_call | solution.py:308
  196.8 1.4 copy-done.6
  198.2 0.8 copy-done.8
  199.1 0.6 slice_dynamic-update-slice_fusion.1
  199.7 0.6 slice_dynamic-update-slice_fusion
  200.3 12.7 %all-to-all-start.1 = ((bf16[128,2,64,128]{3,2,1,0:T(8,128)(2,1)}), bf16[128,2,64,128]{3,2,1,0:T(8,128)(2,1)}, u32[]{:S(2)}, u32[]{:S(2)}) async-start(bf16[128,2,64,128]{3,2,1,0:T(8,128)(2,1)} %slice_dynamic-update-slice_fusion), calls=%async_computation.1 | async-start | bytes 8388608 | tf_op jit(solution)/shard_map/all_to_all | solution.py:436
  213.1 3.4 %collective-permute-start.14 = (bf16[2,64,2048]{2,1,0:T(8,128)(2,1)}, bf16[2,64,2048]{2,1,0:T(8,128)(2,1)S(1)}, u32[]{:S(2)}, u32[]{:S(2)}) collective-permute-start(bf16[2,64,2048]{2,1,0:T(8,128)(2,1)} %get-tuple-element.70), channel_id=1, source_target_pairs={{0,2},{2,4},{4,6},{6,8},{8,10},{10,12},{12,14},{14,16},{16,18},{18... | collective-permute-start | bytes 1572872 | tf_op jit(solution)/shard_map/ppermute | solution.py:366
  216.4 6.7 %collective-permute-start.15 = (bf16[2,64,2048]{2,1,0:T(8,128)(2,1)}, bf16[2,64,2048]{2,1,0:T(8,128)(2,1)S(1)}, u32[]{:S(2)}, u32[]{:S(2)}) collective-permute-start(bf16[2,64,2048]{2,1,0:T(8,128)(2,1)} %copy-done.8), channel_id=1, source_target_pairs={{2,0},{4,2},{6,4},{8,6},{10,8},{12,10},{14,12},{16,14},{18,16},{20... | collective-permute-start | bytes 1572872 | tf_op jit(solution)/shard_map/ppermute | solution.py:366
  223.2 0.2 convert_reduce_fusion
  223.4 0.1 select_reduce_fusion.order_ref
  223.5 91.5 %collective-permute-done.14.low_ref = bf16[2,64,2048]{2,1,0:T(8,128)(2,1)S(1)} collective-permute-done((bf16[2,64,2048]{2,1,0:T(8,128)(2,1)}, bf16[2,64,2048]{2,1,0:T(8,128)(2,1)S(1)}, u32[]{:S(2)}, u32[]{:S(2)}) %collective-permute-start.14) | collective-permute-done | bytes 524320 | tf_op jit(solution)/shard_map/ppermute | solution.py:366
  315.0 4.8 %gather.1 = (bf16[128,2048]{1,0:T(8,128)(2,1)}, bf16[128,2048]{1,0:T(8,128)(2,1)}) custom-call(s32[128]{0:T(128)S(1)} %select_reduce_fusion.order_ref, s32[33]{0:T(128)S(1)} %convert_reduce_fusion.1.begin_ref, bf16[128,2,64,128]{3,2,1,0:T(8,128)(2,1)} %all-to-all-done.1.terms_ref, f32[2,128,2048]{2,1,0:T(8,128)S(1)} %copy-done.7, ...), custom_call_target="tpu_custom_call" | custom-call | flops 1000000 | bytes 9437184 | tf_op jit(solution)/shard_map/gather/pallas_call | solution.py:350
  (41 shorter events, 0.7 us)
Async XLA Ops:
  0.6 15.8 %copy-start.2 = (bf16[128,2048]{1,0:T(8,128)(2,1)S(1)}, bf16[128,2048]{1,0:T(8,128)(2,1)}, u32[]{:S(2)}) copy-start(bf16[128,2048]{1,0:T(8,128)(2,1)} %key_ref.5) | copy-start | bytes 1572868
  0.6 15.8 %copy-start.5 = (bf16[128,2048]{1,0:T(8,128)(2,1)S(1)}, bf16[128,2048]{1,0:T(8,128)(2,1)}, u32[]{:S(2)}) copy-start(bf16[128,2048]{1,0:T(8,128)(2,1)} %value_ref.3) | copy-start | bytes 1572868
  0.7 15.4 %copy-start.9 = (s32[256,16,3]{0,1,2:T(8,128)S(1)}, s32[256,16,3]{0,1,2:T(8,128)}, u32[]{:S(2)}) copy-start(s32[256,16,3]{0,1,2:T(8,128)} %param.13) | copy-start | bytes 147460
  2.9 22.6 %collective-permute-start = (bf16[2,64,2048]{2,1,0:T(8,128)(2,1)}, bf16[2,64,2048]{2,1,0:T(8,128)(2,1)S(1)}, u32[]{:S(2)}, u32[]{:S(2)}) collective-permute-start(bf16[2,64,2048]{2,1,0:T(8,128)(2,1)} %pad_maximum_fusion), channel_id=1, source_target_pairs={{0,2},{2,4},{4,6},{6,8},{8,10},{10,12},{12,14},{14,16},{16,18},{18... | collective-permute-start | bytes 1572872 | tf_op jit(solution)/shard_map/ppermute | solution.py:366
  7.5 20.0 %collective-permute-start.1 = (bf16[2,64,2048]{2,1,0:T(8,128)(2,1)}, bf16[2,64,2048]{2,1,0:T(8,128)(2,1)S(1)}, u32[]{:S(2)}, u32[]{:S(2)}) collective-permute-start(bf16[2,64,2048]{2,1,0:T(8,128)(2,1)} %pad_maximum_fusion.1), channel_id=1, source_target_pairs={{2,0},{4,2},{6,4},{8,6},{10,8},{12,10},{14,12},{16,14},{18,16},{20... | collective-permute-start | bytes 1572872 | tf_op jit(solution)/shard_map/ppermute | solution.py:366
  19.4 132.2 %copy-start.3 = (bf16[128,2048]{1,0:T(8,128)(2,1)S(1)}, bf16[128,2048]{1,0:T(8,128)(2,1)}, u32[]{:S(2)}) copy-start(bf16[128,2048]{1,0:T(8,128)(2,1)} %query_ref.5) | copy-start | bytes 1572868
  19.4 132.1 %copy-start.4 = (bf16[128,2048]{1,0:T(8,128)(2,1)S(1)}, bf16[128,2048]{1,0:T(8,128)(2,1)}, u32[]{:S(2)}) copy-start(bf16[128,2048]{1,0:T(8,128)(2,1)} %grad_ref.5) | copy-start | bytes 1572868
  136.0 1.9 copy-start
  138.0 4.3 %collective-permute-start.4 = (bf16[2,2,64,128]{3,2,1,0:T(8,128)(2,1)S(1)}, bf16[2,2,64,128]{3,2,1,0:T(8,128)(2,1)S(1)}, u32[]{:S(2)}, u32[]{:S(2)}) collective-permute-start(bf16[2,2,64,128]{3,2,1,0:T(8,128)(2,1)S(1)} %get-tuple-element.88), channel_id=1, source_target_pairs={{0,48},{2,50},{4,52},{6,54},{8,56},{10,58},{12,60},{14,62},{16,0},... | collective-permute-start | bytes 196616 | tf_op jit(solution)/shard_map/ppermute | solution.py:366
  138.8 5.5 %collective-permute-start.2 = (bf16[2,2,64,128]{3,2,1,0:T(8,128)(2,1)S(1)}, bf16[2,2,64,128]{3,2,1,0:T(8,128)(2,1)S(1)}, u32[]{:S(2)}, u32[]{:S(2)}) collective-permute-start(bf16[2,2,64,128]{3,2,1,0:T(8,128)(2,1)S(1)} %get-tuple-element.88), channel_id=1, source_target_pairs={{0,16},{2,18},{4,20},{6,22},{8,24},{10,26},{12,28},{14,30},{16,32}... | collective-permute-start | bytes 196616 | tf_op jit(solution)/shard_map/ppermute | solution.py:366
  140.1 5.8 %collective-permute-start.3 = (bf16[2,2,64,128]{3,2,1,0:T(8,128)(2,1)S(1)}, bf16[2,2,64,128]{3,2,1,0:T(8,128)(2,1)S(1)}, u32[]{:S(2)}, u32[]{:S(2)}) collective-permute-start(bf16[2,2,64,128]{3,2,1,0:T(8,128)(2,1)S(1)} %get-tuple-element.88), channel_id=1, source_target_pairs={{0,32},{2,34},{4,36},{6,38},{8,40},{10,42},{12,44},{14,46},{16,48}... | collective-permute-start | bytes 196616 | tf_op jit(solution)/shard_map/ppermute | solution.py:366
  142.3 3.5 %copy-start.10 = (bf16[2,2,64,128]{3,2,1,0:T(8,128)(2,1)}, bf16[2,2,64,128]{3,2,1,0:T(8,128)(2,1)S(1)}, u32[]{:S(2)}) copy-start(bf16[2,2,64,128]{3,2,1,0:T(8,128)(2,1)S(1)} %collective-permute-done.4) | copy-start | bytes 196612
  144.2 1.6 copy-start.11
  145.8 0.6 copy-start.12
  147.4 12.8 %collective-permute-start.5 = (bf16[4,2,2,64,128]{4,3,2,1,0:T(8,128)(2,1)S(1)}, bf16[4,2,2,64,128]{4,3,2,1,0:T(8,128)(2,1)}, u32[]{:S(2)}, u32[]{:S(2)}) collective-permute-start(bf16[4,2,2,64,128]{4,3,2,1,0:T(8,128)(2,1)S(1)} %pad_maximum_fusion.2.ends0_ref), channel_id=1, source_target_pairs={{0,64},{2,66},{4,68},{6,70},{8,72},{10,74},{12,76},{14,78},{16,80}... | collective-permute-start | bytes 786440 | tf_op jit(solution)/shard_map/ppermute | solution.py:366
  150.1 10.2 %collective-permute-start.6 = (bf16[4,2,2,64,128]{4,3,2,1,0:T(8,128)(2,1)S(1)}, bf16[4,2,2,64,128]{4,3,2,1,0:T(8,128)(2,1)}, u32[]{:S(2)}, u32[]{:S(2)}) collective-permute-start(bf16[4,2,2,64,128]{4,3,2,1,0:T(8,128)(2,1)S(1)} %pad_maximum_fusion.2.ends0_ref), channel_id=1, source_target_pairs={{0,128},{2,130},{4,132},{6,134},{8,136},{10,138},{12,140},{14,142}... | collective-permute-start | bytes 786440 | tf_op jit(solution)/shard_map/ppermute | solution.py:366
  150.1 10.5 %collective-permute-start.7 = (bf16[4,2,2,64,128]{4,3,2,1,0:T(8,128)(2,1)S(1)}, bf16[4,2,2,64,128]{4,3,2,1,0:T(8,128)(2,1)}, u32[]{:S(2)}, u32[]{:S(2)}) collective-permute-start(bf16[4,2,2,64,128]{4,3,2,1,0:T(8,128)(2,1)S(1)} %pad_maximum_fusion.2.ends0_ref), channel_id=1, source_target_pairs={{0,192},{2,194},{4,196},{6,198},{8,200},{10,202},{12,204},{14,206}... | collective-permute-start | bytes 786440 | tf_op jit(solution)/shard_map/ppermute | solution.py:366
  151.5 2.2 copy-start.1
  174.0 7.6 %collective-permute-start.10 = (bf16[4,2,2,64,128]{4,3,2,1,0:T(8,128)(2,1)S(1)}, bf16[4,2,2,64,128]{4,3,2,1,0:T(8,128)(2,1)S(1)}, u32[]{:S(2)}, u32[]{:S(2)}) collective-permute-start(bf16[4,2,2,64,128]{4,3,2,1,0:T(8,128)(2,1)S(1)} %get-tuple-element.68), channel_id=1, source_target_pairs={{0,192},{2,194},{4,196},{6,198},{8,200},{10,202},{12,204},{14,206}... | collective-permute-start | bytes 786440 | tf_op jit(solution)/shard_map/ppermute | solution.py:366
  176.3 6.4 %collective-permute-start.8 = (bf16[4,2,2,64,128]{4,3,2,1,0:T(8,128)(2,1)S(1)}, bf16[4,2,2,64,128]{4,3,2,1,0:T(8,128)(2,1)S(1)}, u32[]{:S(2)}, u32[]{:S(2)}) collective-permute-start(bf16[4,2,2,64,128]{4,3,2,1,0:T(8,128)(2,1)S(1)} %get-tuple-element.66), channel_id=1, source_target_pairs={{0,64},{2,66},{4,68},{6,70},{8,72},{10,74},{12,76},{14,78},{16,80}... | collective-permute-start | bytes 786440 | tf_op jit(solution)/shard_map/ppermute | solution.py:366
  177.3 7.9 %collective-permute-start.9 = (bf16[4,2,2,64,128]{4,3,2,1,0:T(8,128)(2,1)S(1)}, bf16[4,2,2,64,128]{4,3,2,1,0:T(8,128)(2,1)S(1)}, u32[]{:S(2)}, u32[]{:S(2)}) collective-permute-start(bf16[4,2,2,64,128]{4,3,2,1,0:T(8,128)(2,1)S(1)} %get-tuple-element.67), channel_id=1, source_target_pairs={{0,128},{2,130},{4,132},{6,134},{8,136},{10,138},{12,140},{14,142}... | collective-permute-start | bytes 786440 | tf_op jit(solution)/shard_map/ppermute | solution.py:366
  185.4 13.7 %collective-permute-start.11 = (bf16[2,2,64,128]{3,2,1,0:T(8,128)(2,1)S(1)}, bf16[2,2,64,128]{3,2,1,0:T(8,128)(2,1)S(1)}, u32[]{:S(2)}, u32[]{:S(2)}) collective-permute-start(bf16[2,2,64,128]{3,2,1,0:T(8,128)(2,1)S(1)} %get-tuple-element.84), channel_id=1, source_target_pairs={{0,16},{2,18},{4,20},{6,22},{8,24},{10,26},{12,28},{14,30},{16,32}... | collective-permute-start | bytes 196616 | tf_op jit(solution)/shard_map/ppermute | solution.py:366
  185.4 13.6 %collective-permute-start.12 = (bf16[2,2,64,128]{3,2,1,0:T(8,128)(2,1)S(1)}, bf16[2,2,64,128]{3,2,1,0:T(8,128)(2,1)S(1)}, u32[]{:S(2)}, u32[]{:S(2)}) collective-permute-start(bf16[2,2,64,128]{3,2,1,0:T(8,128)(2,1)S(1)} %get-tuple-element.86), channel_id=1, source_target_pairs={{0,32},{2,34},{4,36},{6,38},{8,40},{10,42},{12,44},{14,46},{16,48}... | collective-permute-start | bytes 196616 | tf_op jit(solution)/shard_map/ppermute | solution.py:366
  188.5 10.5 %collective-permute-start.13 = (bf16[2,2,64,128]{3,2,1,0:T(8,128)(2,1)S(1)}, bf16[2,2,64,128]{3,2,1,0:T(8,128)(2,1)S(1)}, u32[]{:S(2)}, u32[]{:S(2)}) collective-permute-start(bf16[2,2,64,128]{3,2,1,0:T(8,128)(2,1)S(1)} %get-tuple-element.85), channel_id=1, source_target_pairs={{0,48},{2,50},{4,52},{6,54},{8,56},{10,58},{12,60},{14,62},{16,0},... | collective-permute-start | bytes 196616 | tf_op jit(solution)/shard_map/ppermute | solution.py:366
  196.8 1.4 copy-start.6
  198.2 0.8 copy-start.8
  200.3 114.7 %copy-start.7 = (f32[2,128,2048]{2,1,0:T(8,128)S(1)}, f32[2,128,2048]{2,1,0:T(8,128)}, u32[]{:S(2)}) copy-start(f32[2,128,2048]{2,1,0:T(8,128)} %copy-done.6) | copy-start | bytes 6291460
  200.3 114.7 %all-to-all-start.1 = ((bf16[128,2,64,128]{3,2,1,0:T(8,128)(2,1)}), bf16[128,2,64,128]{3,2,1,0:T(8,128)(2,1)}, u32[]{:S(2)}, u32[]{:S(2)}) async-start(bf16[128,2,64,128]{3,2,1,0:T(8,128)(2,1)} %slice_dynamic-update-slice_fusion), calls=%async_computation.1 | async-start | bytes 8388608 | tf_op jit(solution)/shard_map/all_to_all | solution.py:436
  213.1 102.0 %collective-permute-start.14 = (bf16[2,64,2048]{2,1,0:T(8,128)(2,1)}, bf16[2,64,2048]{2,1,0:T(8,128)(2,1)S(1)}, u32[]{:S(2)}, u32[]{:S(2)}) collective-permute-start(bf16[2,64,2048]{2,1,0:T(8,128)(2,1)} %get-tuple-element.70), channel_id=1, source_target_pairs={{0,2},{2,4},{4,6},{6,8},{8,10},{10,12},{12,14},{14,16},{16,18},{18... | collective-permute-start | bytes 1572872 | tf_op jit(solution)/shard_map/ppermute | solution.py:366
  216.4 98.6 %collective-permute-start.15 = (bf16[2,64,2048]{2,1,0:T(8,128)(2,1)}, bf16[2,64,2048]{2,1,0:T(8,128)(2,1)S(1)}, u32[]{:S(2)}, u32[]{:S(2)}) collective-permute-start(bf16[2,64,2048]{2,1,0:T(8,128)(2,1)} %copy-done.8), channel_id=1, source_target_pairs={{2,0},{4,2},{6,4},{8,6},{10,8},{12,10},{14,12},{16,14},{18,16},{20... | collective-permute-start | bytes 1572872 | tf_op jit(solution)/shard_map/ppermute | solution.py:366

commit v4 on v3

v4 whole, which is shorter than its diff:
```python
import math

import jax
import jax.numpy as jnp
from jax import lax
from jax.experimental import pallas as pl
from jax.experimental.pallas import tpu as pltpu
from jax.sharding import PartitionSpec as P

DH = 128
BLOCK = 64
HEADS = 16
SHARDS = 128
LAST = SHARDS - 1
PICKS = 3 * HEADS
NX, NY, NZ = 4, 4, 8
VMEM_BYTES = 60 * 2**20
MASKED = -1e30
SCALE = 1.0 / math.sqrt(DH)
EXP2_SCALE = SCALE * math.log2(math.e)
BF16 = jnp.bfloat16
F32 = jnp.float32

IN_VMEM = pl.BlockSpec(memory_space=pltpu.VMEM)
IN_SMEM = pl.BlockSpec(memory_space=pltpu.SMEM)
IN_HBM = pl.BlockSpec(memory_space=pltpu.HBM)


def params():
    return pltpu.CompilerParams(vmem_limit_bytes=VMEM_BYTES)


def cost(flops, moved, exps=0):
    return pl.CostEstimate(flops=flops, bytes_accessed=moved, transcendentals=exps)


def lanes(head):
    return pl.ds(pl.multiple_of(head * DH, DH), DH)


def rows(block):
    return pl.ds(pl.multiple_of(block * BLOCK, BLOCK), BLOCK)


def nt(a, b):
    return lax.dot_general(a, b, (((1,), (1,)), ((), ())), preferred_element_type=F32)


def nn(a, b):
    return lax.dot_general(a, b, (((1,), (0,)), ((), ())), preferred_element_type=F32)


def tn(a, b):
    return lax.dot_general(a, b, (((0,), (0,)), ((), ())), preferred_element_type=F32)


def pack_kernel(item_ref, key_ref, value_ref, slots_ref, sem):
    def moves(slot):
        item = item_ref[slot]
        block, head = item >> 4, item & 15
        return [
            pltpu.make_async_copy(
                ref.at[rows(block), lanes(head)], slots_ref.at[slot, side], sem.at[side]
            )
            for side, ref in enumerate((key_ref, value_ref))
        ]

    def start(slot, carry):
        for move in moves(slot):
            move.start()
        return carry

    lax.fori_loop(0, SHARDS, start, 0, unroll=8)
    for side in range(2):
        whole = slots_ref.at[:, side]
        pltpu.make_async_copy(whole, whole, sem.at[side]).wait()


def pack(items, key_states, values):
    return pl.pallas_call(
        pack_kernel,
        in_specs=[IN_SMEM, IN_VMEM, IN_VMEM],
        out_specs=pl.BlockSpec(memory_space=pl.ANY),
        out_shape=jax.ShapeDtypeStruct((SHARDS, 2, BLOCK, DH), BF16),
        scratch_shapes=[pltpu.SemaphoreType.DMA((2,))],
        compiler_params=params(),
        cost_estimate=cost(0, 6 * 2**20),
        name="pack",
    )(items, key_states, values)


HALVES = (slice(0, BLOCK), slice(BLOCK, 2 * BLOCK))
TOKENS_HERE = 2 * BLOCK
SOME = 4
STEPS = HEADS // SOME


def struct(shape, dtype=F32):
    return jax.ShapeDtypeStruct(shape, dtype)


def flat_spec(where_to):
    return pl.BlockSpec((TOKENS_HERE, SOME * DH), lambda *at: (0, where_to(*at)))


def edge_spec(where_to):
    return pl.BlockSpec((2, BLOCK, SOME * DH), lambda *at: (0, 0, where_to(*at)))


def head_spec(width, where_to):
    return pl.BlockSpec((SOME, TOKENS_HERE, width), lambda *at: (where_to(*at), 0, 0))


def grid_call(kernel, name, flops, moved, prefetch, in_specs, out_specs, out_shape, scratch=()):
    return pl.pallas_call(
        kernel,
        grid_spec=pltpu.PrefetchScalarGridSpec(
            num_scalar_prefetch=prefetch,
            grid=(STEPS,),
            in_specs=in_specs,
            out_specs=out_specs,
            scratch_shapes=scratch,
        ),
        out_shape=out_shape,
        compiler_params=params(),
        cost_estimate=cost(flops, moved, 10**6),
        name=name,
    )


def step_of(i, *scalars):
    return i


def columns_of(i):
    return slice(i * DH, (i + 1) * DH)


def both(of):
    return jnp.concatenate([of(0), of(1)])


def stacked(of):
    return jnp.concatenate([of(i) for i in range(SOME)])


def rows_of(i):
    return slice(i * TOKENS_HERE, (i + 1) * TOKENS_HERE)


def half_rows(i, b):
    return slice((2 * i + b) * BLOCK, (2 * i + b + 1) * BLOCK)


def owner_of(pick_ref, head, b, r):
    return pick_ref[b * PICKS + head * 3 + r] >> 1


def fetch(pick_ref, far_ref, held_ref, sem):
    def one(head, carry):
        for b in range(2):
            for r in range(3):
                source = far_ref.at[owner_of(pick_ref, head, b, r)]
                if len(held_ref.shape) == 4:
                    source = source.at[0]
                target = held_ref.at[head, b * 3 + r]
                pltpu.make_async_copy(source, target, sem.at[head]).start()
        return carry

    lax.fori_loop(0, HEADS, one, 0, unroll=4)


def fetched(held_ref, sem, head):
    pltpu.make_async_copy(held_ref.at[head], held_ref.at[head], sem.at[head]).wait()


def near_kernel(
    pick_ref,
    where_ref,
    query_ref,
    grad_ref,
    key_ref,
    value_ref,
    far_ref,
    prev_ref,
    next_ref,
    own_exp_ref,
    far_exp_ref,
    own_wgrad_ref,
    far_wgrad_ref,
    part_ref,
    stat_ref,
    held_ref,
    sem,
):
    step = pl.program_id(0)

    @pl.when(step == 0)
    def _():
        fetch(pick_ref, far_ref, held_ref, sem)

    shard = where_ref[0]
    column = lax.broadcasted_iota(jnp.int32, (1, 4 * BLOCK), 1)
    bias = [
        jnp.where((shard == end) & (column < BLOCK), MASKED, 0.0) for end in (0, LAST)
    ]
    edges = (prev_ref, next_ref)
    heads = [step * SOME + i for i in range(SOME)]
    queries = [query_ref[:, columns_of(i)] for i in range(SOME)]
    grads = [grad_ref[:, columns_of(i)] for i in range(SOME)]
    for head in heads:
        fetched(held_ref, sem, head)

    def picked(i, b, side):
        edge = edges[b][side, :, columns_of(i)]
        return jnp.concatenate([edge] + [held_ref[heads[i], b * 3 + r, side] for r in range(3)])

    keys, values = (
        [[picked(i, b, side) for b in range(2)] for i in range(SOME)] for side in range(2)
    )
    own_score = stacked(lambda i: nt(queries[i], key_ref[:, columns_of(i)]))
    far_score = stacked(lambda i: both(lambda b: nt(queries[i][HALVES[b]], keys[i][b]) + bias[b]))
    top = jnp.maximum(
        jnp.maximum(own_score, far_score[:, :TOKENS_HERE]), far_score[:, TOKENS_HERE:]
    )
    top = jnp.max(top, axis=1, keepdims=True)
    own_exp = jnp.exp2((own_score - top) * EXP2_SCALE)
    far_exp = jnp.exp2((far_score - top) * EXP2_SCALE)
    total = own_exp + far_exp[:, :TOKENS_HERE] + far_exp[:, TOKENS_HERE:]
    stat = jnp.concatenate([top, jnp.sum(total, axis=1, keepdims=True)], axis=1)
    own_low, far_low = own_exp.astype(BF16), far_exp.astype(BF16)
    for i in range(SOME):
        at = rows_of(i)
        own_exp_ref[i], far_exp_ref[i], stat_ref[i] = own_exp[at], far_exp[at], stat[at]
        own_wgrad_ref[i] = nt(grads[i], value_ref[:, columns_of(i)])
        far_part = both(lambda b: nn(far_low[half_rows(i, b)], values[i][b]))
        part_ref[i] = nn(own_low[at], value_ref[:, columns_of(i)]) + far_part
        for b in range(2):
            far_wgrad_ref[i, HALVES[b]] = nt(grads[i][HALVES[b]], values[i][b])


def near(picks, where, query, grad, key, value, far, prev, following):
    own, wide = (HEADS, TOKENS_HERE, TOKENS_HERE), (HEADS, TOKENS_HERE, 4 * BLOCK)
    return grid_call(
        near_kernel,
        "near",
        6 * 10**8,
        16 * 2**20,
        2,
        [flat_spec(step_of)] * 4 + [IN_HBM] + [edge_spec(step_of)] * 2,
        [head_spec(w, step_of) for w in (DH, 2 * DH, DH, 2 * DH, DH, 2)],
        [struct(own), struct(wide), struct(own), struct(wide), struct(own), struct(own[:2] + (2,))],
        [pltpu.VMEM((HEADS, 6, 2, BLOCK, DH), BF16), pltpu.SemaphoreType.DMA((HEADS,))],
    )(picks, where, query, grad, key, value, far, prev, following)


def ends_kernel(
    where_ref,
    query_ref,
    grad_ref,
    part_ref,
    stat_ref,
    ends0_ref,
    ends1_ref,
    ends2_ref,
    ends3_ref,
    attended_ref,
    query_part_ref,
    factor_ref,
    terms0_ref,
    terms1_ref,
    terms2_ref,
    terms3_ref,
):
    shard, my_y = where_ref[0], where_ref[2]
    column = lax.broadcasted_iota(jnp.int32, (1, TOKENS_HERE), 1)
    no_end = ((shard == 0) & (column < BLOCK)) | ((shard == LAST) & (column >= BLOCK))
    bias = jnp.where(no_end, MASKED, 0.0)
    ends_refs = (ends0_ref, ends1_ref, ends2_ref, ends3_ref)
    terms_refs = (terms0_ref, terms1_ref, terms2_ref, terms3_ref)

    def line(ends_ref, terms_ref):
        heads = [(my_y - y) & 3 for y in range(SOME)]
        queries = [query_ref[:, lanes(head)] for head in heads]
        grads = [grad_ref[:, lanes(head)] for head in heads]
        keys, values = (
            [jnp.concatenate([ends_ref[y, 0, side], ends_ref[y, 1, side]]) for y in range(SOME)]
            for side in range(2)
        )
        score = stacked(lambda i: nt(queries[i], keys[i])) + bias
        stat = stacked(lambda i: stat_ref[heads[i]])
        old_top = stat[:, 0:1]
        top = jnp.maximum(old_top, jnp.max(score, axis=1, keepdims=True))
        exps = jnp.exp2((score - top) * EXP2_SCALE)
        shrink = jnp.exp2((old_top - top) * EXP2_SCALE)
        total = stat[:, 1:2] * shrink
        inverse = 1.0 / (total + jnp.sum(exps, axis=1, keepdims=True))
        factor = shrink * inverse
        weight = exps * inverse
        low = weight.astype(BF16)
        wgrad = stacked(lambda i: nt(grads[i], values[i]))
        attended = stacked(lambda i: part_ref[heads[i]]) * factor
        attended = attended + stacked(lambda i: nn(low[rows_of(i)], values[i]))
        attended = attended.astype(BF16)
        grad = stacked(lambda i: grads[i].astype(F32))
        row_dot = jnp.sum(grad * attended.astype(F32), axis=1, keepdims=True)
        sgrad = (weight * (wgrad - row_dot) * SCALE).astype(BF16)
        stat = jnp.concatenate([factor, row_dot], axis=1)
        for i, head in enumerate(heads):
            at = rows_of(i)
            attended_ref[:, lanes(head)] = attended[at]
            factor_ref[head] = stat[at]
            query_part_ref[head] = nn(sgrad[at], keys[i])
            for side, left, right in ((0, sgrad, queries[i]), (1, low, grads[i])):
                terms = tn(left[at], right).astype(BF16)
                terms_ref[-i % NY, 0, side] = terms[:BLOCK]
                terms_ref[-i % NY, 1, side] = terms[BLOCK:]

    for x in range(NX):
        pl.when(pl.program_id(0) == x)(
            lambda x=x: line(ends_refs[x], terms_refs[-x % NX])
        )


def ends(where, query, grad, part, stat, lines):
    line = struct((NY, 2, 2, BLOCK, DH), BF16)
    line_spec = pl.BlockSpec(line.shape, lambda i, where: (0,) * 5)
    own = (HEADS, TOKENS_HERE, DH)

    def line_heads(i, where):
        return (where[1] - i) & 3

    return grid_call(
        ends_kernel,
        "ends",
        4 * 10**8,
        8 * 2**20,
        1,
        [flat_spec(line_heads)] * 2
        + [head_spec(DH, line_heads), head_spec(2, line_heads)]
        + [line_spec] * NX,
        [flat_spec(line_heads), head_spec(DH, line_heads), head_spec(2, line_heads)]
        + [line_spec] * NX,
        [struct((TOKENS_HERE, HEADS * DH), BF16), struct(own), struct(own[:2] + (2,))]
        + [line] * NX,
    )(where, query, grad, part, stat, *lines)


def far_terms_kernel(
    pick_ref,
    query_ref,
    grad_ref,
    exp_ref,
    wgrad_ref,
    factor_ref,
    terms_ref,
    prev_terms_ref,
    next_terms_ref,
    made_ref,
    sem,
):
    step = pl.program_id(0)
    no_rows = jnp.zeros((BLOCK, DH), BF16)

    def split(block_rows):
        return jnp.concatenate(
            [
                jnp.concatenate([block_rows[HALVES[0]], no_rows], axis=1),
                jnp.concatenate([no_rows, block_rows[HALVES[1]]], axis=1),
            ]
        )

    for i in range(SOME):
        head = step * SOME + i
        at = columns_of(i)
        weight = exp_ref[i] * factor_ref[i, :, 0:1]
        low = weight.astype(BF16)
        sgrad = (weight * (wgrad_ref[i] - factor_ref[i, :, 1:2]) * SCALE).astype(BF16)
        for side, left, right in ((0, sgrad, query_ref[:, at]), (1, low, grad_ref[:, at])):
            parts = tn(left, split(right)).astype(BF16)
            for b, edge_ref in enumerate((prev_terms_ref, next_terms_ref)):
                part = parts[:, columns_of(b)]
                edge_ref[side, :, at] = part[:BLOCK]
                for r in range(3):
                    made_ref[head, b * 3 + r, side] = part[(r + 1) * BLOCK : (r + 2) * BLOCK]
        for b in range(2):
            for r in range(3):
                pltpu.make_async_copy(
                    made_ref.at[head, b * 3 + r],
                    terms_ref.at[owner_of(pick_ref, head, b, r)],
                    sem.at[0],
                ).start()

    @pl.when(step == STEPS - 1)
    def _():
        pltpu.make_async_copy(made_ref, made_ref, sem.at[0]).wait()


def far_terms(picks, query, grad, exps, wgrads, factor):
    edge = struct((2, BLOCK, HEADS * DH), BF16)
    return grid_call(
        far_terms_kernel,
        "far_terms",
        4 * 10**8,
        14 * 2**20,
        1,
        [flat_spec(step_of)] * 2 + [head_spec(w, step_of) for w in (2 * DH, 2 * DH, 2)],
        [IN_HBM, edge_spec(step_of), edge_spec(step_of)],
        [struct((SHARDS, 2, BLOCK, DH), BF16), edge, edge],
        [pltpu.VMEM((HEADS, 6, 2, BLOCK, DH), BF16), pltpu.SemaphoreType.DMA((1,))],
    )(picks, query, grad, exps, wgrads, factor)


def own_terms_kernel(
    pick_ref,
    query_ref,
    grad_ref,
    key_ref,
    far_ref,
    prev_ref,
    next_ref,
    own_exp_ref,
    far_exp_ref,
    own_wgrad_ref,
    far_wgrad_ref,
    query_part_ref,
    factor_ref,
    query_grad_ref,
    own_ref,
    held_ref,
    sem,
):
    step = pl.program_id(0)

    @pl.when(step == 0)
    def _():
        fetch(pick_ref, far_ref, held_ref, sem)

    edges = (prev_ref, next_ref)
    for i in range(SOME):
        head = step * SOME + i
        at = columns_of(i)
        fetched(held_ref, sem, head)
        factor, row_dot = factor_ref[i, :, 0:1], factor_ref[i, :, 1:2]
        weight = own_exp_ref[i] * factor
        sgrad = (weight * (own_wgrad_ref[i] - row_dot) * SCALE).astype(BF16)
        far_sgrad = far_exp_ref[i] * factor * (far_wgrad_ref[i] - row_dot) * SCALE
        far_sgrad = far_sgrad.astype(BF16)

        def far_key(b):
            picked = [held_ref[head, b * 3 + r] for r in range(3)]
            return jnp.concatenate([edges[b][0, :, at]] + picked)

        query_grad = query_part_ref[i] + nn(sgrad, key_ref[:, at])
        query_grad = query_grad + both(lambda b: nn(far_sgrad[HALVES[b]], far_key(b)))
        query_grad_ref[:, at] = query_grad.astype(BF16)
        own_ref[0, :, at] = tn(sgrad, query_ref[:, at])
        own_ref[1, :, at] = tn(weight.astype(BF16), grad_ref[:, at])


def own_terms(picks, query, grad, key, far, prev, following, exps, wgrads, query_part, factor):
    return grid_call(
        own_terms_kernel,
        "own_terms",
        5 * 10**8,
        16 * 2**20,
        1,
        [flat_spec(step_of)] * 3
        + [IN_HBM]
        + [edge_spec(step_of)] * 2
        + [head_spec(w, step_of) for w in (DH, 2 * DH, DH, 2 * DH, DH, 2)],
        [
            flat_spec(step_of),
            pl.BlockSpec((2, TOKENS_HERE, SOME * DH), lambda i, picks: (0, 0, i)),
        ],
        [
            struct((TOKENS_HERE, HEADS * DH), BF16),
            struct((2, TOKENS_HERE, HEADS * DH)),
        ],
        [pltpu.VMEM((HEADS, 6, BLOCK, DH), BF16), pltpu.SemaphoreType.DMA((HEADS,))],
    )(picks, query, grad, key, far, prev, following, *exps, *wgrads, query_part, factor)


def gather_kernel(
    order_ref, begin_ref, terms_ref, own_ref, low_ref, high_ref, key_ref, value_ref
):
    edges = (low_ref, high_ref)
    outs = (key_ref, value_ref)
    for block in range(2):
        for head in range(HEADS):
            item = block * HEADS + head
            at = slice(head * DH, (head + 1) * DH)

            def add(place, totals):
                slot = order_ref[place]
                return tuple(totals[side] + terms_ref[slot, side].astype(F32) for side in range(2))

            totals = tuple(
                own_ref[side, HALVES[block], at] + edges[block][side, :, at].astype(F32)
                for side in range(2)
            )
            totals = lax.fori_loop(begin_ref[item], begin_ref[item + 1], add, totals)
            for side in range(2):
                outs[side][HALVES[block], at] = totals[side].astype(BF16)


def gather(order, begins, terms, own, low, high):
    flat = struct((2 * BLOCK, HEADS * DH), BF16)
    return pl.pallas_call(
        gather_kernel,
        in_specs=[IN_SMEM, IN_SMEM] + [IN_VMEM] * 4,
        out_specs=[IN_VMEM] * 2,
        out_shape=[flat, flat],
        compiler_params=params(),
        cost_estimate=cost(10**6, 9 * 2**20),
        name="gather",
    )(order, begins, terms, own, low, high)


def shard_of(x, y, z):
    return (x % NX * NY + y % NY) * NZ + z


def send(value, route):
    return lax.ppermute(value, "seq", route)


def x_shift(by):
    cells = [(x, y, z) for x in range(NX) for y in range(NY) for z in range(NZ)]
    return [(shard_of(x, y, z), shard_of(x + by, y, z)) for x, y, z in cells]


def y_shift(by):
    cells = [(x, y, z) for x in range(NX) for y in range(NY) for z in range(NZ)]
    return [(shard_of(x, y, z), shard_of(x, y + by, z)) for x, y, z in cells]


def spread_ends(pair):
    line = jnp.stack([pair] + [send(pair, y_shift(by)) for by in range(1, NY)])
    return [line] + [send(line, x_shift(by)) for by in range(1, NX)]


def sum_line(lines):
    line = lines[0].astype(F32)
    for by in range(1, NX):
        line = line + send(lines[by], x_shift(by)).astype(F32)
    return line.astype(BF16), line[0]


def sum_plane(low_line, pair):
    for by in range(1, NY):
        pair = pair + send(low_line[by], y_shift(by)).astype(F32)
    return pair.astype(BF16)


def on_device(queries, key_states, values, out_grad, rand_blocks):
    shard = lax.axis_index("seq")
    where = jnp.stack([shard, shard // (NY * NZ), shard // NZ % NY]).astype(jnp.int32)
    wanted = rand_blocks // 2 == shard
    item = rand_blocks % 2 * HEADS + lax.broadcasted_iota(jnp.int32, rand_blocks.shape, 1)
    items = jnp.max(jnp.where(wanted, item, -1), axis=(1, 2))
    items = jnp.max(items.reshape(SHARDS, 2), axis=1)
    cell = jnp.arange(SHARDS, dtype=jnp.int32) // NZ
    items = jnp.where(shard == 0, cell, jnp.where(shard == LAST, HEADS + cell, items))
    picks = lax.dynamic_slice_in_dim(rand_blocks, 2 * shard, 2, 0).reshape(2 * PICKS)

    named = jnp.where(items < 0, 2 * HEADS, items)
    place = jnp.arange(SHARDS, dtype=jnp.int32)
    before = (named[None, :] < named[:, None]) | (
        (named[None, :] == named[:, None]) & (place[None, :] < place[:, None])
    )
    rank = jnp.sum(before.astype(jnp.int32), axis=1)
    order = jnp.sum(jnp.where(rank[None, :] == place[:, None], place[None, :], 0), axis=1)
    kinds = jnp.arange(2 * HEADS + 1, dtype=jnp.int32)
    begins = jnp.sum((named[None, :] < kinds[:, None]).astype(jnp.int32), axis=1)

    low = jnp.stack([key_states[:BLOCK], values[:BLOCK]])
    high = jnp.stack([key_states[BLOCK:], values[BLOCK:]])
    up, down = [(i, i + 1) for i in range(LAST)], [(i + 1, i) for i in range(LAST)]
    slots = pack(jnp.maximum(items, 0), key_states, values)
    far = lax.all_to_all(slots, "seq", split_axis=0, concat_axis=0, tiled=True)
    far, low, high = lax.optimization_barrier((far, low, high))
    lines = spread_ends(jnp.stack([far[0], far[LAST]]))
    prev, following = send(high, up), send(low, down)
    own_exps, far_exps, own_wgrads, far_wgrads, part, stat = near(
        picks, where, queries, out_grad, key_states, values, far, prev, following
    )
    attended, query_part, factor, *end_terms = ends(where, queries, out_grad, part, stat, lines)
    low_line, pair = sum_line(end_terms)
    terms, prev_terms, next_terms = far_terms(
        picks, queries, out_grad, far_exps, far_wgrads, factor
    )
    low_line, pair, terms = lax.optimization_barrier((low_line, pair, terms))
    end_pair = sum_plane(low_line, pair)
    terms = terms.at[0].set(end_pair[0]).at[LAST].set(end_pair[1])
    back = lax.all_to_all(terms, "seq", split_axis=0, concat_axis=0, tiled=True)
    from_next, from_prev = send(prev_terms, down), send(next_terms, up)
    query_grad, own = own_terms(
        picks, queries, out_grad, key_states, far, prev, following,
        (own_exps, far_exps), (own_wgrads, far_wgrads), query_part, factor,
    )
    key_grad, value_grad = gather(order, begins, back, own, from_prev, from_next)
    return (attended, query_grad, key_grad, value_grad)


def solution(mesh):
    placed = P("seq", "head")
    return jax.shard_map(
        on_device,
        mesh=mesh,
        in_specs=(placed, placed, placed, placed, P(None, "head", None)),
        out_specs=(placed, placed, placed, placed),
        check_vma=False,
    )
```

time: 320 us -> 311 us (0.972)
  blocking collectives: 108 us -> 0 us
  waiting for transfers between devices: 112 us -> 194 us
  starting transfers between devices: 49.4 us -> 60.7 us
  Pallas kernels: 35.6 us -> 44.1 us
  local copies, waits for them, and re-layouts: 10.1 us -> 6.54 us
    all_to_all x1 -> x0, blocking collectives: 108 us -> none  [on_device(): far = lax.all_to_all(slots, 'seq', split_axis=0, concat_axis=0, tiled=True)]
    all_to_all x0 -> x1, waiting for transfers between devices: none -> 96.5 us  [on_device(): far = lax.all_to_all(slots, 'seq', split_axis=0, concat_axis=0, tiled=True)]
    all_to_all x0 -> x1, starting transfers between devices: none -> 16.5 us  [on_device(): far = lax.all_to_all(slots, 'seq', split_axis=0, concat_axis=0, tiled=True)]
    ppermute x16, waiting for transfers between devices: 112 us -> 97.2 us  [send(): return lax.ppermute(value, 'seq', route)]
    pallas_call x3 -> x4, Pallas kernels: 27.9 us -> 35.3 us  [the longest x1 10.2 us: own_terms(): grid_call(own_terms_kernel, 'own_terms', 5 * 10 ** 8, 16 * 2 ** 20, 1, [f...]
    ppermute x16, starting transfers between devices: 36.6 us -> 32.7 us  [send(): return lax.ppermute(value, 'seq', route)]
    unnamed x26 -> x28, local copies, waits for them, and re-layouts: 6.98 us -> 3.3 us
  transfers between devices with their start and end apart: 17 -> 18, of which waited for: 10 -> 11; matrix products, arithmetic and copies ran while one was open for 1% -> 1% of each run, Pallas kernels for 5% -> 9%
where the time goes in v4:
time: 311 us; the launch traced here: 310 us
  waiting for transfers between devices  194 us (62%)
  starting transfers between devices  60.7 us (20%)
  Pallas kernels  44.1 us (14%)
  local copies, waits for them, and re-layouts  6.54 us (2%)
  other arithmetic  4.02 us (1%)
    ppermute x16, waiting for transfers between devices, send(): return lax.ppermute(value, 'seq', route)  97.2 us
    all_to_all x1, waiting for transfers between devices, on_device(): far = lax.all_to_all(slots, 'seq', split_axis=0, concat_axis=0, tiled=True)  96.5 us
    ppermute x16, starting transfers between devices, send(): return lax.ppermute(value, 'seq', route)  32.7 us
    all_to_all x1, starting transfers between devices, on_device(): far = lax.all_to_all(slots, 'seq', split_axis=0, concat_axis=0, tiled=True)  16.5 us
    all_to_all x1, starting transfers between devices, on_device(): back = lax.all_to_all(terms, 'seq', split_axis=0, concat_axis=0, tiled=True)  11.6 us
    pallas_call x1, Pallas kernels, own_terms(): grid_call(own_terms_kernel, 'own_terms', 5 * 10 ** 8, 16 * 2 ** 20, 1, [f...  10.2 us
    pallas_call x1, Pallas kernels, near(): grid_call(near_kernel, 'near', 6 * 10 ** 8, 16 * 2 ** 20, 2, [flat_spec(s...  8.85 us
    pallas_call x1, Pallas kernels, ends(): grid_call(ends_kernel, 'ends', 4 * 10 ** 8, 8 * 2 ** 20, 1, [flat_spec(li...  8.78 us
  transfers between devices with their start and end apart: 18, of which 11 were waited for; matrix products, arithmetic and copies ran while one was open for 1% of the time, Pallas kernels for 9%

profile of v4, /device:TPU:6, one launch (start us, length us, event | category | flops | bytes accessed | tf_op | source)
XLA Modules:
  0.0 310.1 jit_solution(9730758348278601774)
XLA Ops:
  0.6 0.9 fusion.6
  1.5 0.1 reshape.124
  1.7 0.1 reduce_max.19
  1.8 0.5 broadcast_maximum_fusion.item_ref
  2.3 3.2 %pack.1 = bf16[128,2,64,128]{3,2,1,0:T(8,128)(2,1)} custom-call(s32[128]{0:T(128)} %broadcast_maximum_fusion.item_ref, bf16[128,2048]{1,0:T(8,128)(2,1)} %key_ref.5, bf16[128,2048]{1,0:T(8,128)(2,1)} %value_ref.3), custom_call_target="tpu_custom_call" | custom-call | bytes 6291456 | tf_op jit(solution)/shard_map/pack/pallas_call | solution.py:80
  5.5 16.5 %all-to-all-start = ((bf16[128,2,64,128]{3,2,1,0:T(8,128)(2,1)}), bf16[128,2,64,128]{3,2,1,0:T(8,128)(2,1)}, u32[]{:S(2)}, u32[]{:S(2)}) async-start(bf16[128,2,64,128]{3,2,1,0:T(8,128)(2,1)} %pack.1), calls=%async_computation | async-start | bytes 8388608 | tf_op jit(solution)/shard_map/all_to_all | solution.py:581
  22.3 96.5 %all-to-all-done.far_ref = bf16[128,2,64,128]{3,2,1,0:T(8,128)(2,1)} async-done(((bf16[128,2,64,128]{3,2,1,0:T(8,128)(2,1)}), bf16[128,2,64,128]{3,2,1,0:T(8,128)(2,1)}, u32[]{:S(2)}, u32[]{:S(2)}) %all-to-all-start) | async-done | bytes 4194336 | tf_op jit(solution)/shard_map/all_to_all | solution.py:581
  118.8 2.5 collective-permute-start
  121.3 7.6 %collective-permute-start.1 = (bf16[2,64,2048]{2,1,0:T(8,128)(2,1)S(1)}, bf16[2,64,2048]{2,1,0:T(8,128)(2,1)S(1)}, u32[]{:S(2)}, u32[]{:S(2)}) collective-permute-start(bf16[2,64,2048]{2,1,0:T(8,128)(2,1)S(1)} %get-tuple-element.56), channel_id=1, source_target_pairs={{2,0},{4,2},{6,4},{8,6},{10,8},{12,10},{14,12},{16,14},{18,16},{20... | collective-permute-start | bytes 1572872 | tf_op jit(solution)/shard_map/ppermute | solution.py:525
  128.9 0.8 fusion.11
  129.8 1.9 collective-permute-start.2
  131.8 2.2 collective-permute-done.4
  134.0 3.2 %collective-permute-done.3 = bf16[2,2,64,128]{3,2,1,0:T(8,128)(2,1)S(1)} collective-permute-done((bf16[2,2,64,128]{3,2,1,0:T(8,128)(2,1)S(1)}, bf16[2,2,64,128]{3,2,1,0:T(8,128)(2,1)S(1)}, u32[]{:S(2)}, u32[]{:S(2)}) %collective-permute-start.3) | collective-permute-done | bytes 65568 | tf_op jit(solution)/shard_map/ppermute | solution.py:525
  137.2 1.6 collective-permute-done.2
  138.9 2.4 collective-permute-start.6
  141.3 0.2 copy.11
  141.5 0.7 reshape.123.pick_ref
  142.2 0.6 pad_add_fusion.where_ref
  142.9 0.8 copy-done.2
  143.7 0.8 copy-done.3
  144.5 8.9 %near.1 = (f32[16,128,128]{2,1,0:T(8,128)}, f32[16,128,256]{2,1,0:T(8,128)}, f32[16,128,128]{2,1,0:T(8,128)}, f32[16,128,256]{2,1,0:T(8,128)}, f32[16,128,128]{2,1,0:T(8,128)}, /*index=5*/f32[16,128,2]{2,1,0:T(8,128)}) custom-call(s32[96]{0:T(128)} %reshape.123.pick_ref, s32[3]{0:T(128)} %pad_add_fusion.where_ref, bf16[128,2048]{1,0:T(8,128)(2,1)} %query_ref.7, ...), custom_call_target="tpu_custom_call" | custom-call | flops 600000000 | bytes 16777216 | tf_op jit(solution)/shard_map/near/pallas_call | solution.py:244
  153.4 0.9 collective-permute-done.7.ends3_ref
  154.3 0.7 copy-done.9
  155.0 8.8 %ends.1 = (bf16[128,2048]{1,0:T(8,128)(2,1)}, f32[16,128,128]{2,1,0:T(8,128)}, f32[16,128,2]{2,1,0:T(8,128)}, bf16[4,2,2,64,128]{4,3,2,1,0:T(8,128)(2,1)}, bf16[...) custom-call(s32[3]{0:T(128)} %pad_add_fusion.where_ref, ...), custom_call_target="tpu_custom_call" | custom-call | flops 400000000 | bytes 8388608 | tf_op jit(solution)/shard_map/ends/pallas_call | solution.py:333
  163.8 0.8 collective-permute-start.10
  164.6 3.4 %collective-permute-start.9 = (bf16[4,2,2,64,128]{4,3,2,1,0:T(8,128)(2,1)}, bf16[4,2,2,64,128]{4,3,2,1,0:T(8,128)(2,1)S(1)}, u32[]{:S(2)}, u32[]{:S(2)}) collective-permute-start(bf16[4,2,2,64,128]{4,3,2,1,0:T(8,128)(2,1)} %get-tuple-element.69), channel_id=1, source_target_pairs={{0,128},{2,130},{4,132},{6,134},{8,136},{10,138},{12,140},{14,142}... | collective-permute-start | bytes 786440 | tf_op jit(solution)/shard_map/ppermute | solution.py:525
  168.0 1.7 collective-permute-start.8
  169.7 7.5 %far_terms.1 = (bf16[128,2,64,128]{3,2,1,0:T(8,128)(2,1)}, bf16[2,64,2048]{2,1,0:T(8,128)(2,1)}, bf16[2,64,2048]{2,1,0:T(8,128)(2,1)}) custom-call(s32[96]{0:T(128)} %reshape.123.pick_ref, bf16[128,2048]{1,0:T(8,128)(2,1)} %query_ref.7, bf16[128,2048]{1,0:T(8,128)(2,1)} %grad_ref.7, f32[16,128,256]{2,1,0:T(8,128)} %get-tuple-element.61.far_exp_ref.exp_ref, ...), custom_call_target="tpu_custom_call" | custom-call | flops 400000000 | bytes 14680064 | tf_op jit(solution)/shard_map/far_terms/pallas_call | solution.py:401
  177.3 2.1 collective-permute-done.10
  179.3 0.6 collective-permute-done.8
  180.0 0.2 fusion.10
  180.4 1.9 collective-permute-start.11
  182.3 2.2 collective-permute-done.13
  184.5 2.2 collective-permute-done.12
  186.8 0.6 collective-permute-done.11
  187.4 0.6 slice_dynamic-update-slice_fusion.1
  188.0 0.6 slice_dynamic-update-slice_fusion
  188.6 11.6 %all-to-all-start.1 = ((bf16[128,2,64,128]{3,2,1,0:T(8,128)(2,1)}), bf16[128,2,64,128]{3,2,1,0:T(8,128)(2,1)}, u32[]{:S(2)}, u32[]{:S(2)}) async-start(bf16[128,2,64,128]{3,2,1,0:T(8,128)(2,1)} %slice_dynamic-update-slice_fusion), calls=%async_computation.1 | async-start | bytes 8388608 | tf_op jit(solution)/shard_map/all_to_all | solution.py:596
  200.2 3.4 %collective-permute-start.14 = (bf16[2,64,2048]{2,1,0:T(8,128)(2,1)S(1)}, bf16[2,64,2048]{2,1,0:T(8,128)(2,1)S(1)}, u32[]{:S(2)}, u32[]{:S(2)}) collective-permute-start(bf16[2,64,2048]{2,1,0:T(8,128)(2,1)S(1)} %copy-done.13), channel_id=1, source_target_pairs={{0,2},{2,4},{4,6},{6,8},{8,10},{10,12},{12,14},{14,16},{16,18},{18... | collective-permute-start | bytes 1572872 | tf_op jit(solution)/shard_map/ppermute | solution.py:525
  203.6 6.7 %collective-permute-start.15 = (bf16[2,64,2048]{2,1,0:T(8,128)(2,1)S(1)}, bf16[2,64,2048]{2,1,0:T(8,128)(2,1)S(1)}, u32[]{:S(2)}, u32[]{:S(2)}) collective-permute-start(bf16[2,64,2048]{2,1,0:T(8,128)(2,1)S(1)} %copy-done.12), channel_id=1, source_target_pairs={{2,0},{4,2},{6,4},{8,6},{10,8},{12,10},{14,12},{16,14},{18,16},{20... | collective-permute-start | bytes 1572872 | tf_op jit(solution)/shard_map/ppermute | solution.py:525
  210.3 0.7 convert_reduce_fusion.1.begin_ref
  211.0 0.2 convert_reduce_fusion
  211.2 0.7 select_reduce_fusion.order_ref
  211.8 10.2 %own_terms.1 = (bf16[128,2048]{1,0:T(8,128)(2,1)}, f32[2,128,2048]{2,1,0:T(8,128)}) custom-call(s32[96]{0:T(128)} %reshape.123.pick_ref, bf16[128,2048]{1,0:T(8,128)(2,1)} %query_ref.7, bf16[128,2048]{1,0:T(8,128)(2,1)} %grad_ref.7, bf16[128,2048]{1,0:T(8,128)(2,1)} %key_ref.5, bf16[128,2,64,128]{3,2,1,0:T(8,128)(2,1)} %all-to-all-done.far_ref, ...), custom_call_target="tpu_custom_call" | custom-call | flops 500000000 | bytes 16777216 | tf_op jit(solution)/shard_map/own_terms/pallas_call | solution.py:462
  222.0 81.6 %collective-permute-done.14.low_ref = bf16[2,64,2048]{2,1,0:T(8,128)(2,1)S(1)} collective-permute-done((bf16[2,64,2048]{2,1,0:T(8,128)(2,1)S(1)}, bf16[2,64,2048]{2,1,0:T(8,128)(2,1)S(1)}, u32[]{:S(2)}, u32[]{:S(2)}) %collective-permute-start.14) | collective-permute-done | bytes 524320 | tf_op jit(solution)/shard_map/ppermute | solution.py:525
  303.6 0.8 copy-done.5
  304.4 0.2 copy-done.6
  304.6 5.6 %gather.1 = (bf16[128,2048]{1,0:T(8,128)(2,1)}, bf16[128,2048]{1,0:T(8,128)(2,1)}) custom-call(s32[128]{0:T(128)} %select_reduce_fusion.order_ref, s32[33]{0:T(128)} %convert_reduce_fusion.1.begin_ref, bf16[128,2,64,128]{3,2,1,0:T(8,128)(2,1)} %all-to-all-done.1.terms_ref, f32[2,128,2048]{2,1,0:T(8,128)} %get-tuple-element.75.own_ref, ...), custom_call_target="tpu_custom_call" | custom-call | flops 1000000 | bytes 9437184 | tf_op jit(solution)/shard_map/gather/pallas_call | solution.py:509
  (46 shorter events, 0.9 us)
Async XLA Ops:
  5.5 16.5 %copy-start.1 = (bf16[128,2048]{1,0:T(8,128)(2,1)S(1)}, bf16[128,2048]{1,0:T(8,128)(2,1)}, u32[]{:S(2)}) copy-start(bf16[128,2048]{1,0:T(8,128)(2,1)} %value_ref.3) | copy-start | bytes 1572868
  5.5 16.6 %copy-start = (bf16[128,2048]{1,0:T(8,128)(2,1)S(1)}, bf16[128,2048]{1,0:T(8,128)(2,1)}, u32[]{:S(2)}) copy-start(bf16[128,2048]{1,0:T(8,128)(2,1)} %key_ref.5) | copy-start | bytes 1572868
  5.5 113.3 %all-to-all-start = ((bf16[128,2,64,128]{3,2,1,0:T(8,128)(2,1)}), bf16[128,2,64,128]{3,2,1,0:T(8,128)(2,1)}, u32[]{:S(2)}, u32[]{:S(2)}) async-start(bf16[128,2,64,128]{3,2,1,0:T(8,128)(2,1)} %pack.1), calls=%async_computation | async-start | bytes 8388608 | tf_op jit(solution)/shard_map/all_to_all | solution.py:581
  22.1 119.2 %copy-start.11 = (s32[256,16,3]{0,1,2:T(8,128)S(1)}, s32[256,16,3]{0,1,2:T(8,128)}, u32[]{:S(2)}) copy-start(s32[256,16,3]{0,1,2:T(8,128)} %param.13) | copy-start | bytes 147460
  118.8 24.1 %collective-permute-start = (bf16[2,64,2048]{2,1,0:T(8,128)(2,1)S(1)}, bf16[2,64,2048]{2,1,0:T(8,128)(2,1)S(1)}, u32[]{:S(2)}, u32[]{:S(2)}) collective-permute-start(bf16[2,64,2048]{2,1,0:T(8,128)(2,1)S(1)} %get-tuple-element.55), channel_id=1, source_target_pairs={{0,2},{2,4},{4,6},{6,8},{8,10},{10,12},{12,14},{14,16},{16,18},{18... | collective-permute-start | bytes 1572872 | tf_op jit(solution)/shard_map/ppermute | solution.py:525
  121.3 21.6 %collective-permute-start.1 = (bf16[2,64,2048]{2,1,0:T(8,128)(2,1)S(1)}, bf16[2,64,2048]{2,1,0:T(8,128)(2,1)S(1)}, u32[]{:S(2)}, u32[]{:S(2)}) collective-permute-start(bf16[2,64,2048]{2,1,0:T(8,128)(2,1)S(1)} %get-tuple-element.56), channel_id=1, source_target_pairs={{2,0},{4,2},{6,4},{8,6},{10,8},{12,10},{14,12},{16,14},{18,16},{20... | collective-permute-start | bytes 1572872 | tf_op jit(solution)/shard_map/ppermute | solution.py:525
  129.6 4.3 %collective-permute-start.4 = (bf16[2,2,64,128]{3,2,1,0:T(8,128)(2,1)S(1)}, bf16[2,2,64,128]{3,2,1,0:T(8,128)(2,1)S(1)}, u32[]{:S(2)}, u32[]{:S(2)}) collective-permute-start(bf16[2,2,64,128]{3,2,1,0:T(8,128)(2,1)S(1)} %get-tuple-element.94), channel_id=1, source_target_pairs={{0,48},{2,50},{4,52},{6,54},{8,56},{10,58},{12,60},{14,62},{16,0},... | collective-permute-start | bytes 196616 | tf_op jit(solution)/shard_map/ppermute | solution.py:525
  129.7 7.4 %collective-permute-start.3 = (bf16[2,2,64,128]{3,2,1,0:T(8,128)(2,1)S(1)}, bf16[2,2,64,128]{3,2,1,0:T(8,128)(2,1)S(1)}, u32[]{:S(2)}, u32[]{:S(2)}) collective-permute-start(bf16[2,2,64,128]{3,2,1,0:T(8,128)(2,1)S(1)} %get-tuple-element.94), channel_id=1, source_target_pairs={{0,32},{2,34},{4,36},{6,38},{8,40},{10,42},{12,44},{14,46},{16,48}... | collective-permute-start | bytes 196616 | tf_op jit(solution)/shard_map/ppermute | solution.py:525
  129.8 8.9 %collective-permute-start.2 = (bf16[2,2,64,128]{3,2,1,0:T(8,128)(2,1)S(1)}, bf16[2,2,64,128]{3,2,1,0:T(8,128)(2,1)S(1)}, u32[]{:S(2)}, u32[]{:S(2)}) collective-permute-start(bf16[2,2,64,128]{3,2,1,0:T(8,128)(2,1)S(1)} %get-tuple-element.94), channel_id=1, source_target_pairs={{0,16},{2,18},{4,20},{6,22},{8,24},{10,26},{12,28},{14,30},{16,32}... | collective-permute-start | bytes 196616 | tf_op jit(solution)/shard_map/ppermute | solution.py:525
  138.8 15.5 %copy-start.4 = (bf16[4,2,2,64,128]{4,3,2,1,0:T(8,128)(2,1)}, bf16[4,2,2,64,128]{4,3,2,1,0:T(8,128)(2,1)S(1)}, u32[]{:S(2)}) copy-start(bf16[4,2,2,64,128]{4,3,2,1,0:T(8,128)(2,1)S(1)} %pad_maximum_fusion.2.ends0_ref) | copy-start | bytes 786436
  138.8 14.6 %collective-permute-start.5 = (bf16[4,2,2,64,128]{4,3,2,1,0:T(8,128)(2,1)S(1)}, bf16[4,2,2,64,128]{4,3,2,1,0:T(8,128)(2,1)S(1)}, u32[]{:S(2)}, u32[]{:S(2)}) collective-permute-start(bf16[4,2,2,64,128]{4,3,2,1,0:T(8,128)(2,1)S(1)} %pad_maximum_fusion.2.ends0_ref), channel_id=1, source_target_pairs={{0,64},{2,66},{4,68},{6,70},{8,72},{10,74},{12,76},{14,78},{16,80}... | collective-permute-start | bytes 786440 | tf_op jit(solution)/shard_map/ppermute | solution.py:525
  138.9 14.5 %collective-permute-start.6 = (bf16[4,2,2,64,128]{4,3,2,1,0:T(8,128)(2,1)S(1)}, bf16[4,2,2,64,128]{4,3,2,1,0:T(8,128)(2,1)S(1)}, u32[]{:S(2)}, u32[]{:S(2)}) collective-permute-start(bf16[4,2,2,64,128]{4,3,2,1,0:T(8,128)(2,1)S(1)} %pad_maximum_fusion.2.ends0_ref), channel_id=1, source_target_pairs={{0,128},{2,130},{4,132},{6,134},{8,136},{10,138},{12,140},{14,142}... | collective-permute-start | bytes 786440 | tf_op jit(solution)/shard_map/ppermute | solution.py:525
  141.3 13.0 %collective-permute-start.7 = (bf16[4,2,2,64,128]{4,3,2,1,0:T(8,128)(2,1)S(1)}, bf16[4,2,2,64,128]{4,3,2,1,0:T(8,128)(2,1)S(1)}, u32[]{:S(2)}, u32[]{:S(2)}) collective-permute-start(bf16[4,2,2,64,128]{4,3,2,1,0:T(8,128)(2,1)S(1)} %pad_maximum_fusion.2.ends0_ref), channel_id=1, source_target_pairs={{0,192},{2,194},{4,196},{6,198},{8,200},{10,202},{12,204},{14,206}... | collective-permute-start | bytes 786440 | tf_op jit(solution)/shard_map/ppermute | solution.py:525
  142.9 0.8 copy-start.2
  143.7 0.8 copy-start.3
  153.4 0.9 copy-start.7
  153.4 0.9 copy-start.8
  154.3 0.7 copy-start.9
  163.8 16.2 %copy-start.10 = (bf16[4,2,2,64,128]{4,3,2,1,0:T(8,128)(2,1)S(1)}, bf16[4,2,2,64,128]{4,3,2,1,0:T(8,128)(2,1)}, u32[]{:S(2)}) copy-start(bf16[4,2,2,64,128]{4,3,2,1,0:T(8,128)(2,1)} %get-tuple-element.67) | copy-start | bytes 786436
  163.8 15.5 %collective-permute-start.10 = (bf16[4,2,2,64,128]{4,3,2,1,0:T(8,128)(2,1)}, bf16[4,2,2,64,128]{4,3,2,1,0:T(8,128)(2,1)S(1)}, u32[]{:S(2)}, u32[]{:S(2)}) collective-permute-start(bf16[4,2,2,64,128]{4,3,2,1,0:T(8,128)(2,1)} %get-tuple-element.70), channel_id=1, source_target_pairs={{0,192},{2,194},{4,196},{6,198},{8,200},{10,202},{12,204},{14,206}... | collective-permute-start | bytes 786440 | tf_op jit(solution)/shard_map/ppermute | solution.py:525
  164.6 14.7 %collective-permute-start.9 = (bf16[4,2,2,64,128]{4,3,2,1,0:T(8,128)(2,1)}, bf16[4,2,2,64,128]{4,3,2,1,0:T(8,128)(2,1)S(1)}, u32[]{:S(2)}, u32[]{:S(2)}) collective-permute-start(bf16[4,2,2,64,128]{4,3,2,1,0:T(8,128)(2,1)} %get-tuple-element.69), channel_id=1, source_target_pairs={{0,128},{2,130},{4,132},{6,134},{8,136},{10,138},{12,140},{14,142}... | collective-permute-start | bytes 786440 | tf_op jit(solution)/shard_map/ppermute | solution.py:525
  168.0 11.9 %collective-permute-start.8 = (bf16[4,2,2,64,128]{4,3,2,1,0:T(8,128)(2,1)}, bf16[4,2,2,64,128]{4,3,2,1,0:T(8,128)(2,1)S(1)}, u32[]{:S(2)}, u32[]{:S(2)}) collective-permute-start(bf16[4,2,2,64,128]{4,3,2,1,0:T(8,128)(2,1)} %get-tuple-element.68), channel_id=1, source_target_pairs={{0,64},{2,66},{4,68},{6,70},{8,72},{10,74},{12,76},{14,78},{16,80}... | collective-permute-start | bytes 786440 | tf_op jit(solution)/shard_map/ppermute | solution.py:525
  180.2 4.3 %collective-permute-start.13 = (bf16[2,2,64,128]{3,2,1,0:T(8,128)(2,1)S(1)}, bf16[2,2,64,128]{3,2,1,0:T(8,128)(2,1)S(1)}, u32[]{:S(2)}, u32[]{:S(2)}) collective-permute-start(bf16[2,2,64,128]{3,2,1,0:T(8,128)(2,1)S(1)} %get-tuple-element.91), channel_id=1, source_target_pairs={{0,48},{2,50},{4,52},{6,54},{8,56},{10,58},{12,60},{14,62},{16,0},... | collective-permute-start | bytes 196616 | tf_op jit(solution)/shard_map/ppermute | solution.py:525
  180.3 6.5 %collective-permute-start.12 = (bf16[2,2,64,128]{3,2,1,0:T(8,128)(2,1)S(1)}, bf16[2,2,64,128]{3,2,1,0:T(8,128)(2,1)S(1)}, u32[]{:S(2)}, u32[]{:S(2)}) collective-permute-start(bf16[2,2,64,128]{3,2,1,0:T(8,128)(2,1)S(1)} %get-tuple-element.92), channel_id=1, source_target_pairs={{0,32},{2,34},{4,36},{6,38},{8,40},{10,42},{12,44},{14,46},{16,48}... | collective-permute-start | bytes 196616 | tf_op jit(solution)/shard_map/ppermute | solution.py:525
  180.4 7.0 %collective-permute-start.11 = (bf16[2,2,64,128]{3,2,1,0:T(8,128)(2,1)S(1)}, bf16[2,2,64,128]{3,2,1,0:T(8,128)(2,1)S(1)}, u32[]{:S(2)}, u32[]{:S(2)}) collective-permute-start(bf16[2,2,64,128]{3,2,1,0:T(8,128)(2,1)S(1)} %get-tuple-element.90), channel_id=1, source_target_pairs={{0,16},{2,18},{4,20},{6,22},{8,24},{10,26},{12,28},{14,30},{16,32}... | collective-permute-start | bytes 196616 | tf_op jit(solution)/shard_map/ppermute | solution.py:525
  188.6 11.6 %copy-start.13 = (bf16[2,64,2048]{2,1,0:T(8,128)(2,1)S(1)}, bf16[2,64,2048]{2,1,0:T(8,128)(2,1)}, u32[]{:S(2)}) copy-start(bf16[2,64,2048]{2,1,0:T(8,128)(2,1)} %get-tuple-element.76) | copy-start | bytes 1572868
  188.6 15.0 %copy-start.12 = (bf16[2,64,2048]{2,1,0:T(8,128)(2,1)S(1)}, bf16[2,64,2048]{2,1,0:T(8,128)(2,1)}, u32[]{:S(2)}) copy-start(bf16[2,64,2048]{2,1,0:T(8,128)(2,1)} %get-tuple-element.77) | copy-start | bytes 1572868
  188.6 115.0 %all-to-all-start.1 = ((bf16[128,2,64,128]{3,2,1,0:T(8,128)(2,1)}), bf16[128,2,64,128]{3,2,1,0:T(8,128)(2,1)}, u32[]{:S(2)}, u32[]{:S(2)}) async-start(bf16[128,2,64,128]{3,2,1,0:T(8,128)(2,1)} %slice_dynamic-update-slice_fusion), calls=%async_computation.1 | async-start | bytes 8388608 | tf_op jit(solution)/shard_map/all_to_all | solution.py:596
  200.2 103.4 %collective-permute-start.14 = (bf16[2,64,2048]{2,1,0:T(8,128)(2,1)S(1)}, bf16[2,64,2048]{2,1,0:T(8,128)(2,1)S(1)}, u32[]{:S(2)}, u32[]{:S(2)}) collective-permute-start(bf16[2,64,2048]{2,1,0:T(8,128)(2,1)S(1)} %copy-done.13), channel_id=1, source_target_pairs={{0,2},{2,4},{4,6},{6,8},{8,10},{10,12},{12,14},{14,16},{16,18},{18... | collective-permute-start | bytes 1572872 | tf_op jit(solution)/shard_map/ppermute | solution.py:525
  203.6 100.0 %collective-permute-start.15 = (bf16[2,64,2048]{2,1,0:T(8,128)(2,1)S(1)}, bf16[2,64,2048]{2,1,0:T(8,128)(2,1)S(1)}, u32[]{:S(2)}, u32[]{:S(2)}) collective-permute-start(bf16[2,64,2048]{2,1,0:T(8,128)(2,1)S(1)} %copy-done.12), channel_id=1, source_target_pairs={{2,0},{4,2},{6,4},{8,6},{10,8},{12,10},{14,12},{16,14},{18,16},{20... | collective-permute-start | bytes 1572872 | tf_op jit(solution)/shard_map/ppermute | solution.py:525
  303.6 0.8 copy-start.5
  303.6 1.0 copy-start.6

commit v5 on v4

v5 whole, which is shorter than its diff:
```python
import math

import jax
import jax.numpy as jnp
from jax import lax
from jax.experimental import pallas as pl
from jax.experimental.pallas import tpu as pltpu
from jax.sharding import PartitionSpec as P

DH = 128
BLOCK = 64
HEADS = 16
SHARDS = 128
LAST = SHARDS - 1
PICKS = 3 * HEADS
NX, NY, NZ = 4, 4, 8
VMEM_BYTES = 60 * 2**20
MASKED = -1e30
SCALE = 1.0 / math.sqrt(DH)
EXP2_SCALE = SCALE * math.log2(math.e)
BF16 = jnp.bfloat16
F32 = jnp.float32

IN_VMEM = pl.BlockSpec(memory_space=pltpu.VMEM)
IN_SMEM = pl.BlockSpec(memory_space=pltpu.SMEM)
IN_HBM = pl.BlockSpec(memory_space=pltpu.HBM)


def params():
    return pltpu.CompilerParams(vmem_limit_bytes=VMEM_BYTES)


def cost(flops, moved, exps=0):
    return pl.CostEstimate(flops=flops, bytes_accessed=moved, transcendentals=exps)


def lanes(head):
    return pl.ds(pl.multiple_of(head * DH, DH), DH)


def rows(block):
    return pl.ds(pl.multiple_of(block * BLOCK, BLOCK), BLOCK)


def nt(a, b):
    return lax.dot_general(a, b, (((1,), (1,)), ((), ())), preferred_element_type=F32)


def nn(a, b):
    return lax.dot_general(a, b, (((1,), (0,)), ((), ())), preferred_element_type=F32)


def tn(a, b):
    return lax.dot_general(a, b, (((0,), (0,)), ((), ())), preferred_element_type=F32)


def pack_kernel(item_ref, key_ref, value_ref, slots_ref, sem):
    def moves(slot):
        item = item_ref[slot]
        block, head = item >> 4, item & 15
        return [
            pltpu.make_async_copy(
                ref.at[rows(block), lanes(head)], slots_ref.at[slot, side], sem.at[side]
            )
            for side, ref in enumerate((key_ref, value_ref))
        ]

    def start(slot, carry):
        for move in moves(slot):
            move.start()
        return carry

    lax.fori_loop(0, SHARDS, start, 0, unroll=8)
    for side in range(2):
        whole = slots_ref.at[:, side]
        pltpu.make_async_copy(whole, whole, sem.at[side]).wait()


def pack(items, key_states, values):
    return pl.pallas_call(
        pack_kernel,
        in_specs=[IN_SMEM, IN_VMEM, IN_VMEM],
        out_specs=pl.BlockSpec(memory_space=pl.ANY),
        out_shape=jax.ShapeDtypeStruct((SHARDS, 2, BLOCK, DH), BF16),
        scratch_shapes=[pltpu.SemaphoreType.DMA((2,))],
        compiler_params=params(),
        cost_estimate=cost(0, 6 * 2**20),
        name="pack",
    )(items, key_states, values)


PICKED = slice(0, 3 * BLOCK)
HALVES = (slice(0, BLOCK), slice(BLOCK, 2 * BLOCK))
TOKENS_HERE = 2 * BLOCK
SOME = 4
STEPS = HEADS // SOME


def struct(shape, dtype=F32):
    return jax.ShapeDtypeStruct(shape, dtype)


def flat_spec(where_to):
    return pl.BlockSpec((TOKENS_HERE, SOME * DH), lambda *at: (0, where_to(*at)))


def edge_spec(where_to):
    return pl.BlockSpec((2, BLOCK, SOME * DH), lambda *at: (0, 0, where_to(*at)))


def head_spec(width, where_to):
    return pl.BlockSpec((SOME, TOKENS_HERE, width), lambda *at: (where_to(*at), 0, 0))


def grid_call(kernel, name, flops, moved, prefetch, in_specs, out_specs, out_shape, scratch=()):
    return pl.pallas_call(
        kernel,
        grid_spec=pltpu.PrefetchScalarGridSpec(
            num_scalar_prefetch=prefetch,
            grid=(STEPS,),
            in_specs=in_specs,
            out_specs=out_specs,
            scratch_shapes=scratch,
        ),
        out_shape=out_shape,
        compiler_params=params(),
        cost_estimate=cost(flops, moved, 10**6),
        name=name,
    )


def step_of(i, *scalars):
    return i


def columns_of(i):
    return slice(i * DH, (i + 1) * DH)


def both(of):
    return jnp.concatenate([of(0), of(1)])


def stacked(of):
    return jnp.concatenate([of(i) for i in range(SOME)])


def rows_of(i):
    return slice(i * TOKENS_HERE, (i + 1) * TOKENS_HERE)


def half_rows(i, b):
    return slice((2 * i + b) * BLOCK, (2 * i + b + 1) * BLOCK)


def no_block():
    return jnp.zeros((BLOCK, DH), BF16)


def split(block_rows):
    return jnp.concatenate(
        [
            jnp.concatenate([block_rows[HALVES[0]], no_block()], axis=1),
            jnp.concatenate([no_block(), block_rows[HALVES[1]]], axis=1),
        ]
    )


def owner_of(pick_ref, head, b, r):
    return pick_ref[b * PICKS + head * 3 + r] >> 1


def fetch(pick_ref, far_ref, held_ref, sem):
    def one(head, carry):
        for b in range(2):
            for r in range(3):
                source = far_ref.at[owner_of(pick_ref, head, b, r)]
                if len(held_ref.shape) == 4:
                    source = source.at[0]
                target = held_ref.at[head, b * 3 + r]
                pltpu.make_async_copy(source, target, sem.at[head]).start()
        return carry

    lax.fori_loop(0, HEADS, one, 0, unroll=4)


def fetched(held_ref, sem, head):
    pltpu.make_async_copy(held_ref.at[head], held_ref.at[head], sem.at[head]).wait()


def near_kernel(
    pick_ref,
    query_ref,
    grad_ref,
    key_ref,
    value_ref,
    far_ref,
    own_exp_ref,
    far_exp_ref,
    own_wgrad_ref,
    far_wgrad_ref,
    part_ref,
    stat_ref,
    held_ref,
    sem,
):
    step = pl.program_id(0)

    @pl.when(step == 0)
    def _():
        fetch(pick_ref, far_ref, held_ref, sem)

    column = lax.broadcasted_iota(jnp.int32, (1, 4 * BLOCK), 1)
    bias = jnp.where(column >= 3 * BLOCK, MASKED, 0.0)
    heads = [step * SOME + i for i in range(SOME)]
    queries = [query_ref[:, columns_of(i)] for i in range(SOME)]
    grads = [grad_ref[:, columns_of(i)] for i in range(SOME)]
    for head in heads:
        fetched(held_ref, sem, head)

    def picked(i, b, side):
        blocks = [held_ref[heads[i], b * 3 + r, side] for r in range(3)]
        return jnp.concatenate(blocks + [no_block()])

    keys, values = (
        [[picked(i, b, side) for b in range(2)] for i in range(SOME)] for side in range(2)
    )
    own_score = stacked(lambda i: nt(queries[i], key_ref[:, columns_of(i)]))
    far_score = stacked(lambda i: both(lambda b: nt(queries[i][HALVES[b]], keys[i][b]) + bias))
    top = jnp.maximum(
        jnp.maximum(own_score, far_score[:, :TOKENS_HERE]), far_score[:, TOKENS_HERE:]
    )
    top = jnp.max(top, axis=1, keepdims=True)
    own_exp = jnp.exp2((own_score - top) * EXP2_SCALE)
    far_exp = jnp.exp2((far_score - top) * EXP2_SCALE)
    total = own_exp + far_exp[:, :TOKENS_HERE] + far_exp[:, TOKENS_HERE:]
    stat = jnp.concatenate([top, jnp.sum(total, axis=1, keepdims=True)], axis=1)
    own_low, far_low = own_exp.astype(BF16), far_exp.astype(BF16)
    for i in range(SOME):
        at = rows_of(i)
        own_exp_ref[i], far_exp_ref[i], stat_ref[i] = own_exp[at], far_exp[at], stat[at]
        own_wgrad_ref[i] = nt(grads[i], value_ref[:, columns_of(i)])
        far_part = both(lambda b: nn(far_low[half_rows(i, b)], values[i][b]))
        part_ref[i] = nn(own_low[at], value_ref[:, columns_of(i)]) + far_part
        for b in range(2):
            far_wgrad_ref[i, HALVES[b]] = nt(grads[i][HALVES[b]], values[i][b])


def near(picks, query, grad, key, value, far):
    own, wide = (HEADS, TOKENS_HERE, TOKENS_HERE), (HEADS, TOKENS_HERE, 4 * BLOCK)
    return grid_call(
        near_kernel,
        "near",
        6 * 10**8,
        16 * 2**20,
        1,
        [flat_spec(step_of)] * 4 + [IN_HBM],
        [head_spec(w, step_of) for w in (DH, 2 * DH, DH, 2 * DH, DH, 2)],
        [struct(own), struct(wide), struct(own), struct(wide), struct(own), struct(own[:2] + (2,))],
        [pltpu.VMEM((HEADS, 6, 2, BLOCK, DH), BF16), pltpu.SemaphoreType.DMA((HEADS,))],
    )(picks, query, grad, key, value, far)


def ends_kernel(
    where_ref,
    query_ref,
    grad_ref,
    part_ref,
    stat_ref,
    ends_ref,
    prev_ref,
    next_ref,
    attended_ref,
    query_part_ref,
    factor_ref,
    terms_ref,
    prev_terms_ref,
    next_terms_ref,
):
    shard = where_ref[0]
    column = lax.broadcasted_iota(jnp.int32, (1, TOKENS_HERE), 1)
    no_end = ((shard == 0) & (column < BLOCK)) | ((shard == LAST) & (column >= BLOCK))
    bias = jnp.where(no_end, MASKED, 0.0)
    edge_bias = [
        jnp.where((shard == end) | (column >= BLOCK), MASKED, 0.0) for end in (0, LAST)
    ]
    edges = (prev_ref, next_ref)
    queries = [query_ref[:, columns_of(i)] for i in range(SOME)]
    grads = [grad_ref[:, columns_of(i)] for i in range(SOME)]
    keys, values = (
        [jnp.concatenate([ends_ref[i, 0, side], ends_ref[i, 1, side]]) for i in range(SOME)]
        for side in range(2)
    )
    edge_keys, edge_values = (
        [
            [jnp.concatenate([edge[side, :, columns_of(i)], no_block()]) for edge in edges]
            for i in range(SOME)
        ]
        for side in range(2)
    )

    def by_edge(of):
        return stacked(lambda i: both(lambda b: of(i, b)))

    score = stacked(lambda i: nt(queries[i], keys[i])) + bias
    edge_score = by_edge(lambda i, b: nt(queries[i][HALVES[b]], edge_keys[i][b]) + edge_bias[b])
    stat = stacked(lambda i: stat_ref[i])
    old_top = stat[:, 0:1]
    top = jnp.max(jnp.maximum(score, edge_score), axis=1, keepdims=True)
    top = jnp.maximum(old_top, top)
    exps = jnp.exp2((score - top) * EXP2_SCALE)
    edge_exps = jnp.exp2((edge_score - top) * EXP2_SCALE)
    shrink = jnp.exp2((old_top - top) * EXP2_SCALE)
    total = stat[:, 1:2] * shrink
    inverse = 1.0 / (total + jnp.sum(exps + edge_exps, axis=1, keepdims=True))
    factor = shrink * inverse
    weight, edge_weight = exps * inverse, edge_exps * inverse
    low, edge_low = weight.astype(BF16), edge_weight.astype(BF16)
    wgrad = stacked(lambda i: nt(grads[i], values[i]))
    edge_wgrad = by_edge(lambda i, b: nt(grads[i][HALVES[b]], edge_values[i][b]))
    attended = stacked(lambda i: part_ref[i]) * factor
    attended = attended + stacked(lambda i: nn(low[rows_of(i)], values[i]))
    attended = attended + by_edge(lambda i, b: nn(edge_low[half_rows(i, b)], edge_values[i][b]))
    attended = attended.astype(BF16)
    grad = stacked(lambda i: grads[i].astype(F32))
    row_dot = jnp.sum(grad * attended.astype(F32), axis=1, keepdims=True)
    sgrad = (weight * (wgrad - row_dot) * SCALE).astype(BF16)
    edge_sgrad = (edge_weight * (edge_wgrad - row_dot) * SCALE).astype(BF16)
    stat = jnp.concatenate([factor, row_dot], axis=1)
    for i in range(SOME):
        at, here = rows_of(i), columns_of(i)
        attended_ref[:, here] = attended[at]
        factor_ref[i] = stat[at]
        edge_part = both(lambda b: nn(edge_sgrad[half_rows(i, b)], edge_keys[i][b]))
        query_part_ref[i] = nn(sgrad[at], keys[i]) + edge_part
        for side, left, edge_left, right in (
            (0, sgrad, edge_sgrad, queries[i]),
            (1, low, edge_low, grads[i]),
        ):
            terms = tn(left[at], right).astype(BF16)
            terms_ref[i, 0, side] = terms[:BLOCK]
            terms_ref[i, 1, side] = terms[BLOCK:]
            edge_terms = tn(edge_left[at], split(right))[:BLOCK].astype(BF16)
            prev_terms_ref[side, :, here] = edge_terms[:, :DH]
            next_terms_ref[side, :, here] = edge_terms[:, DH:]


def ends(where, query, grad, part, stat, blocks, prev, following):
    own = (HEADS, TOKENS_HERE, DH)
    edge = struct((2, BLOCK, HEADS * DH), BF16)
    pair_spec = pl.BlockSpec((SOME, 2, 2, BLOCK, DH), lambda i, where: (i, 0, 0, 0, 0))
    heads_specs = [head_spec(DH, step_of), head_spec(2, step_of)]
    return grid_call(
        ends_kernel,
        "ends",
        6 * 10**8,
        10 * 2**20,
        1,
        [flat_spec(step_of)] * 2 + heads_specs + [pair_spec] + [edge_spec(step_of)] * 2,
        [flat_spec(step_of)] + heads_specs + [pair_spec] + [edge_spec(step_of)] * 2,
        [
            struct((TOKENS_HERE, HEADS * DH), BF16),
            struct(own),
            struct(own[:2] + (2,)),
            struct((HEADS, 2, 2, BLOCK, DH), BF16),
            edge,
            edge,
        ],
    )(where, query, grad, part, stat, blocks, prev, following)


def far_terms_kernel(
    pick_ref,
    query_ref,
    grad_ref,
    exp_ref,
    wgrad_ref,
    factor_ref,
    terms_ref,
    made_ref,
    sem,
):
    step = pl.program_id(0)
    for i in range(SOME):
        head = step * SOME + i
        at = columns_of(i)
        weight = exp_ref[i] * factor_ref[i, :, 0:1]
        low = weight.astype(BF16)
        sgrad = (weight * (wgrad_ref[i] - factor_ref[i, :, 1:2]) * SCALE).astype(BF16)
        for side, left, right in ((0, sgrad, query_ref[:, at]), (1, low, grad_ref[:, at])):
            parts = tn(left[:, PICKED], split(right)).astype(BF16)
            for b in range(2):
                for r in range(3):
                    span = slice(r * BLOCK, (r + 1) * BLOCK)
                    made_ref[head, b * 3 + r, side] = parts[span, columns_of(b)]
        for b in range(2):
            for r in range(3):
                pltpu.make_async_copy(
                    made_ref.at[head, b * 3 + r],
                    terms_ref.at[owner_of(pick_ref, head, b, r)],
                    sem.at[0],
                ).start()

    @pl.when(step == STEPS - 1)
    def _():
        pltpu.make_async_copy(made_ref, made_ref, sem.at[0]).wait()


def far_terms(picks, query, grad, exps, wgrads, factor):
    return grid_call(
        far_terms_kernel,
        "far_terms",
        4 * 10**8,
        14 * 2**20,
        1,
        [flat_spec(step_of)] * 2 + [head_spec(w, step_of) for w in (2 * DH, 2 * DH, 2)],
        IN_HBM,
        struct((SHARDS, 2, BLOCK, DH), BF16),
        [pltpu.VMEM((HEADS, 6, 2, BLOCK, DH), BF16), pltpu.SemaphoreType.DMA((1,))],
    )(picks, query, grad, exps, wgrads, factor)


def own_terms_kernel(
    pick_ref,
    query_ref,
    grad_ref,
    key_ref,
    far_ref,
    own_exp_ref,
    far_exp_ref,
    own_wgrad_ref,
    far_wgrad_ref,
    query_part_ref,
    factor_ref,
    query_grad_ref,
    own_ref,
    held_ref,
    sem,
):
    step = pl.program_id(0)

    @pl.when(step == 0)
    def _():
        fetch(pick_ref, far_ref, held_ref, sem)

    for i in range(SOME):
        head = step * SOME + i
        at = columns_of(i)
        fetched(held_ref, sem, head)
        factor, row_dot = factor_ref[i, :, 0:1], factor_ref[i, :, 1:2]
        weight = own_exp_ref[i] * factor
        sgrad = (weight * (own_wgrad_ref[i] - row_dot) * SCALE).astype(BF16)
        far_sgrad = far_exp_ref[i] * factor * (far_wgrad_ref[i] - row_dot) * SCALE
        far_sgrad = far_sgrad.astype(BF16)

        def far_key(b):
            return jnp.concatenate([held_ref[head, b * 3 + r] for r in range(3)])

        query_grad = query_part_ref[i] + nn(sgrad, key_ref[:, at])
        query_grad = query_grad + both(lambda b: nn(far_sgrad[HALVES[b], PICKED], far_key(b)))
        query_grad_ref[:, at] = query_grad.astype(BF16)
        own_ref[0, :, at] = tn(sgrad, query_ref[:, at])
        own_ref[1, :, at] = tn(weight.astype(BF16), grad_ref[:, at])


def own_terms(picks, query, grad, key, far, exps, wgrads, query_part, factor):
    return grid_call(
        own_terms_kernel,
        "own_terms",
        5 * 10**8,
        16 * 2**20,
        1,
        [flat_spec(step_of)] * 3
        + [IN_HBM]
        + [head_spec(w, step_of) for w in (DH, 2 * DH, DH, 2 * DH, DH, 2)],
        [
            flat_spec(step_of),
            pl.BlockSpec((2, TOKENS_HERE, SOME * DH), lambda i, picks: (0, 0, i)),
        ],
        [
            struct((TOKENS_HERE, HEADS * DH), BF16),
            struct((2, TOKENS_HERE, HEADS * DH)),
        ],
        [pltpu.VMEM((HEADS, 6, BLOCK, DH), BF16), pltpu.SemaphoreType.DMA((HEADS,))],
    )(picks, query, grad, key, far, *exps, *wgrads, query_part, factor)


def gather_kernel(
    order_ref, begin_ref, terms_ref, own_ref, low_ref, high_ref, key_ref, value_ref
):
    edges = (low_ref, high_ref)

    def one_side(out_ref):
        for block in range(2):
            for head in range(HEADS):
                item = block * HEADS + head
                at = columns_of(head)

                def add(place, total):
                    return total + terms_ref[order_ref[place], 0].astype(F32)

                total = own_ref[0, HALVES[block], at] + edges[block][0, :, at].astype(F32)
                total = lax.fori_loop(begin_ref[item], begin_ref[item + 1], add, total)
                out_ref[HALVES[block], at] = total.astype(BF16)

    for side, out_ref in enumerate((key_ref, value_ref)):
        pl.when(pl.program_id(0) == side)(lambda out_ref=out_ref: one_side(out_ref))


def gather(order, begins, terms, own, low, high):
    flat = struct((TOKENS_HERE, HEADS * DH), BF16)
    flat_whole = pl.BlockSpec(flat.shape, lambda side, *scalars: (0, 0))

    def side_spec(rows_there):
        return pl.BlockSpec(
            (1, rows_there, HEADS * DH), lambda side, *scalars: (side, 0, 0)
        )

    return pl.pallas_call(
        gather_kernel,
        grid_spec=pltpu.PrefetchScalarGridSpec(
            num_scalar_prefetch=2,
            grid=(2,),
            in_specs=[
                pl.BlockSpec((SHARDS, 1, BLOCK, DH), lambda side, *scalars: (0, side, 0, 0)),
                side_spec(TOKENS_HERE),
                side_spec(BLOCK),
                side_spec(BLOCK),
            ],
            out_specs=[flat_whole, flat_whole],
        ),
        out_shape=[flat, flat],
        compiler_params=params(),
        cost_estimate=cost(10**6, 9 * 2**20),
        name="gather",
    )(order, begins, terms, own, low, high)


def send(value, route):
    return lax.ppermute(value, "seq", route)


def repeat_kernel(far_ref, out_ref, sem):
    for cell in range(HEADS):
        for end, source in enumerate((0, LAST)):
            pltpu.make_async_copy(far_ref.at[source], out_ref.at[cell, end], sem.at[0]).start()
    pltpu.make_async_copy(out_ref, out_ref, sem.at[0]).wait()


def repeat_ends(far):
    return pl.pallas_call(
        repeat_kernel,
        in_specs=[IN_HBM],
        out_specs=IN_HBM,
        out_shape=struct((HEADS, 2, 2, BLOCK, DH), BF16),
        scratch_shapes=[pltpu.SemaphoreType.DMA((1,))],
        compiler_params=params(),
        cost_estimate=cost(0, 2 * 2**20),
        name="repeat_ends",
    )(far)


def swap_in_plane(pieces):
    planes = [[cell * NZ + z for cell in range(NX * NY)] for z in range(NZ)]
    return lax.all_to_all(
        pieces, "seq", split_axis=0, concat_axis=0, tiled=True, axis_index_groups=planes
    )


def on_device(queries, key_states, values, out_grad, rand_blocks):
    shard = lax.axis_index("seq")
    where = shard.astype(jnp.int32).reshape(1)
    wanted = rand_blocks // 2 == shard
    item = rand_blocks % 2 * HEADS + lax.broadcasted_iota(jnp.int32, rand_blocks.shape, 1)
    items = jnp.max(jnp.where(wanted, item, -1), axis=(1, 2))
    items = jnp.max(items.reshape(SHARDS, 2), axis=1)
    cell = jnp.arange(SHARDS, dtype=jnp.int32) // NZ
    items = jnp.where(shard == 0, cell, jnp.where(shard == LAST, HEADS + cell, items))
    picks = lax.dynamic_slice_in_dim(rand_blocks, 2 * shard, 2, 0).reshape(2 * PICKS)

    named = jnp.where(items < 0, 2 * HEADS, items)
    place = jnp.arange(SHARDS, dtype=jnp.int32)
    before = (named[None, :] < named[:, None]) | (
        (named[None, :] == named[:, None]) & (place[None, :] < place[:, None])
    )
    rank = jnp.sum(before.astype(jnp.int32), axis=1)
    order = jnp.sum(jnp.where(rank[None, :] == place[:, None], place[None, :], 0), axis=1)
    kinds = jnp.arange(2 * HEADS + 1, dtype=jnp.int32)
    begins = jnp.sum((named[None, :] < kinds[:, None]).astype(jnp.int32), axis=1)

    low = jnp.stack([key_states[:BLOCK], values[:BLOCK]])
    high = jnp.stack([key_states[BLOCK:], values[BLOCK:]])
    up, down = [(i, i + 1) for i in range(LAST)], [(i + 1, i) for i in range(LAST)]
    slots = pack(jnp.maximum(items, 0), key_states, values)
    far = lax.all_to_all(slots, "seq", split_axis=0, concat_axis=0, tiled=True)
    far, low, high, picks, where = lax.optimization_barrier((far, low, high, picks, where))
    blocks = swap_in_plane(repeat_ends(far))
    prev, following = send(high, up), send(low, down)
    own_exps, far_exps, own_wgrads, far_wgrads, part, stat = near(
        picks, queries, out_grad, key_states, values, far
    )
    attended, query_part, factor, end_terms, prev_terms, next_terms = ends(
        where, queries, out_grad, part, stat, blocks, prev, following
    )
    end_terms = swap_in_plane(end_terms)
    from_next, from_prev = send(prev_terms, down), send(next_terms, up)
    terms = far_terms(picks, queries, out_grad, far_exps, far_wgrads, factor)
    terms, from_next, from_prev = lax.optimization_barrier((terms, from_next, from_prev))
    end_pair = jnp.sum(end_terms.astype(F32), axis=0).astype(BF16)
    terms = terms.at[0].set(end_pair[0]).at[LAST].set(end_pair[1])
    back = lax.all_to_all(terms, "seq", split_axis=0, concat_axis=0, tiled=True)
    query_grad, own = own_terms(
        picks, queries, out_grad, key_states, far,
        (own_exps, far_exps), (own_wgrads, far_wgrads), query_part, factor,
    )
    key_grad, value_grad = gather(order, begins, back, own, from_prev, from_next)
    return (attended, query_grad, key_grad, value_grad)


def solution(mesh):
    placed = P("seq", "head")
    return jax.shard_map(
        on_device,
        mesh=mesh,
        in_specs=(placed, placed, placed, placed, P(None, "head", None)),
        out_specs=(placed, placed, placed, placed),
        check_vma=False,
    )
```

time: 311 us -> 335 us (1.077)
  Pallas kernels: 44.1 us -> 77.2 us
  starting transfers between devices: 60.7 us -> 56.4 us
    ppermute x16 -> x4, waiting for transfers between devices: 97.2 us -> 11.7 us  [send(): return lax.ppermute(value, 'seq', route)]
    all_to_all x1, waiting for transfers between devices: 0.01 us -> 81.4 us  [on_device(): back = lax.all_to_all(terms, 'seq', split_axis=0, concat_axis=0, tiled=True)]
    pallas_call x3 -> x4, Pallas kernels: 23.2 us -> 57.4 us  [the longest x1 32.9 us: repeat_ends(): pl.pallas_call(repeat_kernel, in_specs=[IN_HBM], out_specs=IN_HBM, out_sh...]
    ppermute x16 -> x4, starting transfers between devices: 32.7 us -> 15.9 us  [send(): return lax.ppermute(value, 'seq', route)]
    all_to_all x0 -> x2, starting transfers between devices: none -> 13.4 us  [swap_in_plane(): lax.all_to_all(pieces, 'seq', split_axis=0, concat_axis=0, tiled=True, ax...]
  transfers between devices with their start and end apart: 18 -> 8, of which waited for: 11 -> 7; matrix products, arithmetic and copies ran while one was open for 1% -> 1% of each run, Pallas kernels for 9% -> 8%
where the time goes in v5:
time: 335 us; the launch traced here: 333 us
  waiting for transfers between devices  192 us (57%)
  Pallas kernels  77.2 us (23%)
  starting transfers between devices  56.4 us (17%)
  local copies, waits for them, and re-layouts  3.47 us (1%)
    all_to_all x1, waiting for transfers between devices, on_device(): far = lax.all_to_all(slots, 'seq', split_axis=0, concat_axis=0, tiled=True)  95.5 us
    all_to_all x1, waiting for transfers between devices, on_device(): back = lax.all_to_all(terms, 'seq', split_axis=0, concat_axis=0, tiled=True)  81.4 us
    pallas_call x1, Pallas kernels, repeat_ends(): pl.pallas_call(repeat_kernel, in_specs=[IN_HBM], out_specs=IN_HBM, out_sh...  32.9 us
    all_to_all x1, starting transfers between devices, on_device(): far = lax.all_to_all(slots, 'seq', split_axis=0, concat_axis=0, tiled=True)  16.5 us
    ppermute x4, starting transfers between devices, send(): return lax.ppermute(value, 'seq', route)  15.9 us
    all_to_all x2, starting transfers between devices, swap_in_plane(): lax.all_to_all(pieces, 'seq', split_axis=0, concat_axis=0, tiled=True, ax...  13.4 us
    ppermute x4, waiting for transfers between devices, send(): return lax.ppermute(value, 'seq', route)  11.7 us
    all_to_all x1, starting transfers between devices, on_device(): back = lax.all_to_all(terms, 'seq', split_axis=0, concat_axis=0, tiled=True)  10.6 us
  transfers between devices with their start and end apart: 8, of which 7 were waited for; matrix products, arithmetic and copies ran while one was open for 1% of the time, Pallas kernels for 8%

profile of v5, /device:TPU:6, one launch (start us, length us, event | category | flops | bytes accessed | tf_op | source)
XLA Modules:
  0.0 332.9 jit_solution(10966232748208032272)
XLA Ops:
  0.6 0.9 fusion.6
  1.5 0.1 reshape.126
  1.7 0.1 reduce_max.19
  1.8 0.5 broadcast_maximum_fusion.item_ref
  2.3 3.2 pack.1
  5.5 0.0 copy-start.7
  5.5 0.0 copy-start.1
  5.5 0.0 copy-start
  5.5 16.5 %all-to-all-start = ((bf16[128,2,64,128]{3,2,1,0:T(8,128)(2,1)}), bf16[128,2,64,128]{3,2,1,0:T(8,128)(2,1)}, u32[]{:S(2)}, u32[]{:S(2)}) async-start(bf16[128,2,64,128]{3,2,1,0:T(8,128)(2,1)} %pack.1), calls=%async_computation | async-start | bytes 8388608 | tf_op jit(solution)/shard_map/all_to_all | solution.py:595
  22.1 0.0 copy-done.7
  22.1 0.1 constant_dynamic-slice_fusion
  22.2 0.2 copy.11
  22.4 0.7 reshape.127.pick_ref
  23.1 0.0 copy-done.1
  23.1 0.0 copy-done
  23.2 0.1 pad_maximum_fusion
  23.3 95.5 %all-to-all-done.far_ref = bf16[128,2,64,128]{3,2,1,0:T(8,128)(2,1)} async-done(((bf16[128,2,64,128]{3,2,1,0:T(8,128)(2,1)}), bf16[128,2,64,128]{3,2,1,0:T(8,128)(2,1)}, u32[]{:S(2)}, u32[]{:S(2)}) %all-to-all-start) | async-done | bytes 4194336 | tf_op jit(solution)/shard_map/all_to_all | solution.py:595
  118.8 32.9 %repeat_ends.1 = bf16[16,2,2,64,128]{4,3,2,1,0:T(8,128)(2,1)} custom-call(bf16[128,2,64,128]{3,2,1,0:T(8,128)(2,1)} %all-to-all-done.far_ref), custom_call_target="tpu_custom_call" | custom-call | bytes 2097152 | tf_op jit(solution)/shard_map/repeat_ends/pallas_call | solution.py:551
  151.7 6.1 %all-to-all-start.1 = ((bf16[16,2,2,64,128]{4,3,2,1,0:T(8,128)(2,1)}), bf16[16,2,2,64,128]{4,3,2,1,0:T(8,128)(2,1)S(1)}, u32[]{:S(2)}, u32[]{:S(2)}) async-start(bf16[16,2,2,64,128]{4,3,2,1,0:T(8,128)(2,1)} %repeat_ends.1), calls=%async_computation.1 | async-start | bytes 2097152 | tf_op jit(solution)/shard_map/all_to_all | solution.py:565
  157.8 2.5 collective-permute-start
  160.3 7.6 %collective-permute-start.1 = (bf16[2,64,2048]{2,1,0:T(8,128)(2,1)S(1)}, bf16[2,64,2048]{2,1,0:T(8,128)(2,1)S(1)}, u32[]{:S(2)}, u32[]{:S(2)}) collective-permute-start(bf16[2,64,2048]{2,1,0:T(8,128)(2,1)S(1)} %get-tuple-element.58), channel_id=1, source_target_pairs={{2,0},{4,2},{6,4},{8,6},{10,8},{12,10},{14,12},{16,14},{18,16},{20... | collective-permute-start | bytes 1572872 | tf_op jit(solution)/shard_map/ppermute | solution.py:540
  167.9 8.5 %near.1 = (f32[16,128,128]{2,1,0:T(8,128)}, f32[16,128,256]{2,1,0:T(8,128)}, f32[16,128,128]{2,1,0:T(8,128)}, f32[16,128,256]{2,1,0:T(8,128)}, f32[16,128,128]{2,1,0:T(8,128)}, /*index=5*/f32[16,128,2]{2,1,0:T(8,128)}) custom-call(s32[96]{0:T(128)} %reshape.127.pick_ref, bf16[128,2048]{1,0:T(8,128)(2,1)} %query_ref.7, bf16[128,2048]{1,0:T(8,128)(2,1)} %grad_ref.7, ...), custom_call_target="tpu_custom_call" | custom-call | flops 600000000 | bytes 16777216 | tf_op jit(solution)/shard_map/near/pallas_call | solution.py:251
  176.3 2.6 collective-permute-done.prev_ref
  179.0 0.0 collective-permute-done.1.next_ref
  179.0 2.0 all-to-all-done.1.ends_ref
  180.9 0.0 copy-done.5
  180.9 0.0 copy-done.6
  180.9 1.0 copy-done.2
  181.9 10.2 %ends.1 = (bf16[128,2048]{1,0:T(8,128)(2,1)}, f32[16,128,128]{2,1,0:T(8,128)}, f32[16,128,2]{2,1,0:T(8,128)}, bf16[16,2,2,64,128]{4,3,2,1,0:T(8,128)(2,1)}, bf16...) custom-call(s32[1]{0:T(128)} %bitcast.4.where_ref, bf16[128,2048]{1,0:T(8,128)(2,1)} %query_ref.7, ...), custom_call_target="tpu_custom_call" | custom-call | flops 600000000 | bytes 10485760 | tf_op jit(solution)/shard_map/ends/pallas_call | solution.py:353
  192.2 7.3 %all-to-all-start.2 = ((bf16[16,2,2,64,128]{4,3,2,1,0:T(8,128)(2,1)}), bf16[16,2,2,64,128]{4,3,2,1,0:T(8,128)(2,1)S(1)}, u32[]{:S(2)}, u32[]{:S(2)}) async-start(bf16[16,2,2,64,128]{4,3,2,1,0:T(8,128)(2,1)} %get-tuple-element.70), calls=%async_computation.2 | async-start | bytes 2097152 | tf_op jit(solution)/shard_map/all_to_all | solution.py:565
  199.4 3.4 %collective-permute-start.2 = (bf16[2,64,2048]{2,1,0:T(8,128)(2,1)}, bf16[2,64,2048]{2,1,0:T(8,128)(2,1)S(1)}, u32[]{:S(2)}, u32[]{:S(2)}) collective-permute-start(bf16[2,64,2048]{2,1,0:T(8,128)(2,1)} %get-tuple-element.67), channel_id=1, source_target_pairs={{2,0},{4,2},{6,4},{8,6},{10,8},{12,10},{14,12},{16,14},{18,16},{20... | collective-permute-start | bytes 1572872 | tf_op jit(solution)/shard_map/ppermute | solution.py:540
  202.8 2.5 collective-permute-start.3
  205.3 6.6 %far_terms.1 = bf16[128,2,64,128]{3,2,1,0:T(8,128)(2,1)} custom-call(s32[96]{0:T(128)} %reshape.127.pick_ref, bf16[128,2048]{1,0:T(8,128)(2,1)} %query_ref.7, bf16[128,2048]{1,0:T(8,128)(2,1)} %grad_ref.7, f32[16,128,256]{2,1,0:T(8,128)} %get-tuple-element.61.far_exp_ref.exp_ref, f32[16,128,256]{2,1,0:T(8,128)} %get-tuple-element.63.far_wgrad_ref.wgrad_ref, ...), custom_call_target="tpu_custom_call" | custom-call | flops 400000000 | bytes 14680064 | tf_op jit(solution)/shard_map/far_terms/pallas_call | solution.py:410
  211.9 1.2 collective-permute-done.2.high_ref
  213.1 7.9 %collective-permute-done.3.low_ref = bf16[2,64,2048]{2,1,0:T(8,128)(2,1)S(1)} collective-permute-done((bf16[2,64,2048]{2,1,0:T(8,128)(2,1)}, bf16[2,64,2048]{2,1,0:T(8,128)(2,1)S(1)}, u32[]{:S(2)}, u32[]{:S(2)}) %collective-permute-start.3) | collective-permute-done | bytes 524320 | tf_op jit(solution)/shard_map/ppermute | solution.py:540
  221.0 1.0 all-to-all-done.2
  222.1 0.2 reduce_sum.42
  222.3 0.6 slice_dynamic-update-slice_fusion.1
  222.9 0.6 slice_dynamic-update-slice_fusion
  223.5 0.0 copy-done.3
  223.5 0.0 copy-done.4
  223.5 10.6 %all-to-all-start.3 = ((bf16[128,2,64,128]{3,2,1,0:T(8,128)(2,1)}), bf16[128,2,64,128]{3,2,1,0:T(8,128)(2,1)}, u32[]{:S(2)}, u32[]{:S(2)}) async-start(bf16[128,2,64,128]{3,2,1,0:T(8,128)(2,1)} %slice_dynamic-update-slice_fusion), calls=%async_computation.3 | async-start | bytes 8388608 | tf_op jit(solution)/shard_map/all_to_all | solution.py:611
  234.2 0.6 convert_reduce_fusion.1.begin_ref
  234.8 0.2 convert_reduce_fusion
  234.9 0.7 select_reduce_fusion.order_ref
  235.6 10.0 %own_terms.1 = (bf16[128,2048]{1,0:T(8,128)(2,1)}, f32[2,128,2048]{2,1,0:T(8,128)}) custom-call(s32[96]{0:T(128)} %reshape.127.pick_ref, bf16[128,2048]{1,0:T(8,128)(2,1)} %query_ref.7, bf16[128,2048]{1,0:T(8,128)(2,1)} %grad_ref.7, bf16[128,2048]{1,0:T(8,128)(2,1)} %key_ref.5, bf16[128,2,64,128]{3,2,1,0:T(8,128)(2,1)} %all-to-all-done.far_ref, ...), custom_call_target="tpu_custom_call" | custom-call | flops 500000000 | bytes 16777216 | tf_op jit(solution)/shard_map/own_terms/pallas_call | solution.py:467
  245.6 81.4 %all-to-all-done.3.terms_ref = bf16[128,2,64,128]{3,2,1,0:T(8,128)(2,1)} async-done(((bf16[128,2,64,128]{3,2,1,0:T(8,128)(2,1)}), bf16[128,2,64,128]{3,2,1,0:T(8,128)(2,1)}, u32[]{:S(2)}, u32[]{:S(2)}) %all-to-all-start.3) | async-done | bytes 4194336 | tf_op jit(solution)/shard_map/all_to_all | solution.py:611
  327.1 5.8 %gather.1 = (bf16[128,2048]{1,0:T(8,128)(2,1)}, bf16[128,2048]{1,0:T(8,128)(2,1)}) custom-call(s32[128]{0:T(128)} %select_reduce_fusion.order_ref, s32[33]{0:T(128)} %convert_reduce_fusion.1.begin_ref, bf16[128,2,64,128]{3,2,1,0:T(8,128)(2,1)} %all-to-all-done.3.terms_ref, f32[2,128,2048]{2,1,0:T(8,128)} %get-tuple-element.71.own_ref, ...), custom_call_target="tpu_custom_call" | custom-call | flops 1000000 | bytes 9437184 | tf_op jit(solution)/shard_map/gather/pallas_call | solution.py:519
  (8 shorter events, 0.1 us)
Async XLA Ops:
  5.5 16.6 %copy-start.7 = (s32[256,16,3]{0,1,2:T(8,128)S(1)}, s32[256,16,3]{0,1,2:T(8,128)}, u32[]{:S(2)}) copy-start(s32[256,16,3]{0,1,2:T(8,128)} %param.13) | copy-start | bytes 147460
  5.5 17.5 %copy-start.1 = (bf16[128,2048]{1,0:T(8,128)(2,1)S(1)}, bf16[128,2048]{1,0:T(8,128)(2,1)}, u32[]{:S(2)}) copy-start(bf16[128,2048]{1,0:T(8,128)(2,1)} %value_ref.3) | copy-start | bytes 1572868
  5.5 17.6 %copy-start = (bf16[128,2048]{1,0:T(8,128)(2,1)S(1)}, bf16[128,2048]{1,0:T(8,128)(2,1)}, u32[]{:S(2)}) copy-start(bf16[128,2048]{1,0:T(8,128)(2,1)} %key_ref.5) | copy-start | bytes 1572868
  5.5 113.3 %all-to-all-start = ((bf16[128,2,64,128]{3,2,1,0:T(8,128)(2,1)}), bf16[128,2,64,128]{3,2,1,0:T(8,128)(2,1)}, u32[]{:S(2)}, u32[]{:S(2)}) async-start(bf16[128,2,64,128]{3,2,1,0:T(8,128)(2,1)} %pack.1), calls=%async_computation | async-start | bytes 8388608 | tf_op jit(solution)/shard_map/all_to_all | solution.py:595
  151.7 29.3 %all-to-all-start.1 = ((bf16[16,2,2,64,128]{4,3,2,1,0:T(8,128)(2,1)}), bf16[16,2,2,64,128]{4,3,2,1,0:T(8,128)(2,1)S(1)}, u32[]{:S(2)}, u32[]{:S(2)}) async-start(bf16[16,2,2,64,128]{4,3,2,1,0:T(8,128)(2,1)} %repeat_ends.1), calls=%async_computation.1 | async-start | bytes 2097152 | tf_op jit(solution)/shard_map/all_to_all | solution.py:565
  157.8 21.2 %collective-permute-start = (bf16[2,64,2048]{2,1,0:T(8,128)(2,1)S(1)}, bf16[2,64,2048]{2,1,0:T(8,128)(2,1)S(1)}, u32[]{:S(2)}, u32[]{:S(2)}) collective-permute-start(bf16[2,64,2048]{2,1,0:T(8,128)(2,1)S(1)} %get-tuple-element.57), channel_id=1, source_target_pairs={{0,2},{2,4},{4,6},{6,8},{8,10},{10,12},{12,14},{14,16},{16,18},{18... | collective-permute-start | bytes 1572872 | tf_op jit(solution)/shard_map/ppermute | solution.py:540
  160.3 18.7 %collective-permute-start.1 = (bf16[2,64,2048]{2,1,0:T(8,128)(2,1)S(1)}, bf16[2,64,2048]{2,1,0:T(8,128)(2,1)S(1)}, u32[]{:S(2)}, u32[]{:S(2)}) collective-permute-start(bf16[2,64,2048]{2,1,0:T(8,128)(2,1)S(1)} %get-tuple-element.58), channel_id=1, source_target_pairs={{2,0},{4,2},{6,4},{8,6},{10,8},{12,10},{14,12},{16,14},{18,16},{20... | collective-permute-start | bytes 1572872 | tf_op jit(solution)/shard_map/ppermute | solution.py:540
  179.0 2.0 copy-start.5
  179.0 2.0 copy-start.6
  180.9 1.0 copy-start.2
  192.2 29.9 %all-to-all-start.2 = ((bf16[16,2,2,64,128]{4,3,2,1,0:T(8,128)(2,1)}), bf16[16,2,2,64,128]{4,3,2,1,0:T(8,128)(2,1)S(1)}, u32[]{:S(2)}, u32[]{:S(2)}) async-start(bf16[16,2,2,64,128]{4,3,2,1,0:T(8,128)(2,1)} %get-tuple-element.70), calls=%async_computation.2 | async-start | bytes 2097152 | tf_op jit(solution)/shard_map/all_to_all | solution.py:565
  199.4 13.7 %collective-permute-start.2 = (bf16[2,64,2048]{2,1,0:T(8,128)(2,1)}, bf16[2,64,2048]{2,1,0:T(8,128)(2,1)S(1)}, u32[]{:S(2)}, u32[]{:S(2)}) collective-permute-start(bf16[2,64,2048]{2,1,0:T(8,128)(2,1)} %get-tuple-element.67), channel_id=1, source_target_pairs={{2,0},{4,2},{6,4},{8,6},{10,8},{12,10},{14,12},{16,14},{18,16},{20... | collective-permute-start | bytes 1572872 | tf_op jit(solution)/shard_map/ppermute | solution.py:540
  202.8 18.2 %collective-permute-start.3 = (bf16[2,64,2048]{2,1,0:T(8,128)(2,1)}, bf16[2,64,2048]{2,1,0:T(8,128)(2,1)S(1)}, u32[]{:S(2)}, u32[]{:S(2)}) collective-permute-start(bf16[2,64,2048]{2,1,0:T(8,128)(2,1)} %get-tuple-element.68), channel_id=1, source_target_pairs={{0,2},{2,4},{4,6},{6,8},{8,10},{10,12},{12,14},{14,16},{16,18},{18... | collective-permute-start | bytes 1572872 | tf_op jit(solution)/shard_map/ppermute | solution.py:540
  213.1 10.4 %copy-start.3 = (bf16[2,64,2048]{2,1,0:T(8,128)(2,1)}, bf16[2,64,2048]{2,1,0:T(8,128)(2,1)S(1)}, u32[]{:S(2)}) copy-start(bf16[2,64,2048]{2,1,0:T(8,128)(2,1)S(1)} %collective-permute-done.2.high_ref) | copy-start | bytes 1572868
  221.0 2.5 copy-start.4
  223.5 103.6 %all-to-all-start.3 = ((bf16[128,2,64,128]{3,2,1,0:T(8,128)(2,1)}), bf16[128,2,64,128]{3,2,1,0:T(8,128)(2,1)}, u32[]{:S(2)}, u32[]{:S(2)}) async-start(bf16[128,2,64,128]{3,2,1,0:T(8,128)(2,1)} %slice_dynamic-update-slice_fusion), calls=%async_computation.3 | async-start | bytes 8388608 | tf_op jit(solution)/shard_map/all_to_all | solution.py:611

commit v6 on v4

--- a/solution.py
+++ b/solution.py
@@ -260,90 +260,71 @@
     grad_ref,
     part_ref,
     stat_ref,
-    ends0_ref,
-    ends1_ref,
-    ends2_ref,
-    ends3_ref,
+    ends_ref,
     attended_ref,
     query_part_ref,
     factor_ref,
-    terms0_ref,
-    terms1_ref,
-    terms2_ref,
-    terms3_ref,
+    terms_ref,
 ):
-    shard, my_y = where_ref[0], where_ref[2]
+    shard = where_ref[0]
     column = lax.broadcasted_iota(jnp.int32, (1, TOKENS_HERE), 1)
     no_end = ((shard == 0) & (column < BLOCK)) | ((shard == LAST) & (column >= BLOCK))
     bias = jnp.where(no_end, MASKED, 0.0)
-    ends_refs = (ends0_ref, ends1_ref, ends2_ref, ends3_ref)
-    terms_refs = (terms0_ref, terms1_ref, terms2_ref, terms3_ref)
-
-    def line(ends_ref, terms_ref):
-        heads = [(my_y - y) & 3 for y in range(SOME)]
-        queries = [query_ref[:, lanes(head)] for head in heads]
-        grads = [grad_ref[:, lanes(head)] for head in heads]
-        keys, values = (
-            [jnp.concatenate([ends_ref[y, 0, side], ends_ref[y, 1, side]]) for y in range(SOME)]
-            for side in range(2)
-        )
-        score = stacked(lambda i: nt(queries[i], keys[i])) + bias
-        stat = stacked(lambda i: stat_ref[heads[i]])
-        old_top = stat[:, 0:1]
-        top = jnp.maximum(old_top, jnp.max(score, axis=1, keepdims=True))
-        exps = jnp.exp2((score - top) * EXP2_SCALE)
-        shrink = jnp.exp2((old_top - top) * EXP2_SCALE)
-        total = stat[:, 1:2] * shrink
-        inverse = 1.0 / (total + jnp.sum(exps, axis=1, keepdims=True))
-        factor = shrink * inverse
-        weight = exps * inverse
-        low = weight.astype(BF16)
-        wgrad = stacked(lambda i: nt(grads[i], values[i]))
-        attended = stacked(lambda i: part_ref[heads[i]]) * factor
-        attended = attended + stacked(lambda i: nn(low[rows_of(i)], values[i]))
-        attended = attended.astype(BF16)
-        grad = stacked(lambda i: grads[i].astype(F32))
-        row_dot = jnp.sum(grad * attended.astype(F32), axis=1, keepdims=True)
-        sgrad = (weight * (wgrad - row_dot) * SCALE).astype(BF16)
-        stat = jnp.concatenate([factor, row_dot], axis=1)
-        for i, head in enumerate(heads):
-            at = rows_of(i)
-            attended_ref[:, lanes(head)] = attended[at]
-            factor_ref[head] = stat[at]
-            query_part_ref[head] = nn(sgrad[at], keys[i])
-            for side, left, right in ((0, sgrad, queries[i]), (1, low, grads[i])):
-                terms = tn(left[at], right).astype(BF16)
-                terms_ref[-i % NY, 0, side] = terms[:BLOCK]
-                terms_ref[-i % NY, 1, side] = terms[BLOCK:]
-
-    for x in range(NX):
-        pl.when(pl.program_id(0) == x)(
-            lambda x=x: line(ends_refs[x], terms_refs[-x % NX])
-        )
-
-
-def ends(where, query, grad, part, stat, lines):
-    line = struct((NY, 2, 2, BLOCK, DH), BF16)
-    line_spec = pl.BlockSpec(line.shape, lambda i, where: (0,) * 5)
+    queries = [query_ref[:, columns_of(i)] for i in range(SOME)]
+    grads = [grad_ref[:, columns_of(i)] for i in range(SOME)]
+    keys, values = (
+        [jnp.concatenate([ends_ref[i, 0, side], ends_ref[i, 1, side]]) for i in range(SOME)]
+        for side in range(2)
+    )
+    score = stacked(lambda i: nt(queries[i], keys[i])) + bias
+    stat = stacked(lambda i: stat_ref[i])
+    old_top = stat[:, 0:1]
+    top = jnp.maximum(old_top, jnp.max(score, axis=1, keepdims=True))
+    exps = jnp.exp2((score - top) * EXP2_SCALE)
+    shrink = jnp.exp2((old_top - top) * EXP2_SCALE)
+    total = stat[:, 1:2] * shrink
+    inverse = 1.0 / (total + jnp.sum(exps, axis=1, keepdims=True))
+    factor = shrink * inverse
+    weight = exps * inverse
+    low = weight.astype(BF16)
+    wgrad = stacked(lambda i: nt(grads[i], values[i]))
+    attended = stacked(lambda i: part_ref[i]) * factor
+    attended = attended + stacked(lambda i: nn(low[rows_of(i)], values[i]))
+    attended = attended.astype(BF16)
+    grad = stacked(lambda i: grads[i].astype(F32))
+    row_dot = jnp.sum(grad * attended.astype(F32), axis=1, keepdims=True)
+    sgrad = (weight * (wgrad - row_dot) * SCALE).astype(BF16)
+    stat = jnp.concatenate([factor, row_dot], axis=1)
+    for i in range(SOME):
+        at = rows_of(i)
+        attended_ref[:, columns_of(i)] = attended[at]
+        factor_ref[i] = stat[at]
+        query_part_ref[i] = nn(sgrad[at], keys[i])
+        for side, left, right in ((0, sgrad, queries[i]), (1, low, grads[i])):
+            terms = tn(left[at], right).astype(BF16)
+            terms_ref[i, 0, side] = terms[:BLOCK]
+            terms_ref[i, 1, side] = terms[BLOCK:]
+
+
+def ends(where, query, grad, part, stat, blocks):
     own = (HEADS, TOKENS_HERE, DH)
-
-    def line_heads(i, where):
-        return (where[1] - i) & 3
-
+    pair_spec = pl.BlockSpec((SOME, 2, 2, BLOCK, DH), lambda i, where: (i, 0, 0, 0, 0))
+    heads_specs = [head_spec(DH, step_of), head_spec(2, step_of)]
     return grid_call(
         ends_kernel,
         "ends",
         4 * 10**8,
         8 * 2**20,
         1,
-        [flat_spec(line_heads)] * 2
-        + [head_spec(DH, line_heads), head_spec(2, line_heads)]
-        + [line_spec] * NX,
-        [flat_spec(line_heads), head_spec(DH, line_heads), head_spec(2, line_heads)]
-        + [line_spec] * NX,
-        [struct((TOKENS_HERE, HEADS * DH), BF16), struct(own), struct(own[:2] + (2,))]
-        + [line] * NX,
-    )(where, query, grad, part, stat, *lines)
+        [flat_spec(step_of)] * 2 + heads_specs + [pair_spec],
+        [flat_spec(step_of)] + heads_specs + [pair_spec],
+        [
+            struct((TOKENS_HERE, HEADS * DH), BF16),
+            struct(own),
+            struct(own[:2] + (2,)),
+            struct((HEADS, 2, 2, BLOCK, DH), BF16),
+        ],
+    )(where, query, grad, part, stat, blocks)
 
 
 def far_terms_kernel(
@@ -517,45 +498,20 @@
     )(order, begins, terms, own, low, high)
 
 
-def shard_of(x, y, z):
-    return (x % NX * NY + y % NY) * NZ + z
-
-
 def send(value, route):
     return lax.ppermute(value, "seq", route)
 
 
-def x_shift(by):
-    cells = [(x, y, z) for x in range(NX) for y in range(NY) for z in range(NZ)]
-    return [(shard_of(x, y, z), shard_of(x + by, y, z)) for x, y, z in cells]
-
-
-def y_shift(by):
-    cells = [(x, y, z) for x in range(NX) for y in range(NY) for z in range(NZ)]
-    return [(shard_of(x, y, z), shard_of(x, y + by, z)) for x, y, z in cells]
-
-
-def spread_ends(pair):
-    line = jnp.stack([pair] + [send(pair, y_shift(by)) for by in range(1, NY)])
-    return [line] + [send(line, x_shift(by)) for by in range(1, NX)]
-
-
-def sum_line(lines):
-    line = lines[0].astype(F32)
-    for by in range(1, NX):
-        line = line + send(lines[by], x_shift(by)).astype(F32)
-    return line.astype(BF16), line[0]
-
-
-def sum_plane(low_line, pair):
-    for by in range(1, NY):
-        pair = pair + send(low_line[by], y_shift(by)).astype(F32)
-    return pair.astype(BF16)
+def swap_in_plane(pieces):
+    planes = [[cell * NZ + z for cell in range(NX * NY)] for z in range(NZ)]
+    return lax.all_to_all(
+        pieces, "seq", split_axis=0, concat_axis=0, tiled=True, axis_index_groups=planes
+    )
 
 
 def on_device(queries, key_states, values, out_grad, rand_blocks):
     shard = lax.axis_index("seq")
-    where = jnp.stack([shard, shard // (NY * NZ), shard // NZ % NY]).astype(jnp.int32)
+    where = shard.astype(jnp.int32).reshape(1)
     wanted = rand_blocks // 2 == shard
     item = rand_blocks % 2 * HEADS + lax.broadcasted_iota(jnp.int32, rand_blocks.shape, 1)
     items = jnp.max(jnp.where(wanted, item, -1), axis=(1, 2))
@@ -579,19 +535,21 @@
     up, down = [(i, i + 1) for i in range(LAST)], [(i + 1, i) for i in range(LAST)]
     slots = pack(jnp.maximum(items, 0), key_states, values)
     far = lax.all_to_all(slots, "seq", split_axis=0, concat_axis=0, tiled=True)
-    far, low, high = lax.optimization_barrier((far, low, high))
-    lines = spread_ends(jnp.stack([far[0], far[LAST]]))
     prev, following = send(high, up), send(low, down)
+    far, prev, following, picks, where = lax.optimization_barrier(
+        (far, prev, following, picks, where)
+    )
+    pair = jnp.stack([far[0], far[LAST]])
+    blocks = swap_in_plane(jnp.broadcast_to(pair[None], (HEADS,) + pair.shape))
     own_exps, far_exps, own_wgrads, far_wgrads, part, stat = near(
         picks, where, queries, out_grad, key_states, values, far, prev, following
     )
-    attended, query_part, factor, *end_terms = ends(where, queries, out_grad, part, stat, lines)
-    low_line, pair = sum_line(end_terms)
+    attended, query_part, factor, end_terms = ends(where, queries, out_grad, part, stat, blocks)
+    end_terms = swap_in_plane(end_terms)
     terms, prev_terms, next_terms = far_terms(
         picks, queries, out_grad, far_exps, far_wgrads, factor
     )
-    low_line, pair, terms = lax.optimization_barrier((low_line, pair, terms))
-    end_pair = sum_plane(low_line, pair)
+    end_pair = jnp.sum(end_terms.astype(F32), axis=0).astype(BF16)
     terms = terms.at[0].set(end_pair[0]).at[LAST].set(end_pair[1])
     back = lax.all_to_all(terms, "seq", split_axis=0, concat_axis=0, tiled=True)
     from_next, from_prev = send(prev_terms, down), send(next_terms, up)

time: 311 us -> 300 us (0.965)
  waiting for transfers between devices: 194 us -> 188 us
    all_to_all x1, waiting for transfers between devices: 96.5 us -> 0.01 us  [on_device(): far = lax.all_to_all(slots, 'seq', split_axis=0, concat_axis=0, tiled=True)]
    ppermute x16 -> x4, waiting for transfers between devices: 97.2 us -> 176 us  [send(): return lax.ppermute(value, 'seq', route)]
    ppermute x16 -> x4, starting transfers between devices: 32.7 us -> 20.1 us  [send(): return lax.ppermute(value, 'seq', route)]
    all_to_all x0 -> x2, waiting for transfers between devices: none -> 11.6 us  [swap_in_plane(): lax.all_to_all(pieces, 'seq', split_axis=0, concat_axis=0, tiled=True, ax...]
    all_to_all x0 -> x2, starting transfers between devices: none -> 10.3 us  [swap_in_plane(): lax.all_to_all(pieces, 'seq', split_axis=0, concat_axis=0, tiled=True, ax...]
  transfers between devices with their start and end apart: 18 -> 8, of which waited for: 11 -> 4; matrix products, arithmetic and copies ran while one was open for 1% -> 1% of each run, Pallas kernels for 9% -> 9%
where the time goes in v6:
time: 300 us; the launch traced here: 299 us
  waiting for transfers between devices  188 us (63%)
  starting transfers between devices  57.9 us (19%)
  Pallas kernels  42.8 us (14%)
  local copies, waits for them, and re-layouts  6.42 us (2%)
  other arithmetic  3.29 us (1%)
    ppermute x4, waiting for transfers between devices, send(): return lax.ppermute(value, 'seq', route)  176 us
    ppermute x4, starting transfers between devices, send(): return lax.ppermute(value, 'seq', route)  20.1 us
    all_to_all x1, starting transfers between devices, on_device(): far = lax.all_to_all(slots, 'seq', split_axis=0, concat_axis=0, tiled=True)  16.5 us
    all_to_all x2, waiting for transfers between devices, swap_in_plane(): lax.all_to_all(pieces, 'seq', split_axis=0, concat_axis=0, tiled=True, ax...  11.6 us
    all_to_all x1, starting transfers between devices, on_device(): back = lax.all_to_all(terms, 'seq', split_axis=0, concat_axis=0, tiled=True)  11 us
    all_to_all x2, starting transfers between devices, swap_in_plane(): lax.all_to_all(pieces, 'seq', split_axis=0, concat_axis=0, tiled=True, ax...  10.3 us
    pallas_call x1, Pallas kernels, own_terms(): grid_call(own_terms_kernel, 'own_terms', 5 * 10 ** 8, 16 * 2 ** 20, 1, [f...  10.2 us
    pallas_call x1, Pallas kernels, near(): grid_call(near_kernel, 'near', 6 * 10 ** 8, 16 * 2 ** 20, 2, [flat_spec(s...  8.84 us
  transfers between devices with their start and end apart: 8, of which 4 were waited for; matrix products, arithmetic and copies ran while one was open for 1% of the time, Pallas kernels for 9%

profile of v6, /device:TPU:6, one launch (start us, length us, event | category | flops | bytes accessed | tf_op | source)
XLA Modules:
  0.0 299.0 jit_solution(17265915872041945100)
XLA Ops:
  0.6 0.9 fusion.6
  1.5 0.1 reshape.127
  1.7 0.1 reduce_max.19
  1.8 0.5 broadcast_maximum_fusion.item_ref
  2.3 3.2 %pack.1 = bf16[128,2,64,128]{3,2,1,0:T(8,128)(2,1)} custom-call(s32[128]{0:T(128)} %broadcast_maximum_fusion.item_ref, bf16[128,2048]{1,0:T(8,128)(2,1)} %key_ref.5, bf16[128,2048]{1,0:T(8,128)(2,1)} %value_ref.3), custom_call_target="tpu_custom_call" | custom-call | bytes 6291456 | tf_op jit(solution)/shard_map/pack/pallas_call | solution.py:80
  5.5 0.0 copy-start
  5.5 0.0 copy-start.1
  5.5 16.5 %all-to-all-start = ((bf16[128,2,64,128]{3,2,1,0:T(8,128)(2,1)}), bf16[128,2,64,128]{3,2,1,0:T(8,128)(2,1)}, u32[]{:S(2)}, u32[]{:S(2)}) async-start(bf16[128,2,64,128]{3,2,1,0:T(8,128)(2,1)} %pack.1), calls=%async_computation | async-start | bytes 8388608 | tf_op jit(solution)/shard_map/all_to_all | solution.py:537
  22.0 0.0 copy-done
  22.1 0.0 copy-start.7
  22.1 0.1 slice_bitcast_fusion
  22.1 0.1 pad_maximum_fusion
  22.2 3.4 %collective-permute-start = (bf16[2,64,2048]{2,1,0:T(8,128)(2,1)S(1)}, bf16[2,64,2048]{2,1,0:T(8,128)(2,1)S(1)}, u32[]{:S(2)}, u32[]{:S(2)}) collective-permute-start(bf16[2,64,2048]{2,1,0:T(8,128)(2,1)S(1)} %pad_maximum_fusion), channel_id=1, source_target_pairs={{0,2},{2,4},{4,6},{6,8},{8,10},{10,12},{12,14},{14,16},{16,18},{18... | collective-permute-start | bytes 1572872 | tf_op jit(solution)/shard_map/ppermute | solution.py:502
  25.6 0.1 pad_maximum_fusion.1
  25.7 6.7 %collective-permute-start.1 = (bf16[2,64,2048]{2,1,0:T(8,128)(2,1)S(1)}, bf16[2,64,2048]{2,1,0:T(8,128)(2,1)S(1)}, u32[]{:S(2)}, u32[]{:S(2)}) collective-permute-start(bf16[2,64,2048]{2,1,0:T(8,128)(2,1)S(1)} %pad_maximum_fusion.1), channel_id=1, source_target_pairs={{2,0},{4,2},{6,4},{8,6},{10,8},{12,10},{14,12},{16,14},{18,16},{20... | collective-permute-start | bytes 1572872 | tf_op jit(solution)/shard_map/ppermute | solution.py:502
  32.4 0.1 constant_dynamic-slice_fusion
  32.4 0.2 copy.11
  32.6 0.6 reshape.128.pick_ref
  33.3 93.9 %collective-permute-done.prev_ref = bf16[2,64,2048]{2,1,0:T(8,128)(2,1)S(1)} collective-permute-done((bf16[2,64,2048]{2,1,0:T(8,128)(2,1)S(1)}, bf16[2,64,2048]{2,1,0:T(8,128)(2,1)S(1)}, u32[]{:S(2)}, u32[]{:S(2)}) %collective-permute-start) | collective-permute-done | bytes 524320 | tf_op jit(solution)/shard_map/ppermute | solution.py:502
  127.2 0.0 collective-permute-done.1.next_ref
  127.2 0.0 all-to-all-done.far_ref
  127.2 0.9 fusion.9
  128.1 1.2 broadcast_in_dim.14
  129.3 4.8 %all-to-all-start.1 = ((bf16[16,2,2,64,128]{4,3,2,1,0:T(8,128)(2,1)}), bf16[16,2,2,64,128]{4,3,2,1,0:T(8,128)(2,1)S(1)}, u32[]{:S(2)}, u32[]{:S(2)}) async-start(bf16[16,2,2,64,128]{4,3,2,1,0:T(8,128)(2,1)} %broadcast_in_dim.14), calls=%async_computation.1 | async-start | bytes 2097152 | tf_op jit(solution)/shard_map/all_to_all | solution.py:507
  134.1 0.0 copy-done.4
  134.1 8.8 %near.1 = (f32[16,128,128]{2,1,0:T(8,128)}, f32[16,128,256]{2,1,0:T(8,128)}, f32[16,128,128]{2,1,0:T(8,128)}, f32[16,128,256]{2,1,0:T(8,128)}, f32[16,128,128]{2,1,0:T(8,128)}, /*index=5*/f32[16,128,2]{2,1,0:T(8,128)}) custom-call(s32[96]{0:T(128)} %reshape.128.pick_ref, s32[1]{0:T(128)} %bitcast.4.where_ref, bf16[128,2048]{1,0:T(8,128)(2,1)} %query_ref.7, ...), custom_call_target="tpu_custom_call" | custom-call | flops 600000000 | bytes 16777216 | tf_op jit(solution)/shard_map/near/pallas_call | solution.py:244
  143.0 5.2 %all-to-all-done.1.ends_ref = bf16[16,2,2,64,128]{4,3,2,1,0:T(8,128)(2,1)S(1)} async-done(((bf16[16,2,2,64,128]{4,3,2,1,0:T(8,128)(2,1)}), bf16[16,2,2,64,128]{4,3,2,1,0:T(8,128)(2,1)S(1)}, u32[]{:S(2)}, u32[]{:S(2)}) %all-to-all-start.1) | async-done | bytes 1048608 | tf_op jit(solution)/shard_map/all_to_all | solution.py:507
  148.2 1.0 copy-done.2
  149.2 7.3 %ends.1 = (bf16[128,2048]{1,0:T(8,128)(2,1)}, f32[16,128,128]{2,1,0:T(8,128)}, f32[16,128,2]{2,1,0:T(8,128)}, bf16[16,2,2,64,128]{4,3,2,1,0:T(8,128)(2,1)}) custom-call(s32[1]{0:T(128)} %bitcast.4.where_ref, bf16[128,2048]{1,0:T(8,128)(2,1)} %query_ref.7, bf16[128,2048]{1,0:T(8,128)(2,1)} %grad_ref.7, f32[16,128,128]{2,1,0:T(8,128)} %get-tuple-element.55.part_ref, ...), custom_call_target="tpu_custom_call" | custom-call | flops 400000000 | bytes 8388608 | tf_op jit(solution)/shard_map/ends/pallas_call | solution.py:313
  156.5 5.5 %all-to-all-start.2 = ((bf16[16,2,2,64,128]{4,3,2,1,0:T(8,128)(2,1)}), bf16[16,2,2,64,128]{4,3,2,1,0:T(8,128)(2,1)S(1)}, u32[]{:S(2)}, u32[]{:S(2)}) async-start(bf16[16,2,2,64,128]{4,3,2,1,0:T(8,128)(2,1)} %get-tuple-element.66), calls=%async_computation.2 | async-start | bytes 2097152 | tf_op jit(solution)/shard_map/all_to_all | solution.py:507
  162.0 7.6 %far_terms.1 = (bf16[128,2,64,128]{3,2,1,0:T(8,128)(2,1)}, bf16[2,64,2048]{2,1,0:T(8,128)(2,1)}, bf16[2,64,2048]{2,1,0:T(8,128)(2,1)}) custom-call(s32[96]{0:T(128)} %reshape.128.pick_ref, bf16[128,2048]{1,0:T(8,128)(2,1)} %query_ref.7, bf16[128,2048]{1,0:T(8,128)(2,1)} %grad_ref.7, f32[16,128,256]{2,1,0:T(8,128)} %get-tuple-element.59.far_exp_ref.exp_ref, ...), custom_call_target="tpu_custom_call" | custom-call | flops 400000000 | bytes 14680064 | tf_op jit(solution)/shard_map/far_terms/pallas_call | solution.py:382
  169.6 6.4 %all-to-all-done.2 = bf16[16,2,2,64,128]{4,3,2,1,0:T(8,128)(2,1)S(1)} async-done(((bf16[16,2,2,64,128]{4,3,2,1,0:T(8,128)(2,1)}), bf16[16,2,2,64,128]{4,3,2,1,0:T(8,128)(2,1)S(1)}, u32[]{:S(2)}, u32[]{:S(2)}) %all-to-all-start.2) | async-done | bytes 1048608 | tf_op jit(solution)/shard_map/all_to_all | solution.py:507
  176.0 0.2 reduce_sum.42
  176.2 0.6 slice_dynamic-update-slice_fusion.1
  176.8 0.6 slice_dynamic-update-slice_fusion
  177.4 11.0 %all-to-all-start.3 = ((bf16[128,2,64,128]{3,2,1,0:T(8,128)(2,1)}), bf16[128,2,64,128]{3,2,1,0:T(8,128)(2,1)}, u32[]{:S(2)}, u32[]{:S(2)}) async-start(bf16[128,2,64,128]{3,2,1,0:T(8,128)(2,1)} %slice_dynamic-update-slice_fusion), calls=%async_computation.3 | async-start | bytes 8388608 | tf_op jit(solution)/shard_map/all_to_all | solution.py:554
  188.4 3.4 %collective-permute-start.2 = (bf16[2,64,2048]{2,1,0:T(8,128)(2,1)S(1)}, bf16[2,64,2048]{2,1,0:T(8,128)(2,1)S(1)}, u32[]{:S(2)}, u32[]{:S(2)}) collective-permute-start(bf16[2,64,2048]{2,1,0:T(8,128)(2,1)S(1)} %copy-done.9), channel_id=1, source_target_pairs={{0,2},{2,4},{4,6},{6,8},{8,10},{10,12},{12,14},{14,16},{16,18},{18... | collective-permute-start | bytes 1572872 | tf_op jit(solution)/shard_map/ppermute | solution.py:502
  191.8 6.7 %collective-permute-start.3 = (bf16[2,64,2048]{2,1,0:T(8,128)(2,1)S(1)}, bf16[2,64,2048]{2,1,0:T(8,128)(2,1)S(1)}, u32[]{:S(2)}, u32[]{:S(2)}) collective-permute-start(bf16[2,64,2048]{2,1,0:T(8,128)(2,1)S(1)} %copy-done.8), channel_id=1, source_target_pairs={{2,0},{4,2},{6,4},{8,6},{10,8},{12,10},{14,12},{16,14},{18,16},{20... | collective-permute-start | bytes 1572872 | tf_op jit(solution)/shard_map/ppermute | solution.py:502
  198.5 0.7 convert_reduce_fusion.1.begin_ref
  199.2 0.2 convert_reduce_fusion
  199.4 0.6 select_reduce_fusion.order_ref
  200.0 10.2 %own_terms.1 = (bf16[128,2048]{1,0:T(8,128)(2,1)}, f32[2,128,2048]{2,1,0:T(8,128)}) custom-call(s32[96]{0:T(128)} %reshape.128.pick_ref, bf16[128,2048]{1,0:T(8,128)(2,1)} %query_ref.7, bf16[128,2048]{1,0:T(8,128)(2,1)} %grad_ref.7, bf16[128,2048]{1,0:T(8,128)(2,1)} %key_ref.5, bf16[128,2,64,128]{3,2,1,0:T(8,128)(2,1)} %all-to-all-done.far_ref, ...), custom_call_target="tpu_custom_call" | custom-call | flops 500000000 | bytes 16777216 | tf_op jit(solution)/shard_map/own_terms/pallas_call | solution.py:443
  210.1 82.3 %collective-permute-done.2.low_ref = bf16[2,64,2048]{2,1,0:T(8,128)(2,1)S(1)} collective-permute-done((bf16[2,64,2048]{2,1,0:T(8,128)(2,1)S(1)}, bf16[2,64,2048]{2,1,0:T(8,128)(2,1)S(1)}, u32[]{:S(2)}, u32[]{:S(2)}) %collective-permute-start.2) | collective-permute-done | bytes 524320 | tf_op jit(solution)/shard_map/ppermute | solution.py:502
  292.4 0.0 collective-permute-done.3.high_ref
  292.4 0.0 all-to-all-done.3.terms_ref
  292.4 0.8 copy-done.5
  293.2 0.2 copy-done.6
  293.4 5.7 %gather.1 = (bf16[128,2048]{1,0:T(8,128)(2,1)}, bf16[128,2048]{1,0:T(8,128)(2,1)}) custom-call(s32[128]{0:T(128)} %select_reduce_fusion.order_ref, s32[33]{0:T(128)} %convert_reduce_fusion.1.begin_ref, bf16[128,2,64,128]{3,2,1,0:T(8,128)(2,1)} %all-to-all-done.3.terms_ref, f32[2,128,2048]{2,1,0:T(8,128)} %get-tuple-element.67.own_ref, ...), custom_call_target="tpu_custom_call" | custom-call | flops 1000000 | bytes 9437184 | tf_op jit(solution)/shard_map/gather/pallas_call | solution.py:490
  (14 shorter events, 0.0 us)
Async XLA Ops:
  5.5 16.5 %copy-start = (bf16[128,2048]{1,0:T(8,128)(2,1)S(1)}, bf16[128,2048]{1,0:T(8,128)(2,1)}, u32[]{:S(2)}) copy-start(bf16[128,2048]{1,0:T(8,128)(2,1)} %key_ref.5) | copy-start | bytes 1572868
  5.5 16.5 %copy-start.1 = (bf16[128,2048]{1,0:T(8,128)(2,1)S(1)}, bf16[128,2048]{1,0:T(8,128)(2,1)}, u32[]{:S(2)}) copy-start(bf16[128,2048]{1,0:T(8,128)(2,1)} %value_ref.3) | copy-start | bytes 1572868
  5.5 121.7 %all-to-all-start = ((bf16[128,2,64,128]{3,2,1,0:T(8,128)(2,1)}), bf16[128,2,64,128]{3,2,1,0:T(8,128)(2,1)}, u32[]{:S(2)}, u32[]{:S(2)}) async-start(bf16[128,2,64,128]{3,2,1,0:T(8,128)(2,1)} %pack.1), calls=%async_computation | async-start | bytes 8388608 | tf_op jit(solution)/shard_map/all_to_all | solution.py:537
  22.1 10.3 %copy-start.7 = (s32[256,16,3]{0,1,2:T(8,128)S(1)}, s32[256,16,3]{0,1,2:T(8,128)}, u32[]{:S(2)}) copy-start(s32[256,16,3]{0,1,2:T(8,128)} %param.13) | copy-start | bytes 147460
  22.2 105.0 %collective-permute-start = (bf16[2,64,2048]{2,1,0:T(8,128)(2,1)S(1)}, bf16[2,64,2048]{2,1,0:T(8,128)(2,1)S(1)}, u32[]{:S(2)}, u32[]{:S(2)}) collective-permute-start(bf16[2,64,2048]{2,1,0:T(8,128)(2,1)S(1)} %pad_maximum_fusion), channel_id=1, source_target_pairs={{0,2},{2,4},{4,6},{6,8},{8,10},{10,12},{12,14},{14,16},{16,18},{18... | collective-permute-start | bytes 1572872 | tf_op jit(solution)/shard_map/ppermute | solution.py:502
  25.7 101.6 %collective-permute-start.1 = (bf16[2,64,2048]{2,1,0:T(8,128)(2,1)S(1)}, bf16[2,64,2048]{2,1,0:T(8,128)(2,1)S(1)}, u32[]{:S(2)}, u32[]{:S(2)}) collective-permute-start(bf16[2,64,2048]{2,1,0:T(8,128)(2,1)S(1)} %pad_maximum_fusion.1), channel_id=1, source_target_pairs={{2,0},{4,2},{6,4},{8,6},{10,8},{12,10},{14,12},{16,14},{18,16},{20... | collective-permute-start | bytes 1572872 | tf_op jit(solution)/shard_map/ppermute | solution.py:502
  127.2 6.9 %copy-start.3 = (bf16[2,64,2048]{2,1,0:T(8,128)(2,1)}, bf16[2,64,2048]{2,1,0:T(8,128)(2,1)S(1)}, u32[]{:S(2)}) copy-start(bf16[2,64,2048]{2,1,0:T(8,128)(2,1)S(1)} %collective-permute-done.prev_ref) | copy-start | bytes 1572868
  127.2 6.9 %copy-start.4 = (bf16[2,64,2048]{2,1,0:T(8,128)(2,1)}, bf16[2,64,2048]{2,1,0:T(8,128)(2,1)S(1)}, u32[]{:S(2)}) copy-start(bf16[2,64,2048]{2,1,0:T(8,128)(2,1)S(1)} %collective-permute-done.1.next_ref) | copy-start | bytes 1572868
  129.3 18.9 %all-to-all-start.1 = ((bf16[16,2,2,64,128]{4,3,2,1,0:T(8,128)(2,1)}), bf16[16,2,2,64,128]{4,3,2,1,0:T(8,128)(2,1)S(1)}, u32[]{:S(2)}, u32[]{:S(2)}) async-start(bf16[16,2,2,64,128]{4,3,2,1,0:T(8,128)(2,1)} %broadcast_in_dim.14), calls=%async_computation.1 | async-start | bytes 2097152 | tf_op jit(solution)/shard_map/all_to_all | solution.py:507
  148.2 1.0 copy-start.2
  156.5 19.4 %all-to-all-start.2 = ((bf16[16,2,2,64,128]{4,3,2,1,0:T(8,128)(2,1)}), bf16[16,2,2,64,128]{4,3,2,1,0:T(8,128)(2,1)S(1)}, u32[]{:S(2)}, u32[]{:S(2)}) async-start(bf16[16,2,2,64,128]{4,3,2,1,0:T(8,128)(2,1)} %get-tuple-element.66), calls=%async_computation.2 | async-start | bytes 2097152 | tf_op jit(solution)/shard_map/all_to_all | solution.py:507
  177.4 11.0 %copy-start.9 = (bf16[2,64,2048]{2,1,0:T(8,128)(2,1)S(1)}, bf16[2,64,2048]{2,1,0:T(8,128)(2,1)}, u32[]{:S(2)}) copy-start(bf16[2,64,2048]{2,1,0:T(8,128)(2,1)} %get-tuple-element.68) | copy-start | bytes 1572868
  177.4 14.4 %copy-start.8 = (bf16[2,64,2048]{2,1,0:T(8,128)(2,1)S(1)}, bf16[2,64,2048]{2,1,0:T(8,128)(2,1)}, u32[]{:S(2)}) copy-start(bf16[2,64,2048]{2,1,0:T(8,128)(2,1)} %get-tuple-element.69) | copy-start | bytes 1572868
  177.4 115.0 %all-to-all-start.3 = ((bf16[128,2,64,128]{3,2,1,0:T(8,128)(2,1)}), bf16[128,2,64,128]{3,2,1,0:T(8,128)(2,1)}, u32[]{:S(2)}, u32[]{:S(2)}) async-start(bf16[128,2,64,128]{3,2,1,0:T(8,128)(2,1)} %slice_dynamic-update-slice_fusion), calls=%async_computation.3 | async-start | bytes 8388608 | tf_op jit(solution)/shard_map/all_to_all | solution.py:554
  188.4 104.0 %collective-permute-start.2 = (bf16[2,64,2048]{2,1,0:T(8,128)(2,1)S(1)}, bf16[2,64,2048]{2,1,0:T(8,128)(2,1)S(1)}, u32[]{:S(2)}, u32[]{:S(2)}) collective-permute-start(bf16[2,64,2048]{2,1,0:T(8,128)(2,1)S(1)} %copy-done.9), channel_id=1, source_target_pairs={{0,2},{2,4},{4,6},{6,8},{8,10},{10,12},{12,14},{14,16},{16,18},{18... | collective-permute-start | bytes 1572872 | tf_op jit(solution)/shard_map/ppermute | solution.py:502
  191.8 100.6 %collective-permute-start.3 = (bf16[2,64,2048]{2,1,0:T(8,128)(2,1)S(1)}, bf16[2,64,2048]{2,1,0:T(8,128)(2,1)S(1)}, u32[]{:S(2)}, u32[]{:S(2)}) collective-permute-start(bf16[2,64,2048]{2,1,0:T(8,128)(2,1)S(1)} %copy-done.8), channel_id=1, source_target_pairs={{2,0},{4,2},{6,4},{8,6},{10,8},{12,10},{14,12},{16,14},{18,16},{20... | collective-permute-start | bytes 1572872 | tf_op jit(solution)/shard_map/ppermute | solution.py:502
  292.4 0.8 copy-start.5
  292.4 1.0 copy-start.6

commit v7 on v6

--- a/solution.py
+++ b/solution.py
@@ -262,7 +262,7 @@
     stat_ref,
     ends_ref,
     attended_ref,
-    query_part_ref,
+    sgrad_ref,
     factor_ref,
     terms_ref,
 ):
@@ -299,7 +299,7 @@
         at = rows_of(i)
         attended_ref[:, columns_of(i)] = attended[at]
         factor_ref[i] = stat[at]
-        query_part_ref[i] = nn(sgrad[at], keys[i])
+        sgrad_ref[i] = sgrad[at]
         for side, left, right in ((0, sgrad, queries[i]), (1, low, grads[i])):
             terms = tn(left[at], right).astype(BF16)
             terms_ref[i, 0, side] = terms[:BLOCK]
@@ -320,7 +320,7 @@
         [flat_spec(step_of)] + heads_specs + [pair_spec],
         [
             struct((TOKENS_HERE, HEADS * DH), BF16),
-            struct(own),
+            struct(own, BF16),
             struct(own[:2] + (2,)),
             struct((HEADS, 2, 2, BLOCK, DH), BF16),
         ],
@@ -404,7 +404,8 @@
     far_exp_ref,
     own_wgrad_ref,
     far_wgrad_ref,
-    query_part_ref,
+    end_sgrad_ref,
+    ends_ref,
     factor_ref,
     query_grad_ref,
     own_ref,
@@ -432,14 +433,15 @@
             picked = [held_ref[head, b * 3 + r] for r in range(3)]
             return jnp.concatenate([edges[b][0, :, at]] + picked)
 
-        query_grad = query_part_ref[i] + nn(sgrad, key_ref[:, at])
+        end_key = jnp.concatenate([ends_ref[i, 0, 0], ends_ref[i, 1, 0]])
+        query_grad = nn(end_sgrad_ref[i], end_key) + nn(sgrad, key_ref[:, at])
         query_grad = query_grad + both(lambda b: nn(far_sgrad[HALVES[b]], far_key(b)))
         query_grad_ref[:, at] = query_grad.astype(BF16)
         own_ref[0, :, at] = tn(sgrad, query_ref[:, at])
         own_ref[1, :, at] = tn(weight.astype(BF16), grad_ref[:, at])
 
 
-def own_terms(picks, query, grad, key, far, prev, following, exps, wgrads, query_part, factor):
+def own_terms(picks, query, grad, key, far, prev, following, exps, wgrads, end_sgrad, blocks, factor):
     return grid_call(
         own_terms_kernel,
         "own_terms",
@@ -449,7 +451,9 @@
         [flat_spec(step_of)] * 3
         + [IN_HBM]
         + [edge_spec(step_of)] * 2
-        + [head_spec(w, step_of) for w in (DH, 2 * DH, DH, 2 * DH, DH, 2)],
+        + [head_spec(w, step_of) for w in (DH, 2 * DH, DH, 2 * DH, DH)]
+        + [pl.BlockSpec((SOME, 2, 2, BLOCK, DH), lambda i, picks: (i, 0, 0, 0, 0))]
+        + [head_spec(2, step_of)],
         [
             flat_spec(step_of),
             pl.BlockSpec((2, TOKENS_HERE, SOME * DH), lambda i, picks: (0, 0, i)),
@@ -459,38 +463,62 @@
             struct((2, TOKENS_HERE, HEADS * DH)),
         ],
         [pltpu.VMEM((HEADS, 6, BLOCK, DH), BF16), pltpu.SemaphoreType.DMA((HEADS,))],
-    )(picks, query, grad, key, far, prev, following, *exps, *wgrads, query_part, factor)
+    )(picks, query, grad, key, far, prev, following, *exps, *wgrads, end_sgrad, blocks, factor)
+
+
+USUAL = 4
 
 
 def gather_kernel(
     order_ref, begin_ref, terms_ref, own_ref, low_ref, high_ref, key_ref, value_ref
 ):
     edges = (low_ref, high_ref)
-    outs = (key_ref, value_ref)
-    for block in range(2):
-        for head in range(HEADS):
-            item = block * HEADS + head
-            at = slice(head * DH, (head + 1) * DH)
-
-            def add(place, totals):
-                slot = order_ref[place]
-                return tuple(totals[side] + terms_ref[slot, side].astype(F32) for side in range(2))
-
-            totals = tuple(
-                own_ref[side, HALVES[block], at] + edges[block][side, :, at].astype(F32)
-                for side in range(2)
-            )
-            totals = lax.fori_loop(begin_ref[item], begin_ref[item + 1], add, totals)
-            for side in range(2):
-                outs[side][HALVES[block], at] = totals[side].astype(BF16)
+
+    def one_side(out_ref):
+        for block in range(2):
+            for head in range(HEADS):
+                item = block * HEADS + head
+                at = columns_of(head)
+                begin, end = begin_ref[item], begin_ref[item + 1]
+
+                def term(place):
+                    return terms_ref[order_ref[place], 0].astype(F32)
+
+                total = own_ref[0, HALVES[block], at] + edges[block][0, :, at].astype(F32)
+                for i in range(USUAL):
+                    found = term(jnp.minimum(begin + i, SHARDS - 1))
+                    total = total + jnp.where(begin + i < end, found, 0.0)
+                total = lax.fori_loop(
+                    jnp.minimum(begin + USUAL, end), end, lambda p, sums: sums + term(p), total
+                )
+                out_ref[HALVES[block], at] = total.astype(BF16)
+
+    for side, out_ref in enumerate((key_ref, value_ref)):
+        pl.when(pl.program_id(0) == side)(lambda out_ref=out_ref: one_side(out_ref))
 
 
 def gather(order, begins, terms, own, low, high):
-    flat = struct((2 * BLOCK, HEADS * DH), BF16)
+    flat = struct((TOKENS_HERE, HEADS * DH), BF16)
+    flat_whole = pl.BlockSpec(flat.shape, lambda side, *scalars: (0, 0))
+
+    def side_spec(rows_there):
+        return pl.BlockSpec(
+            (1, rows_there, HEADS * DH), lambda side, *scalars: (side, 0, 0)
+        )
+
     return pl.pallas_call(
         gather_kernel,
-        in_specs=[IN_SMEM, IN_SMEM] + [IN_VMEM] * 4,
-        out_specs=[IN_VMEM] * 2,
+        grid_spec=pltpu.PrefetchScalarGridSpec(
+            num_scalar_prefetch=2,
+            grid=(2,),
+            in_specs=[
+                pl.BlockSpec((SHARDS, 1, BLOCK, DH), lambda side, *scalars: (0, side, 0, 0)),
+                side_spec(TOKENS_HERE),
+                side_spec(BLOCK),
+                side_spec(BLOCK),
+            ],
+            out_specs=[flat_whole, flat_whole],
+        ),
         out_shape=[flat, flat],
         compiler_params=params(),
         cost_estimate=cost(10**6, 9 * 2**20),
@@ -544,7 +572,7 @@
     own_exps, far_exps, own_wgrads, far_wgrads, part, stat = near(
         picks, where, queries, out_grad, key_states, values, far, prev, following
     )
-    attended, query_part, factor, end_terms = ends(where, queries, out_grad, part, stat, blocks)
+    attended, end_sgrad, factor, end_terms = ends(where, queries, out_grad, part, stat, blocks)
     end_terms = swap_in_plane(end_terms)
     terms, prev_terms, next_terms = far_terms(
         picks, queries, out_grad, far_exps, far_wgrads, factor
@@ -555,7 +583,7 @@
     from_next, from_prev = send(prev_terms, down), send(next_terms, up)
     query_grad, own = own_terms(
         picks, queries, out_grad, key_states, far, prev, following,
-        (own_exps, far_exps), (own_wgrads, far_wgrads), query_part, factor,
+        (own_exps, far_exps), (own_wgrads, far_wgrads), end_sgrad, blocks, factor,
     )
     key_grad, value_grad = gather(order, begins, back, own, from_prev, from_next)
     return (attended, query_grad, key_grad, value_grad)

time: 300 us -> 300 us (level)
  no operation moved by 1% of the time
where the time goes in v7:
time: 300 us; the launch traced here: 298 us
  waiting for transfers between devices  188 us (63%)
  starting transfers between devices  57.9 us (19%)
  Pallas kernels  42.3 us (14%)
  local copies, waits for them, and re-layouts  6.34 us (2%)
  other arithmetic  3.38 us (1%)
    ppermute x4, waiting for transfers between devices, send(): return lax.ppermute(value, 'seq', route)  176 us
    ppermute x4, starting transfers between devices, send(): return lax.ppermute(value, 'seq', route)  20.1 us
    all_to_all x1, starting transfers between devices, on_device(): far = lax.all_to_all(slots, 'seq', split_axis=0, concat_axis=0, tiled=True)  16.5 us
    all_to_all x2, waiting for transfers between devices, swap_in_plane(): lax.all_to_all(pieces, 'seq', split_axis=0, concat_axis=0, tiled=True, ax...  11.6 us
    all_to_all x1, starting transfers between devices, on_device(): back = lax.all_to_all(terms, 'seq', split_axis=0, concat_axis=0, tiled=True)  11 us
    all_to_all x2, starting transfers between devices, swap_in_plane(): lax.all_to_all(pieces, 'seq', split_axis=0, concat_axis=0, tiled=True, ax...  10.3 us
    pallas_call x1, Pallas kernels, own_terms(): grid_call(own_terms_kernel, 'own_terms', 5 * 10 ** 8, 16 * 2 ** 20, 1, [f...  10.2 us
    pallas_call x1, Pallas kernels, near(): grid_call(near_kernel, 'near', 6 * 10 ** 8, 16 * 2 ** 20, 2, [flat_spec(s...  8.84 us
  transfers between devices with their start and end apart: 8, of which 4 were waited for; matrix products, arithmetic and copies ran while one was open for 1% of the time, Pallas kernels for 9%

profile of v7, /device:TPU:6, one launch (start us, length us, event | category | flops | bytes accessed | tf_op | source)
XLA Modules:
  0.0 298.5 jit_solution(15255360818858735038)
XLA Ops:
  0.6 0.9 fusion.6
  1.5 0.1 reshape.127
  1.7 0.1 reduce_max.19
  1.8 0.5 broadcast_maximum_fusion.item_ref
  2.3 3.2 %pack.1 = bf16[128,2,64,128]{3,2,1,0:T(8,128)(2,1)} custom-call(s32[128]{0:T(128)} %broadcast_maximum_fusion.item_ref, bf16[128,2048]{1,0:T(8,128)(2,1)} %key_ref.5, bf16[128,2048]{1,0:T(8,128)(2,1)} %value_ref.3), custom_call_target="tpu_custom_call" | custom-call | bytes 6291456 | tf_op jit(solution)/shard_map/pack/pallas_call | solution.py:80
  5.5 0.0 copy-start.1
  5.5 0.0 copy-start.2
  5.5 16.5 %all-to-all-start = ((bf16[128,2,64,128]{3,2,1,0:T(8,128)(2,1)}), bf16[128,2,64,128]{3,2,1,0:T(8,128)(2,1)}, u32[]{:S(2)}, u32[]{:S(2)}) async-start(bf16[128,2,64,128]{3,2,1,0:T(8,128)(2,1)} %pack.1), calls=%async_computation | async-start | bytes 8388608 | tf_op jit(solution)/shard_map/all_to_all | solution.py:565
  22.0 0.0 copy-done.1
  22.0 0.0 copy-done.2
  22.1 0.0 copy-start.7
  22.1 0.1 slice_bitcast_fusion
  22.1 0.1 pad_maximum_fusion
  22.2 3.4 %collective-permute-start = (bf16[2,64,2048]{2,1,0:T(8,128)(2,1)S(1)}, bf16[2,64,2048]{2,1,0:T(8,128)(2,1)S(1)}, u32[]{:S(2)}, u32[]{:S(2)}) collective-permute-start(bf16[2,64,2048]{2,1,0:T(8,128)(2,1)S(1)} %pad_maximum_fusion), channel_id=1, source_target_pairs={{0,2},{2,4},{4,6},{6,8},{8,10},{10,12},{12,14},{14,16},{16,18},{18... | collective-permute-start | bytes 1572872 | tf_op jit(solution)/shard_map/ppermute | solution.py:530
  25.6 0.1 pad_maximum_fusion.1
  25.7 6.7 %collective-permute-start.1 = (bf16[2,64,2048]{2,1,0:T(8,128)(2,1)S(1)}, bf16[2,64,2048]{2,1,0:T(8,128)(2,1)S(1)}, u32[]{:S(2)}, u32[]{:S(2)}) collective-permute-start(bf16[2,64,2048]{2,1,0:T(8,128)(2,1)S(1)} %pad_maximum_fusion.1), channel_id=1, source_target_pairs={{2,0},{4,2},{6,4},{8,6},{10,8},{12,10},{14,12},{16,14},{18,16},{20... | collective-permute-start | bytes 1572872 | tf_op jit(solution)/shard_map/ppermute | solution.py:530
  32.4 0.1 constant_dynamic-slice_fusion
  32.4 0.2 copy.11
  32.6 0.6 reshape.128.pick_ref
  33.2 94.0 %collective-permute-done.prev_ref = bf16[2,64,2048]{2,1,0:T(8,128)(2,1)S(1)} collective-permute-done((bf16[2,64,2048]{2,1,0:T(8,128)(2,1)S(1)}, bf16[2,64,2048]{2,1,0:T(8,128)(2,1)S(1)}, u32[]{:S(2)}, u32[]{:S(2)}) %collective-permute-start) | collective-permute-done | bytes 524320 | tf_op jit(solution)/shard_map/ppermute | solution.py:530
  127.2 0.0 collective-permute-done.1.next_ref
  127.2 0.0 all-to-all-done.far_ref
  127.2 0.9 fusion.9
  128.1 1.2 broadcast_in_dim.14
  129.3 4.8 %all-to-all-start.1 = ((bf16[16,2,2,64,128]{4,3,2,1,0:T(8,128)(2,1)}), bf16[16,2,2,64,128]{4,3,2,1,0:T(8,128)(2,1)S(1)}, u32[]{:S(2)}, u32[]{:S(2)}) async-start(bf16[16,2,2,64,128]{4,3,2,1,0:T(8,128)(2,1)} %broadcast_in_dim.14), calls=%async_computation.1 | async-start | bytes 2097152 | tf_op jit(solution)/shard_map/all_to_all | solution.py:535
  134.1 8.8 %near.1 = (f32[16,128,128]{2,1,0:T(8,128)}, f32[16,128,256]{2,1,0:T(8,128)}, f32[16,128,128]{2,1,0:T(8,128)}, f32[16,128,256]{2,1,0:T(8,128)}, f32[16,128,128]{2,1,0:T(8,128)}, /*index=5*/f32[16,128,2]{2,1,0:T(8,128)}) custom-call(s32[96]{0:T(128)} %reshape.128.pick_ref, s32[1]{0:T(128)} %bitcast.4.where_ref, bf16[128,2048]{1,0:T(8,128)(2,1)} %query_ref.7, ...), custom_call_target="tpu_custom_call" | custom-call | flops 600000000 | bytes 16777216 | tf_op jit(solution)/shard_map/near/pallas_call | solution.py:244
  143.0 5.2 %all-to-all-done.1.ends_ref = bf16[16,2,2,64,128]{4,3,2,1,0:T(8,128)(2,1)S(1)} async-done(((bf16[16,2,2,64,128]{4,3,2,1,0:T(8,128)(2,1)}), bf16[16,2,2,64,128]{4,3,2,1,0:T(8,128)(2,1)S(1)}, u32[]{:S(2)}, u32[]{:S(2)}) %all-to-all-start.1) | async-done | bytes 1048608 | tf_op jit(solution)/shard_map/all_to_all | solution.py:535
  148.2 1.0 copy-done
  149.2 6.9 %ends.1 = (bf16[128,2048]{1,0:T(8,128)(2,1)}, bf16[16,128,128]{2,1,0:T(8,128)(2,1)}, f32[16,128,2]{2,1,0:T(8,128)}, bf16[16,2,2,64,128]{4,3,2,1,0:T(8,128)(2,1)}) custom-call(s32[1]{0:T(128)} %bitcast.4.where_ref, bf16[128,2048]{1,0:T(8,128)(2,1)} %query_ref.7, bf16[128,2048]{1,0:T(8,128)(2,1)} %grad_ref.7, f32[16,128,128]{2,1,0:T(8,128)} %get-tuple-element.55.part_ref, ...), custom_call_target="tpu_custom_call" | custom-call | flops 400000000 | bytes 8388608 | tf_op jit(solution)/shard_map/ends/pallas_call | solution.py:313
  156.1 5.5 %all-to-all-start.2 = ((bf16[16,2,2,64,128]{4,3,2,1,0:T(8,128)(2,1)}), bf16[16,2,2,64,128]{4,3,2,1,0:T(8,128)(2,1)S(1)}, u32[]{:S(2)}, u32[]{:S(2)}) async-start(bf16[16,2,2,64,128]{4,3,2,1,0:T(8,128)(2,1)} %get-tuple-element.66), calls=%async_computation.2 | async-start | bytes 2097152 | tf_op jit(solution)/shard_map/all_to_all | solution.py:535
  161.5 7.6 %far_terms.1 = (bf16[128,2,64,128]{3,2,1,0:T(8,128)(2,1)}, bf16[2,64,2048]{2,1,0:T(8,128)(2,1)}, bf16[2,64,2048]{2,1,0:T(8,128)(2,1)}) custom-call(s32[96]{0:T(128)} %reshape.128.pick_ref, bf16[128,2048]{1,0:T(8,128)(2,1)} %query_ref.7, bf16[128,2048]{1,0:T(8,128)(2,1)} %grad_ref.7, f32[16,128,256]{2,1,0:T(8,128)} %get-tuple-element.59.far_exp_ref.exp_ref, ...), custom_call_target="tpu_custom_call" | custom-call | flops 400000000 | bytes 14680064 | tf_op jit(solution)/shard_map/far_terms/pallas_call | solution.py:382
  169.1 6.4 %all-to-all-done.2 = bf16[16,2,2,64,128]{4,3,2,1,0:T(8,128)(2,1)S(1)} async-done(((bf16[16,2,2,64,128]{4,3,2,1,0:T(8,128)(2,1)}), bf16[16,2,2,64,128]{4,3,2,1,0:T(8,128)(2,1)S(1)}, u32[]{:S(2)}, u32[]{:S(2)}) %all-to-all-start.2) | async-done | bytes 1048608 | tf_op jit(solution)/shard_map/all_to_all | solution.py:535
  175.5 0.2 reduce_sum.42
  175.7 0.6 slice_dynamic-update-slice_fusion.1
  176.3 0.6 slice_dynamic-update-slice_fusion
  176.9 11.0 %all-to-all-start.3 = ((bf16[128,2,64,128]{3,2,1,0:T(8,128)(2,1)}), bf16[128,2,64,128]{3,2,1,0:T(8,128)(2,1)}, u32[]{:S(2)}, u32[]{:S(2)}) async-start(bf16[128,2,64,128]{3,2,1,0:T(8,128)(2,1)} %slice_dynamic-update-slice_fusion), calls=%async_computation.3 | async-start | bytes 8388608 | tf_op jit(solution)/shard_map/all_to_all | solution.py:582
  187.9 3.4 %collective-permute-start.2 = (bf16[2,64,2048]{2,1,0:T(8,128)(2,1)S(1)}, bf16[2,64,2048]{2,1,0:T(8,128)(2,1)S(1)}, u32[]{:S(2)}, u32[]{:S(2)}) collective-permute-start(bf16[2,64,2048]{2,1,0:T(8,128)(2,1)S(1)} %copy-done.9), channel_id=1, source_target_pairs={{0,2},{2,4},{4,6},{6,8},{8,10},{10,12},{12,14},{14,16},{16,18},{18... | collective-permute-start | bytes 1572872 | tf_op jit(solution)/shard_map/ppermute | solution.py:530
  191.3 6.7 %collective-permute-start.3 = (bf16[2,64,2048]{2,1,0:T(8,128)(2,1)S(1)}, bf16[2,64,2048]{2,1,0:T(8,128)(2,1)S(1)}, u32[]{:S(2)}, u32[]{:S(2)}) collective-permute-start(bf16[2,64,2048]{2,1,0:T(8,128)(2,1)S(1)} %copy-done.8), channel_id=1, source_target_pairs={{2,0},{4,2},{6,4},{8,6},{10,8},{12,10},{14,12},{16,14},{18,16},{20... | collective-permute-start | bytes 1572872 | tf_op jit(solution)/shard_map/ppermute | solution.py:530
  198.0 0.7 convert_reduce_fusion.1.begin_ref
  198.7 0.2 convert_reduce_fusion
  198.9 0.7 select_reduce_fusion.order_ref
  199.6 10.2 %own_terms.1 = (bf16[128,2048]{1,0:T(8,128)(2,1)}, f32[2,128,2048]{2,1,0:T(8,128)}) custom-call(s32[96]{0:T(128)} %reshape.128.pick_ref, bf16[128,2048]{1,0:T(8,128)(2,1)} %query_ref.7, bf16[128,2048]{1,0:T(8,128)(2,1)} %grad_ref.7, bf16[128,2048]{1,0:T(8,128)(2,1)} %key_ref.5, bf16[128,2,64,128]{3,2,1,0:T(8,128)(2,1)} %all-to-all-done.far_ref, ...), custom_call_target="tpu_custom_call" | custom-call | flops 500000000 | bytes 16777216 | tf_op jit(solution)/shard_map/own_terms/pallas_call | solution.py:445
  209.8 82.2 %collective-permute-done.2.low_ref = bf16[2,64,2048]{2,1,0:T(8,128)(2,1)S(1)} collective-permute-done((bf16[2,64,2048]{2,1,0:T(8,128)(2,1)S(1)}, bf16[2,64,2048]{2,1,0:T(8,128)(2,1)S(1)}, u32[]{:S(2)}, u32[]{:S(2)}) %collective-permute-start.2) | collective-permute-done | bytes 524320 | tf_op jit(solution)/shard_map/ppermute | solution.py:530
  292.0 0.0 collective-permute-done.3.high_ref
  292.0 0.0 all-to-all-done.3.terms_ref
  292.0 0.8 copy-done.5
  292.8 0.2 copy-done.6
  292.9 5.6 %gather.1 = (bf16[128,2048]{1,0:T(8,128)(2,1)}, bf16[128,2048]{1,0:T(8,128)(2,1)}) custom-call(s32[128]{0:T(128)} %select_reduce_fusion.order_ref, s32[33]{0:T(128)} %convert_reduce_fusion.1.begin_ref, bf16[128,2,64,128]{3,2,1,0:T(8,128)(2,1)} %all-to-all-done.3.terms_ref, f32[2,128,2048]{2,1,0:T(8,128)} %get-tuple-element.67.own_ref, ...), custom_call_target="tpu_custom_call" | custom-call | flops 1000000 | bytes 9437184 | tf_op jit(solution)/shard_map/gather/pallas_call | solution.py:509
  (14 shorter events, 0.0 us)
Async XLA Ops:
  5.5 16.5 %copy-start.1 = (bf16[128,2048]{1,0:T(8,128)(2,1)S(1)}, bf16[128,2048]{1,0:T(8,128)(2,1)}, u32[]{:S(2)}) copy-start(bf16[128,2048]{1,0:T(8,128)(2,1)} %key_ref.5) | copy-start | bytes 1572868
  5.5 16.5 %copy-start.2 = (bf16[128,2048]{1,0:T(8,128)(2,1)S(1)}, bf16[128,2048]{1,0:T(8,128)(2,1)}, u32[]{:S(2)}) copy-start(bf16[128,2048]{1,0:T(8,128)(2,1)} %value_ref.3) | copy-start | bytes 1572868
  5.5 121.7 %all-to-all-start = ((bf16[128,2,64,128]{3,2,1,0:T(8,128)(2,1)}), bf16[128,2,64,128]{3,2,1,0:T(8,128)(2,1)}, u32[]{:S(2)}, u32[]{:S(2)}) async-start(bf16[128,2,64,128]{3,2,1,0:T(8,128)(2,1)} %pack.1), calls=%async_computation | async-start | bytes 8388608 | tf_op jit(solution)/shard_map/all_to_all | solution.py:565
  22.1 10.3 %copy-start.7 = (s32[256,16,3]{0,1,2:T(8,128)S(1)}, s32[256,16,3]{0,1,2:T(8,128)}, u32[]{:S(2)}) copy-start(s32[256,16,3]{0,1,2:T(8,128)} %param.13) | copy-start | bytes 147460
  22.2 105.0 %collective-permute-start = (bf16[2,64,2048]{2,1,0:T(8,128)(2,1)S(1)}, bf16[2,64,2048]{2,1,0:T(8,128)(2,1)S(1)}, u32[]{:S(2)}, u32[]{:S(2)}) collective-permute-start(bf16[2,64,2048]{2,1,0:T(8,128)(2,1)S(1)} %pad_maximum_fusion), channel_id=1, source_target_pairs={{0,2},{2,4},{4,6},{6,8},{8,10},{10,12},{12,14},{14,16},{16,18},{18... | collective-permute-start | bytes 1572872 | tf_op jit(solution)/shard_map/ppermute | solution.py:530
  25.7 101.6 %collective-permute-start.1 = (bf16[2,64,2048]{2,1,0:T(8,128)(2,1)S(1)}, bf16[2,64,2048]{2,1,0:T(8,128)(2,1)S(1)}, u32[]{:S(2)}, u32[]{:S(2)}) collective-permute-start(bf16[2,64,2048]{2,1,0:T(8,128)(2,1)S(1)} %pad_maximum_fusion.1), channel_id=1, source_target_pairs={{2,0},{4,2},{6,4},{8,6},{10,8},{12,10},{14,12},{16,14},{18,16},{20... | collective-permute-start | bytes 1572872 | tf_op jit(solution)/shard_map/ppermute | solution.py:530
  127.2 6.9 %copy-start.3 = (bf16[2,64,2048]{2,1,0:T(8,128)(2,1)}, bf16[2,64,2048]{2,1,0:T(8,128)(2,1)S(1)}, u32[]{:S(2)}) copy-start(bf16[2,64,2048]{2,1,0:T(8,128)(2,1)S(1)} %collective-permute-done.prev_ref) | copy-start | bytes 1572868
  127.2 6.9 %copy-start.4 = (bf16[2,64,2048]{2,1,0:T(8,128)(2,1)}, bf16[2,64,2048]{2,1,0:T(8,128)(2,1)S(1)}, u32[]{:S(2)}) copy-start(bf16[2,64,2048]{2,1,0:T(8,128)(2,1)S(1)} %collective-permute-done.1.next_ref) | copy-start | bytes 1572868
  129.3 18.9 %all-to-all-start.1 = ((bf16[16,2,2,64,128]{4,3,2,1,0:T(8,128)(2,1)}), bf16[16,2,2,64,128]{4,3,2,1,0:T(8,128)(2,1)S(1)}, u32[]{:S(2)}, u32[]{:S(2)}) async-start(bf16[16,2,2,64,128]{4,3,2,1,0:T(8,128)(2,1)} %broadcast_in_dim.14), calls=%async_computation.1 | async-start | bytes 2097152 | tf_op jit(solution)/shard_map/all_to_all | solution.py:535
  148.2 1.0 copy-start
  156.1 19.4 %all-to-all-start.2 = ((bf16[16,2,2,64,128]{4,3,2,1,0:T(8,128)(2,1)}), bf16[16,2,2,64,128]{4,3,2,1,0:T(8,128)(2,1)S(1)}, u32[]{:S(2)}, u32[]{:S(2)}) async-start(bf16[16,2,2,64,128]{4,3,2,1,0:T(8,128)(2,1)} %get-tuple-element.66), calls=%async_computation.2 | async-start | bytes 2097152 | tf_op jit(solution)/shard_map/all_to_all | solution.py:535
  176.9 11.0 %copy-start.9 = (bf16[2,64,2048]{2,1,0:T(8,128)(2,1)S(1)}, bf16[2,64,2048]{2,1,0:T(8,128)(2,1)}, u32[]{:S(2)}) copy-start(bf16[2,64,2048]{2,1,0:T(8,128)(2,1)} %get-tuple-element.68) | copy-start | bytes 1572868
  176.9 14.4 %copy-start.8 = (bf16[2,64,2048]{2,1,0:T(8,128)(2,1)S(1)}, bf16[2,64,2048]{2,1,0:T(8,128)(2,1)}, u32[]{:S(2)}) copy-start(bf16[2,64,2048]{2,1,0:T(8,128)(2,1)} %get-tuple-element.69) | copy-start | bytes 1572868
  176.9 115.1 %all-to-all-start.3 = ((bf16[128,2,64,128]{3,2,1,0:T(8,128)(2,1)}), bf16[128,2,64,128]{3,2,1,0:T(8,128)(2,1)}, u32[]{:S(2)}, u32[]{:S(2)}) async-start(bf16[128,2,64,128]{3,2,1,0:T(8,128)(2,1)} %slice_dynamic-update-slice_fusion), calls=%async_computation.3 | async-start | bytes 8388608 | tf_op jit(solution)/shard_map/all_to_all | solution.py:582
  187.9 104.0 %collective-permute-start.2 = (bf16[2,64,2048]{2,1,0:T(8,128)(2,1)S(1)}, bf16[2,64,2048]{2,1,0:T(8,128)(2,1)S(1)}, u32[]{:S(2)}, u32[]{:S(2)}) collective-permute-start(bf16[2,64,2048]{2,1,0:T(8,128)(2,1)S(1)} %copy-done.9), channel_id=1, source_target_pairs={{0,2},{2,4},{4,6},{6,8},{8,10},{10,12},{12,14},{14,16},{16,18},{18... | collective-permute-start | bytes 1572872 | tf_op jit(solution)/shard_map/ppermute | solution.py:530
  191.3 100.6 %collective-permute-start.3 = (bf16[2,64,2048]{2,1,0:T(8,128)(2,1)S(1)}, bf16[2,64,2048]{2,1,0:T(8,128)(2,1)S(1)}, u32[]{:S(2)}, u32[]{:S(2)}) collective-permute-start(bf16[2,64,2048]{2,1,0:T(8,128)(2,1)S(1)} %copy-done.8), channel_id=1, source_target_pairs={{2,0},{4,2},{6,4},{8,6},{10,8},{12,10},{14,12},{16,14},{18,16},{20... | collective-permute-start | bytes 1572872 | tf_op jit(solution)/shard_map/ppermute | solution.py:530
  291.9 0.8 copy-start.5
  292.0 1.0 copy-start.6

commit v8 on v7

--- a/solution.py
+++ b/solution.py
@@ -26,8 +26,8 @@
 IN_HBM = pl.BlockSpec(memory_space=pltpu.HBM)
 
 
-def params():
-    return pltpu.CompilerParams(vmem_limit_bytes=VMEM_BYTES)
+def params(vmem_bytes=VMEM_BYTES):
+    return pltpu.CompilerParams(vmem_limit_bytes=vmem_bytes)
 
 
 def cost(flops, moved, exps=0):
@@ -109,6 +109,21 @@
 
 def head_spec(width, where_to):
     return pl.BlockSpec((SOME, TOKENS_HERE, width), lambda *at: (where_to(*at), 0, 0))
+
+
+def stat_spec(where_to):
+    return pl.BlockSpec((1, TOKENS_HERE, 2 * SOME), lambda *at: (where_to(*at), 0, 0))
+
+
+STATS = (STEPS, TOKENS_HERE, 2 * SOME)
+
+
+def side_by_side(stat):
+    return jnp.concatenate([stat[rows_of(i)] for i in range(SOME)], axis=1)
+
+
+def stat_of(stat_ref, i, which):
+    return stat_ref[0, :, 2 * i + which : 2 * i + which + 1]
 
 
 def grid_call(kernel, name, flops, moved, prefetch, in_specs, out_specs, out_shape, scratch=()):
@@ -228,10 +243,11 @@
     far_exp = jnp.exp2((far_score - top) * EXP2_SCALE)
     total = own_exp + far_exp[:, :TOKENS_HERE] + far_exp[:, TOKENS_HERE:]
     stat = jnp.concatenate([top, jnp.sum(total, axis=1, keepdims=True)], axis=1)
+    stat_ref[0] = side_by_side(stat)
     own_low, far_low = own_exp.astype(BF16), far_exp.astype(BF16)
     for i in range(SOME):
         at = rows_of(i)
-        own_exp_ref[i], far_exp_ref[i], stat_ref[i] = own_exp[at], far_exp[at], stat[at]
+        own_exp_ref[i], far_exp_ref[i] = own_exp[at], far_exp[at]
         own_wgrad_ref[i] = nt(grads[i], value_ref[:, columns_of(i)])
         far_part = both(lambda b: nn(far_low[half_rows(i, b)], values[i][b]))
         part_ref[i] = nn(own_low[at], value_ref[:, columns_of(i)]) + far_part
@@ -248,8 +264,8 @@
         16 * 2**20,
         2,
         [flat_spec(step_of)] * 4 + [IN_HBM] + [edge_spec(step_of)] * 2,
-        [head_spec(w, step_of) for w in (DH, 2 * DH, DH, 2 * DH, DH, 2)],
-        [struct(own), struct(wide), struct(own), struct(wide), struct(own), struct(own[:2] + (2,))],
+        [head_spec(w, step_of) for w in (DH, 2 * DH, DH, 2 * DH, DH)] + [stat_spec(step_of)],
+        [struct(own), struct(wide), struct(own), struct(wide), struct(own), struct(STATS)],
         [pltpu.VMEM((HEADS, 6, 2, BLOCK, DH), BF16), pltpu.SemaphoreType.DMA((HEADS,))],
     )(picks, where, query, grad, key, value, far, prev, following)
 
@@ -277,12 +293,11 @@
         for side in range(2)
     )
     score = stacked(lambda i: nt(queries[i], keys[i])) + bias
-    stat = stacked(lambda i: stat_ref[i])
-    old_top = stat[:, 0:1]
+    old_top = stacked(lambda i: stat_of(stat_ref, i, 0))
     top = jnp.maximum(old_top, jnp.max(score, axis=1, keepdims=True))
     exps = jnp.exp2((score - top) * EXP2_SCALE)
     shrink = jnp.exp2((old_top - top) * EXP2_SCALE)
-    total = stat[:, 1:2] * shrink
+    total = stacked(lambda i: stat_of(stat_ref, i, 1)) * shrink
     inverse = 1.0 / (total + jnp.sum(exps, axis=1, keepdims=True))
     factor = shrink * inverse
     weight = exps * inverse
@@ -294,11 +309,10 @@
     grad = stacked(lambda i: grads[i].astype(F32))
     row_dot = jnp.sum(grad * attended.astype(F32), axis=1, keepdims=True)
     sgrad = (weight * (wgrad - row_dot) * SCALE).astype(BF16)
-    stat = jnp.concatenate([factor, row_dot], axis=1)
+    factor_ref[0] = side_by_side(jnp.concatenate([factor, row_dot], axis=1))
     for i in range(SOME):
         at = rows_of(i)
         attended_ref[:, columns_of(i)] = attended[at]
-        factor_ref[i] = stat[at]
         sgrad_ref[i] = sgrad[at]
         for side, left, right in ((0, sgrad, queries[i]), (1, low, grads[i])):
             terms = tn(left[at], right).astype(BF16)
@@ -309,7 +323,7 @@
 def ends(where, query, grad, part, stat, blocks):
     own = (HEADS, TOKENS_HERE, DH)
     pair_spec = pl.BlockSpec((SOME, 2, 2, BLOCK, DH), lambda i, where: (i, 0, 0, 0, 0))
-    heads_specs = [head_spec(DH, step_of), head_spec(2, step_of)]
+    heads_specs = [head_spec(DH, step_of), stat_spec(step_of)]
     return grid_call(
         ends_kernel,
         "ends",
@@ -321,7 +335,7 @@
         [
             struct((TOKENS_HERE, HEADS * DH), BF16),
             struct(own, BF16),
-            struct(own[:2] + (2,)),
+            struct(STATS),
             struct((HEADS, 2, 2, BLOCK, DH), BF16),
         ],
     )(where, query, grad, part, stat, blocks)
@@ -354,9 +368,9 @@
     for i in range(SOME):
         head = step * SOME + i
         at = columns_of(i)
-        weight = exp_ref[i] * factor_ref[i, :, 0:1]
+        weight = exp_ref[i] * stat_of(factor_ref, i, 0)
         low = weight.astype(BF16)
-        sgrad = (weight * (wgrad_ref[i] - factor_ref[i, :, 1:2]) * SCALE).astype(BF16)
+        sgrad = (weight * (wgrad_ref[i] - stat_of(factor_ref, i, 1)) * SCALE).astype(BF16)
         for side, left, right in ((0, sgrad, query_ref[:, at]), (1, low, grad_ref[:, at])):
             parts = tn(left, split(right)).astype(BF16)
             for b, edge_ref in enumerate((prev_terms_ref, next_terms_ref)):
@@ -385,7 +399,7 @@
         4 * 10**8,
         14 * 2**20,
         1,
-        [flat_spec(step_of)] * 2 + [head_spec(w, step_of) for w in (2 * DH, 2 * DH, 2)],
+        [flat_spec(step_of)] * 2 + [head_spec(2 * DH, step_of)] * 2 + [stat_spec(step_of)],
         [IN_HBM, edge_spec(step_of), edge_spec(step_of)],
         [struct((SHARDS, 2, BLOCK, DH), BF16), edge, edge],
         [pltpu.VMEM((HEADS, 6, 2, BLOCK, DH), BF16), pltpu.SemaphoreType.DMA((1,))],
@@ -423,7 +437,7 @@
         head = step * SOME + i
         at = columns_of(i)
         fetched(held_ref, sem, head)
-        factor, row_dot = factor_ref[i, :, 0:1], factor_ref[i, :, 1:2]
+        factor, row_dot = stat_of(factor_ref, i, 0), stat_of(factor_ref, i, 1)
         weight = own_exp_ref[i] * factor
         sgrad = (weight * (own_wgrad_ref[i] - row_dot) * SCALE).astype(BF16)
         far_sgrad = far_exp_ref[i] * factor * (far_wgrad_ref[i] - row_dot) * SCALE
@@ -453,7 +467,7 @@
         + [edge_spec(step_of)] * 2
         + [head_spec(w, step_of) for w in (DH, 2 * DH, DH, 2 * DH, DH)]
         + [pl.BlockSpec((SOME, 2, 2, BLOCK, DH), lambda i, picks: (i, 0, 0, 0, 0))]
-        + [head_spec(2, step_of)],
+        + [stat_spec(step_of)],
         [
             flat_spec(step_of),
             pl.BlockSpec((2, TOKENS_HERE, SOME * DH), lambda i, picks: (0, 0, i)),
@@ -520,7 +534,7 @@
             out_specs=[flat_whole, flat_whole],
         ),
         out_shape=[flat, flat],
-        compiler_params=params(),
+        compiler_params=params(16 * 2**20),
         cost_estimate=cost(10**6, 9 * 2**20),
         name="gather",
     )(order, begins, terms, own, low, high)
@@ -528,6 +542,29 @@
 
 def send(value, route):
     return lax.ppermute(value, "seq", route)
+
+
+def repeat_kernel(first_ref, last_ref, out_ref):
+    for cell in range(HEADS):
+        out_ref[cell, 0] = first_ref[0]
+        out_ref[cell, 1] = last_ref[0]
+
+
+def repeat_ends(far):
+    def slot_spec(slot):
+        return pl.BlockSpec((1, 2, BLOCK, DH), lambda i: (slot, 0, 0, 0))
+
+    out = struct((HEADS, 2, 2, BLOCK, DH), BF16)
+    return pl.pallas_call(
+        repeat_kernel,
+        grid=(1,),
+        in_specs=[slot_spec(0), slot_spec(LAST)],
+        out_specs=pl.BlockSpec(out.shape, lambda i: (0,) * 5),
+        out_shape=out,
+        compiler_params=params(),
+        cost_estimate=cost(0, 2**20),
+        name="repeat_ends",
+    )(far, far)
 
 
 def swap_in_plane(pieces):
@@ -567,8 +604,7 @@
     far, prev, following, picks, where = lax.optimization_barrier(
         (far, prev, following, picks, where)
     )
-    pair = jnp.stack([far[0], far[LAST]])
-    blocks = swap_in_plane(jnp.broadcast_to(pair[None], (HEADS,) + pair.shape))
+    blocks = swap_in_plane(repeat_ends(far))
     own_exps, far_exps, own_wgrads, far_wgrads, part, stat = near(
         picks, where, queries, out_grad, key_states, values, far, prev, following
     )

time: 300 us -> 300 us (level)
  transfers between devices with their start and end apart: 8 -> 8, of which waited for: 4 -> 4; matrix products, arithmetic and copies ran while one was open for 1% -> 0% of each run, Pallas kernels for 9% -> 9%
where the time goes in v8:
time: 300 us; the launch traced here: 298 us
  waiting for transfers between devices  190 us (63%)
  starting transfers between devices  57.9 us (19%)
  Pallas kernels  42.7 us (14%)
  local copies, waits for them, and re-layouts  4.9 us (2%)
    ppermute x4, waiting for transfers between devices, send(): return lax.ppermute(value, 'seq', route)  177 us
    ppermute x4, starting transfers between devices, send(): return lax.ppermute(value, 'seq', route)  20.1 us
    all_to_all x1, starting transfers between devices, on_device(): far = lax.all_to_all(slots, 'seq', split_axis=0, concat_axis=0, tiled=True)  16.5 us
    all_to_all x2, waiting for transfers between devices, swap_in_plane(): lax.all_to_all(pieces, 'seq', split_axis=0, concat_axis=0, tiled=True, ax...  12.4 us
    all_to_all x1, starting transfers between devices, on_device(): back = lax.all_to_all(terms, 'seq', split_axis=0, concat_axis=0, tiled=True)  11 us
    all_to_all x2, starting transfers between devices, swap_in_plane(): lax.all_to_all(pieces, 'seq', split_axis=0, concat_axis=0, tiled=True, ax...  10.3 us
    pallas_call x1, Pallas kernels, own_terms(): grid_call(own_terms_kernel, 'own_terms', 5 * 10 ** 8, 16 * 2 ** 20, 1, [f...  10.1 us
    pallas_call x1, Pallas kernels, near(): grid_call(near_kernel, 'near', 6 * 10 ** 8, 16 * 2 ** 20, 2, [flat_spec(s...  8.37 us
  transfers between devices with their start and end apart: 8, of which 4 were waited for; matrix products, arithmetic and copies ran while one was open for 0% of the time, Pallas kernels for 9%

profile of v8, /device:TPU:6, one launch (start us, length us, event | category | flops | bytes accessed | tf_op | source)
XLA Modules:
  0.0 298.4 jit_solution(6394669864738072521)
XLA Ops:
  0.6 0.9 fusion.6
  1.5 0.1 reshape.126
  1.7 0.1 reduce_max.19
  1.8 0.5 broadcast_maximum_fusion.item_ref
  2.3 3.2 %pack.1 = bf16[128,2,64,128]{3,2,1,0:T(8,128)(2,1)} custom-call(s32[128]{0:T(128)} %broadcast_maximum_fusion.item_ref, bf16[128,2048]{1,0:T(8,128)(2,1)} %key_ref.5, bf16[128,2048]{1,0:T(8,128)(2,1)} %value_ref.3), custom_call_target="tpu_custom_call" | custom-call | bytes 6291456 | tf_op jit(solution)/shard_map/pack/pallas_call | solution.py:80
  5.5 0.0 copy-start.2
  5.5 0.0 copy-start.3
  5.5 16.5 %all-to-all-start = ((bf16[128,2,64,128]{3,2,1,0:T(8,128)(2,1)}), bf16[128,2,64,128]{3,2,1,0:T(8,128)(2,1)}, u32[]{:S(2)}, u32[]{:S(2)}) async-start(bf16[128,2,64,128]{3,2,1,0:T(8,128)(2,1)} %pack.1), calls=%async_computation | async-start | bytes 8388608 | tf_op jit(solution)/shard_map/all_to_all | solution.py:602
  22.0 0.0 copy-done.2
  22.1 0.0 copy-done.3
  22.1 0.0 copy-start.6
  22.1 0.1 slice_bitcast_fusion
  22.2 0.1 pad_maximum_fusion
  22.2 3.4 %collective-permute-start = (bf16[2,64,2048]{2,1,0:T(8,128)(2,1)S(1)}, bf16[2,64,2048]{2,1,0:T(8,128)(2,1)S(1)}, u32[]{:S(2)}, u32[]{:S(2)}) collective-permute-start(bf16[2,64,2048]{2,1,0:T(8,128)(2,1)S(1)} %pad_maximum_fusion), channel_id=1, source_target_pairs={{0,2},{2,4},{4,6},{6,8},{8,10},{10,12},{12,14},{14,16},{16,18},{18... | collective-permute-start | bytes 1572872 | tf_op jit(solution)/shard_map/ppermute | solution.py:544
  25.6 0.1 pad_maximum_fusion.1
  25.7 6.7 %collective-permute-start.1 = (bf16[2,64,2048]{2,1,0:T(8,128)(2,1)S(1)}, bf16[2,64,2048]{2,1,0:T(8,128)(2,1)S(1)}, u32[]{:S(2)}, u32[]{:S(2)}) collective-permute-start(bf16[2,64,2048]{2,1,0:T(8,128)(2,1)S(1)} %pad_maximum_fusion.1), channel_id=1, source_target_pairs={{2,0},{4,2},{6,4},{8,6},{10,8},{12,10},{14,12},{16,14},{18,16},{20... | collective-permute-start | bytes 1572872 | tf_op jit(solution)/shard_map/ppermute | solution.py:544
  32.4 0.0 copy-done.6
  32.4 0.1 constant_dynamic-slice_fusion
  32.4 0.2 copy.11
  32.7 0.6 reshape.127.pick_ref
  33.2 94.0 %collective-permute-done.prev_ref = bf16[2,64,2048]{2,1,0:T(8,128)(2,1)S(1)} collective-permute-done((bf16[2,64,2048]{2,1,0:T(8,128)(2,1)S(1)}, bf16[2,64,2048]{2,1,0:T(8,128)(2,1)S(1)}, u32[]{:S(2)}, u32[]{:S(2)}) %collective-permute-start) | collective-permute-done | bytes 524320 | tf_op jit(solution)/shard_map/ppermute | solution.py:544
  127.2 0.0 collective-permute-done.1.next_ref
  127.2 0.0 all-to-all-done.far_ref.first_ref.last_ref
  127.3 2.0 repeat_ends.1
  129.3 4.8 %all-to-all-start.1 = ((bf16[16,2,2,64,128]{4,3,2,1,0:T(8,128)(2,1)}), bf16[16,2,2,64,128]{4,3,2,1,0:T(8,128)(2,1)S(1)}, u32[]{:S(2)}, u32[]{:S(2)}) async-start(bf16[16,2,2,64,128]{4,3,2,1,0:T(8,128)(2,1)} %repeat_ends.1), calls=%async_computation.1 | async-start | bytes 2097152 | tf_op jit(solution)/shard_map/all_to_all | solution.py:572
  134.0 8.4 %near.1 = (f32[16,128,128]{2,1,0:T(8,128)}, f32[16,128,256]{2,1,0:T(8,128)}, f32[16,128,128]{2,1,0:T(8,128)}, f32[16,128,256]{2,1,0:T(8,128)}, f32[16,128,128]{2,1,0:T(8,128)}, /*index=5*/f32[4,128,8]{2,1,0:T(8,128)}) custom-call(s32[96]{0:T(128)} %reshape.127.pick_ref, s32[1]{0:T(128)} %bitcast.4.where_ref, bf16[128,2048]{1,0:T(8,128)(2,1)} %query_ref.7, ...), custom_call_target="tpu_custom_call" | custom-call | flops 600000000 | bytes 16777216 | tf_op jit(solution)/shard_map/near/pallas_call | solution.py:260
  142.4 5.7 %all-to-all-done.1.ends_ref = bf16[16,2,2,64,128]{4,3,2,1,0:T(8,128)(2,1)S(1)} async-done(((bf16[16,2,2,64,128]{4,3,2,1,0:T(8,128)(2,1)}), bf16[16,2,2,64,128]{4,3,2,1,0:T(8,128)(2,1)S(1)}, u32[]{:S(2)}, u32[]{:S(2)}) %all-to-all-start.1) | async-done | bytes 1048608 | tf_op jit(solution)/shard_map/all_to_all | solution.py:572
  148.1 1.0 copy-done.1
  149.1 6.9 %ends.1 = (bf16[128,2048]{1,0:T(8,128)(2,1)}, bf16[16,128,128]{2,1,0:T(8,128)(2,1)}, f32[4,128,8]{2,1,0:T(8,128)}, bf16[16,2,2,64,128]{4,3,2,1,0:T(8,128)(2,1)}) custom-call(s32[1]{0:T(128)} %bitcast.4.where_ref, bf16[128,2048]{1,0:T(8,128)(2,1)} %query_ref.7, bf16[128,2048]{1,0:T(8,128)(2,1)} %grad_ref.7, f32[16,128,128]{2,1,0:T(8,128)} %get-tuple-element.55.part_ref, ...), custom_call_target="tpu_custom_call" | custom-call | flops 400000000 | bytes 8388608 | tf_op jit(solution)/shard_map/ends/pallas_call | solution.py:327
  156.0 5.5 %all-to-all-start.2 = ((bf16[16,2,2,64,128]{4,3,2,1,0:T(8,128)(2,1)}), bf16[16,2,2,64,128]{4,3,2,1,0:T(8,128)(2,1)S(1)}, u32[]{:S(2)}, u32[]{:S(2)}) async-start(bf16[16,2,2,64,128]{4,3,2,1,0:T(8,128)(2,1)} %get-tuple-element.66), calls=%async_computation.2 | async-start | bytes 2097152 | tf_op jit(solution)/shard_map/all_to_all | solution.py:572
  161.5 7.3 %far_terms.1 = (bf16[128,2,64,128]{3,2,1,0:T(8,128)(2,1)}, bf16[2,64,2048]{2,1,0:T(8,128)(2,1)}, bf16[2,64,2048]{2,1,0:T(8,128)(2,1)}) custom-call(s32[96]{0:T(128)} %reshape.127.pick_ref, bf16[128,2048]{1,0:T(8,128)(2,1)} %query_ref.7, bf16[128,2048]{1,0:T(8,128)(2,1)} %grad_ref.7, f32[16,128,256]{2,1,0:T(8,128)} %get-tuple-element.59.far_exp_ref.exp_ref, ...), custom_call_target="tpu_custom_call" | custom-call | flops 400000000 | bytes 14680064 | tf_op jit(solution)/shard_map/far_terms/pallas_call | solution.py:396
  168.7 6.7 %all-to-all-done.2 = bf16[16,2,2,64,128]{4,3,2,1,0:T(8,128)(2,1)S(1)} async-done(((bf16[16,2,2,64,128]{4,3,2,1,0:T(8,128)(2,1)}), bf16[16,2,2,64,128]{4,3,2,1,0:T(8,128)(2,1)S(1)}, u32[]{:S(2)}, u32[]{:S(2)}) %all-to-all-start.2) | async-done | bytes 1048608 | tf_op jit(solution)/shard_map/all_to_all | solution.py:572
  175.4 0.2 reduce_sum.42
  175.6 0.6 slice_dynamic-update-slice_fusion.1
  176.2 0.6 slice_dynamic-update-slice_fusion
  176.8 11.0 %all-to-all-start.3 = ((bf16[128,2,64,128]{3,2,1,0:T(8,128)(2,1)}), bf16[128,2,64,128]{3,2,1,0:T(8,128)(2,1)}, u32[]{:S(2)}, u32[]{:S(2)}) async-start(bf16[128,2,64,128]{3,2,1,0:T(8,128)(2,1)} %slice_dynamic-update-slice_fusion), calls=%async_computation.3 | async-start | bytes 8388608 | tf_op jit(solution)/shard_map/all_to_all | solution.py:618
  187.9 3.4 %collective-permute-start.2 = (bf16[2,64,2048]{2,1,0:T(8,128)(2,1)S(1)}, bf16[2,64,2048]{2,1,0:T(8,128)(2,1)S(1)}, u32[]{:S(2)}, u32[]{:S(2)}) collective-permute-start(bf16[2,64,2048]{2,1,0:T(8,128)(2,1)S(1)} %copy-done.8), channel_id=1, source_target_pairs={{0,2},{2,4},{4,6},{6,8},{8,10},{10,12},{12,14},{14,16},{16,18},{18... | collective-permute-start | bytes 1572872 | tf_op jit(solution)/shard_map/ppermute | solution.py:544
  191.2 0.0 copy-done.7
  191.3 6.7 %collective-permute-start.3 = (bf16[2,64,2048]{2,1,0:T(8,128)(2,1)S(1)}, bf16[2,64,2048]{2,1,0:T(8,128)(2,1)S(1)}, u32[]{:S(2)}, u32[]{:S(2)}) collective-permute-start(bf16[2,64,2048]{2,1,0:T(8,128)(2,1)S(1)} %copy-done.7), channel_id=1, source_target_pairs={{2,0},{4,2},{6,4},{8,6},{10,8},{12,10},{14,12},{16,14},{18,16},{20... | collective-permute-start | bytes 1572872 | tf_op jit(solution)/shard_map/ppermute | solution.py:544
  198.0 0.1 convert_reduce_fusion.1.begin_ref
  198.1 0.2 convert_reduce_fusion
  198.2 0.1 select_reduce_fusion.order_ref
  198.4 10.1 %own_terms.1 = (bf16[128,2048]{1,0:T(8,128)(2,1)}, f32[2,128,2048]{2,1,0:T(8,128)}) custom-call(s32[96]{0:T(128)} %reshape.127.pick_ref, bf16[128,2048]{1,0:T(8,128)(2,1)} %query_ref.7, bf16[128,2048]{1,0:T(8,128)(2,1)} %grad_ref.7, bf16[128,2048]{1,0:T(8,128)(2,1)} %key_ref.5, bf16[128,2,64,128]{3,2,1,0:T(8,128)(2,1)} %all-to-all-done.far_ref.first_ref.last_ref, ...), custom_call_target="tpu_custom_call" | custom-call | flops 500000000 | bytes 16777216 | tf_op jit(solution)/shard_map/own_terms/pallas_call | solution.py:459
  208.5 83.4 %collective-permute-done.2.low_ref = bf16[2,64,2048]{2,1,0:T(8,128)(2,1)S(1)} collective-permute-done((bf16[2,64,2048]{2,1,0:T(8,128)(2,1)S(1)}, bf16[2,64,2048]{2,1,0:T(8,128)(2,1)S(1)}, u32[]{:S(2)}, u32[]{:S(2)}) %collective-permute-start.2) | collective-permute-done | bytes 524320 | tf_op jit(solution)/shard_map/ppermute | solution.py:544
  291.9 0.0 collective-permute-done.3.high_ref
  291.9 0.0 all-to-all-done.3.terms_ref
  291.9 1.6 copy-done
  293.5 4.9 %gather.1 = (bf16[128,2048]{1,0:T(8,128)(2,1)}, bf16[128,2048]{1,0:T(8,128)(2,1)}) custom-call(s32[128]{0:T(128)S(1)} %select_reduce_fusion.order_ref, s32[33]{0:T(128)S(1)} %convert_reduce_fusion.1.begin_ref, bf16[128,2,64,128]{3,2,1,0:T(8,128)(2,1)} %all-to-all-done.3.terms_ref, f32[2,128,2048]{2,1,0:T(8,128)S(1)} %copy-done, ...), custom_call_target="tpu_custom_call" | custom-call | flops 1000000 | bytes 9437184 | tf_op jit(solution)/shard_map/gather/pallas_call | solution.py:523
  (10 shorter events, 0.0 us)
Async XLA Ops:
  5.5 16.5 %copy-start.2 = (bf16[128,2048]{1,0:T(8,128)(2,1)S(1)}, bf16[128,2048]{1,0:T(8,128)(2,1)}, u32[]{:S(2)}) copy-start(bf16[128,2048]{1,0:T(8,128)(2,1)} %key_ref.5) | copy-start | bytes 1572868
  5.5 16.5 %copy-start.3 = (bf16[128,2048]{1,0:T(8,128)(2,1)S(1)}, bf16[128,2048]{1,0:T(8,128)(2,1)}, u32[]{:S(2)}) copy-start(bf16[128,2048]{1,0:T(8,128)(2,1)} %value_ref.3) | copy-start | bytes 1572868
  5.5 121.7 %all-to-all-start = ((bf16[128,2,64,128]{3,2,1,0:T(8,128)(2,1)}), bf16[128,2,64,128]{3,2,1,0:T(8,128)(2,1)}, u32[]{:S(2)}, u32[]{:S(2)}) async-start(bf16[128,2,64,128]{3,2,1,0:T(8,128)(2,1)} %pack.1), calls=%async_computation | async-start | bytes 8388608 | tf_op jit(solution)/shard_map/all_to_all | solution.py:602
  22.1 10.3 %copy-start.6 = (s32[256,16,3]{0,1,2:T(8,128)S(1)}, s32[256,16,3]{0,1,2:T(8,128)}, u32[]{:S(2)}) copy-start(s32[256,16,3]{0,1,2:T(8,128)} %param.13) | copy-start | bytes 147460
  22.2 105.0 %collective-permute-start = (bf16[2,64,2048]{2,1,0:T(8,128)(2,1)S(1)}, bf16[2,64,2048]{2,1,0:T(8,128)(2,1)S(1)}, u32[]{:S(2)}, u32[]{:S(2)}) collective-permute-start(bf16[2,64,2048]{2,1,0:T(8,128)(2,1)S(1)} %pad_maximum_fusion), channel_id=1, source_target_pairs={{0,2},{2,4},{4,6},{6,8},{8,10},{10,12},{12,14},{14,16},{16,18},{18... | collective-permute-start | bytes 1572872 | tf_op jit(solution)/shard_map/ppermute | solution.py:544
  25.7 101.6 %collective-permute-start.1 = (bf16[2,64,2048]{2,1,0:T(8,128)(2,1)S(1)}, bf16[2,64,2048]{2,1,0:T(8,128)(2,1)S(1)}, u32[]{:S(2)}, u32[]{:S(2)}) collective-permute-start(bf16[2,64,2048]{2,1,0:T(8,128)(2,1)S(1)} %pad_maximum_fusion.1), channel_id=1, source_target_pairs={{2,0},{4,2},{6,4},{8,6},{10,8},{12,10},{14,12},{16,14},{18,16},{20... | collective-permute-start | bytes 1572872 | tf_op jit(solution)/shard_map/ppermute | solution.py:544
  127.2 2.0 copy-start.4
  127.2 2.0 copy-start.5
  129.3 18.9 %all-to-all-start.1 = ((bf16[16,2,2,64,128]{4,3,2,1,0:T(8,128)(2,1)}), bf16[16,2,2,64,128]{4,3,2,1,0:T(8,128)(2,1)S(1)}, u32[]{:S(2)}, u32[]{:S(2)}) async-start(bf16[16,2,2,64,128]{4,3,2,1,0:T(8,128)(2,1)} %repeat_ends.1), calls=%async_computation.1 | async-start | bytes 2097152 | tf_op jit(solution)/shard_map/all_to_all | solution.py:572
  148.1 1.0 copy-start.1
  156.0 19.4 %all-to-all-start.2 = ((bf16[16,2,2,64,128]{4,3,2,1,0:T(8,128)(2,1)}), bf16[16,2,2,64,128]{4,3,2,1,0:T(8,128)(2,1)S(1)}, u32[]{:S(2)}, u32[]{:S(2)}) async-start(bf16[16,2,2,64,128]{4,3,2,1,0:T(8,128)(2,1)} %get-tuple-element.66), calls=%async_computation.2 | async-start | bytes 2097152 | tf_op jit(solution)/shard_map/all_to_all | solution.py:572
  176.8 11.0 %copy-start.8 = (bf16[2,64,2048]{2,1,0:T(8,128)(2,1)S(1)}, bf16[2,64,2048]{2,1,0:T(8,128)(2,1)}, u32[]{:S(2)}) copy-start(bf16[2,64,2048]{2,1,0:T(8,128)(2,1)} %get-tuple-element.68) | copy-start | bytes 1572868
  176.8 14.4 %copy-start.7 = (bf16[2,64,2048]{2,1,0:T(8,128)(2,1)S(1)}, bf16[2,64,2048]{2,1,0:T(8,128)(2,1)}, u32[]{:S(2)}) copy-start(bf16[2,64,2048]{2,1,0:T(8,128)(2,1)} %get-tuple-element.69) | copy-start | bytes 1572868
  176.8 115.1 %all-to-all-start.3 = ((bf16[128,2,64,128]{3,2,1,0:T(8,128)(2,1)}), bf16[128,2,64,128]{3,2,1,0:T(8,128)(2,1)}, u32[]{:S(2)}, u32[]{:S(2)}) async-start(bf16[128,2,64,128]{3,2,1,0:T(8,128)(2,1)} %slice_dynamic-update-slice_fusion), calls=%async_computation.3 | async-start | bytes 8388608 | tf_op jit(solution)/shard_map/all_to_all | solution.py:618
  187.9 104.0 %collective-permute-start.2 = (bf16[2,64,2048]{2,1,0:T(8,128)(2,1)S(1)}, bf16[2,64,2048]{2,1,0:T(8,128)(2,1)S(1)}, u32[]{:S(2)}, u32[]{:S(2)}) collective-permute-start(bf16[2,64,2048]{2,1,0:T(8,128)(2,1)S(1)} %copy-done.8), channel_id=1, source_target_pairs={{0,2},{2,4},{4,6},{6,8},{8,10},{10,12},{12,14},{14,16},{16,18},{18... | collective-permute-start | bytes 1572872 | tf_op jit(solution)/shard_map/ppermute | solution.py:544
  191.3 100.6 %collective-permute-start.3 = (bf16[2,64,2048]{2,1,0:T(8,128)(2,1)S(1)}, bf16[2,64,2048]{2,1,0:T(8,128)(2,1)S(1)}, u32[]{:S(2)}, u32[]{:S(2)}) collective-permute-start(bf16[2,64,2048]{2,1,0:T(8,128)(2,1)S(1)} %copy-done.7), channel_id=1, source_target_pairs={{2,0},{4,2},{6,4},{8,6},{10,8},{12,10},{14,12},{16,14},{18,16},{20... | collective-permute-start | bytes 1572872 | tf_op jit(solution)/shard_map/ppermute | solution.py:544
  291.9 1.6 copy-start

commit v9 on v8

--- a/solution.py
+++ b/solution.py
@@ -484,28 +484,34 @@
 
 
 def gather_kernel(
-    order_ref, begin_ref, terms_ref, own_ref, low_ref, high_ref, key_ref, value_ref
+    order_ref, begin_ref, terms_ref, own_ref, low_ref, high_ref, key_ref, value_ref, total_ref
 ):
     edges = (low_ref, high_ref)
+    places = [(block, head) for block in range(2) for head in range(HEADS)]
+
+    def term(place):
+        return terms_ref[order_ref[place], 0].astype(F32)
 
     def one_side(out_ref):
-        for block in range(2):
-            for head in range(HEADS):
-                item = block * HEADS + head
-                at = columns_of(head)
-                begin, end = begin_ref[item], begin_ref[item + 1]
-
-                def term(place):
-                    return terms_ref[order_ref[place], 0].astype(F32)
-
-                total = own_ref[0, HALVES[block], at] + edges[block][0, :, at].astype(F32)
-                for i in range(USUAL):
-                    found = term(jnp.minimum(begin + i, SHARDS - 1))
-                    total = total + jnp.where(begin + i < end, found, 0.0)
-                total = lax.fori_loop(
-                    jnp.minimum(begin + USUAL, end), end, lambda p, sums: sums + term(p), total
-                )
-                out_ref[HALVES[block], at] = total.astype(BF16)
+        for item, (block, head) in enumerate(places):
+            at = columns_of(head)
+            begin, end = begin_ref[item], begin_ref[item + 1]
+            total = own_ref[0, HALVES[block], at] + edges[block][0, :, at].astype(F32)
+            for i in range(USUAL):
+                found = term(jnp.minimum(begin + i, SHARDS - 1))
+                total = total + jnp.where(begin + i < end, found, 0.0)
+            total_ref[item] = total
+
+        def more(item, carry):
+            def add(place, carry):
+                total_ref[item] += term(place)
+                return carry
+
+            return lax.fori_loop(begin_ref[item] + USUAL, begin_ref[item + 1], add, carry)
+
+        lax.fori_loop(0, 2 * HEADS, more, 0)
+        for item, (block, head) in enumerate(places):
+            out_ref[HALVES[block], columns_of(head)] = total_ref[item].astype(BF16)
 
     for side, out_ref in enumerate((key_ref, value_ref)):
         pl.when(pl.program_id(0) == side)(lambda out_ref=out_ref: one_side(out_ref))
@@ -532,6 +538,7 @@
                 side_spec(BLOCK),
             ],
             out_specs=[flat_whole, flat_whole],
+            scratch_shapes=[pltpu.VMEM((2 * HEADS, BLOCK, DH), F32)],
         ),
         out_shape=[flat, flat],
         compiler_params=params(16 * 2**20),

time: 300 us -> 300 us (level)
  no operation moved by 1% of the time
where the time goes in v9:
time: 300 us; the launch traced here: 299 us
  waiting for transfers between devices  190 us (63%)
  starting transfers between devices  57.9 us (19%)
  Pallas kernels  43.2 us (14%)
  local copies, waits for them, and re-layouts  4.9 us (2%)
    ppermute x4, waiting for transfers between devices, send(): return lax.ppermute(value, 'seq', route)  177 us
    ppermute x4, starting transfers between devices, send(): return lax.ppermute(value, 'seq', route)  20.1 us
    all_to_all x1, starting transfers between devices, on_device(): far = lax.all_to_all(slots, 'seq', split_axis=0, concat_axis=0, tiled=True)  16.5 us
    all_to_all x2, waiting for transfers between devices, swap_in_plane(): lax.all_to_all(pieces, 'seq', split_axis=0, concat_axis=0, tiled=True, ax...  12.4 us
    all_to_all x1, starting transfers between devices, on_device(): back = lax.all_to_all(terms, 'seq', split_axis=0, concat_axis=0, tiled=True)  11 us
    all_to_all x2, starting transfers between devices, swap_in_plane(): lax.all_to_all(pieces, 'seq', split_axis=0, concat_axis=0, tiled=True, ax...  10.3 us
    pallas_call x1, Pallas kernels, own_terms(): grid_call(own_terms_kernel, 'own_terms', 5 * 10 ** 8, 16 * 2 ** 20, 1, [f...  10.1 us
    pallas_call x1, Pallas kernels, near(): grid_call(near_kernel, 'near', 6 * 10 ** 8, 16 * 2 ** 20, 2, [flat_spec(s...  8.37 us
  transfers between devices with their start and end apart: 8, of which 4 were waited for; matrix products, arithmetic and copies ran while one was open for 0% of the time, Pallas kernels for 9%

profile of v9, /device:TPU:6, one launch (start us, length us, event | category | flops | bytes accessed | tf_op | source)
XLA Modules:
  0.0 298.9 jit_solution(3561364452169209021)
XLA Ops:
  0.6 0.9 fusion.6
  1.5 0.1 reshape.126
  1.7 0.1 reduce_max.19
  1.8 0.5 broadcast_maximum_fusion.item_ref
  2.3 3.2 %pack.1 = bf16[128,2,64,128]{3,2,1,0:T(8,128)(2,1)} custom-call(s32[128]{0:T(128)} %broadcast_maximum_fusion.item_ref, bf16[128,2048]{1,0:T(8,128)(2,1)} %key_ref.5, bf16[128,2048]{1,0:T(8,128)(2,1)} %value_ref.3), custom_call_target="tpu_custom_call" | custom-call | bytes 6291456 | tf_op jit(solution)/shard_map/pack/pallas_call | solution.py:80
  5.5 0.0 copy-start.2
  5.5 0.0 copy-start.3
  5.5 16.5 %all-to-all-start = ((bf16[128,2,64,128]{3,2,1,0:T(8,128)(2,1)}), bf16[128,2,64,128]{3,2,1,0:T(8,128)(2,1)}, u32[]{:S(2)}, u32[]{:S(2)}) async-start(bf16[128,2,64,128]{3,2,1,0:T(8,128)(2,1)} %pack.1), calls=%async_computation | async-start | bytes 8388608 | tf_op jit(solution)/shard_map/all_to_all | solution.py:609
  22.0 0.0 copy-done.2
  22.1 0.0 copy-done.3
  22.1 0.0 copy-start.6
  22.1 0.1 slice_bitcast_fusion
  22.2 0.1 pad_maximum_fusion
  22.2 3.4 %collective-permute-start = (bf16[2,64,2048]{2,1,0:T(8,128)(2,1)S(1)}, bf16[2,64,2048]{2,1,0:T(8,128)(2,1)S(1)}, u32[]{:S(2)}, u32[]{:S(2)}) collective-permute-start(bf16[2,64,2048]{2,1,0:T(8,128)(2,1)S(1)} %pad_maximum_fusion), channel_id=1, source_target_pairs={{0,2},{2,4},{4,6},{6,8},{8,10},{10,12},{12,14},{14,16},{16,18},{18... | collective-permute-start | bytes 1572872 | tf_op jit(solution)/shard_map/ppermute | solution.py:551
  25.6 0.1 pad_maximum_fusion.1
  25.7 6.7 %collective-permute-start.1 = (bf16[2,64,2048]{2,1,0:T(8,128)(2,1)S(1)}, bf16[2,64,2048]{2,1,0:T(8,128)(2,1)S(1)}, u32[]{:S(2)}, u32[]{:S(2)}) collective-permute-start(bf16[2,64,2048]{2,1,0:T(8,128)(2,1)S(1)} %pad_maximum_fusion.1), channel_id=1, source_target_pairs={{2,0},{4,2},{6,4},{8,6},{10,8},{12,10},{14,12},{16,14},{18,16},{20... | collective-permute-start | bytes 1572872 | tf_op jit(solution)/shard_map/ppermute | solution.py:551
  32.4 0.1 constant_dynamic-slice_fusion
  32.4 0.2 copy.11
  32.7 0.6 reshape.127.pick_ref
  33.2 94.0 %collective-permute-done.prev_ref = bf16[2,64,2048]{2,1,0:T(8,128)(2,1)S(1)} collective-permute-done((bf16[2,64,2048]{2,1,0:T(8,128)(2,1)S(1)}, bf16[2,64,2048]{2,1,0:T(8,128)(2,1)S(1)}, u32[]{:S(2)}, u32[]{:S(2)}) %collective-permute-start) | collective-permute-done | bytes 524320 | tf_op jit(solution)/shard_map/ppermute | solution.py:551
  127.2 0.0 collective-permute-done.1.next_ref
  127.2 0.0 all-to-all-done.far_ref.first_ref.last_ref
  127.3 2.0 repeat_ends.1
  129.3 0.0 copy-done.4
  129.3 4.8 %all-to-all-start.1 = ((bf16[16,2,2,64,128]{4,3,2,1,0:T(8,128)(2,1)}), bf16[16,2,2,64,128]{4,3,2,1,0:T(8,128)(2,1)S(1)}, u32[]{:S(2)}, u32[]{:S(2)}) async-start(bf16[16,2,2,64,128]{4,3,2,1,0:T(8,128)(2,1)} %repeat_ends.1), calls=%async_computation.1 | async-start | bytes 2097152 | tf_op jit(solution)/shard_map/all_to_all | solution.py:579
  134.0 8.4 %near.1 = (f32[16,128,128]{2,1,0:T(8,128)}, f32[16,128,256]{2,1,0:T(8,128)}, f32[16,128,128]{2,1,0:T(8,128)}, f32[16,128,256]{2,1,0:T(8,128)}, f32[16,128,128]{2,1,0:T(8,128)}, /*index=5*/f32[4,128,8]{2,1,0:T(8,128)}) custom-call(s32[96]{0:T(128)} %reshape.127.pick_ref, s32[1]{0:T(128)} %bitcast.4.where_ref, bf16[128,2048]{1,0:T(8,128)(2,1)} %query_ref.7, ...), custom_call_target="tpu_custom_call" | custom-call | flops 600000000 | bytes 16777216 | tf_op jit(solution)/shard_map/near/pallas_call | solution.py:260
  142.4 5.7 %all-to-all-done.1.ends_ref = bf16[16,2,2,64,128]{4,3,2,1,0:T(8,128)(2,1)S(1)} async-done(((bf16[16,2,2,64,128]{4,3,2,1,0:T(8,128)(2,1)}), bf16[16,2,2,64,128]{4,3,2,1,0:T(8,128)(2,1)S(1)}, u32[]{:S(2)}, u32[]{:S(2)}) %all-to-all-start.1) | async-done | bytes 1048608 | tf_op jit(solution)/shard_map/all_to_all | solution.py:579
  148.1 1.0 copy-done.1
  149.1 6.9 %ends.1 = (bf16[128,2048]{1,0:T(8,128)(2,1)}, bf16[16,128,128]{2,1,0:T(8,128)(2,1)}, f32[4,128,8]{2,1,0:T(8,128)}, bf16[16,2,2,64,128]{4,3,2,1,0:T(8,128)(2,1)}) custom-call(s32[1]{0:T(128)} %bitcast.4.where_ref, bf16[128,2048]{1,0:T(8,128)(2,1)} %query_ref.7, bf16[128,2048]{1,0:T(8,128)(2,1)} %grad_ref.7, f32[16,128,128]{2,1,0:T(8,128)} %get-tuple-element.55.part_ref, ...), custom_call_target="tpu_custom_call" | custom-call | flops 400000000 | bytes 8388608 | tf_op jit(solution)/shard_map/ends/pallas_call | solution.py:327
  156.0 5.5 %all-to-all-start.2 = ((bf16[16,2,2,64,128]{4,3,2,1,0:T(8,128)(2,1)}), bf16[16,2,2,64,128]{4,3,2,1,0:T(8,128)(2,1)S(1)}, u32[]{:S(2)}, u32[]{:S(2)}) async-start(bf16[16,2,2,64,128]{4,3,2,1,0:T(8,128)(2,1)} %get-tuple-element.66), calls=%async_computation.2 | async-start | bytes 2097152 | tf_op jit(solution)/shard_map/all_to_all | solution.py:579
  161.5 7.3 %far_terms.1 = (bf16[128,2,64,128]{3,2,1,0:T(8,128)(2,1)}, bf16[2,64,2048]{2,1,0:T(8,128)(2,1)}, bf16[2,64,2048]{2,1,0:T(8,128)(2,1)}) custom-call(s32[96]{0:T(128)} %reshape.127.pick_ref, bf16[128,2048]{1,0:T(8,128)(2,1)} %query_ref.7, bf16[128,2048]{1,0:T(8,128)(2,1)} %grad_ref.7, f32[16,128,256]{2,1,0:T(8,128)} %get-tuple-element.59.far_exp_ref.exp_ref, ...), custom_call_target="tpu_custom_call" | custom-call | flops 400000000 | bytes 14680064 | tf_op jit(solution)/shard_map/far_terms/pallas_call | solution.py:396
  168.7 6.6 %all-to-all-done.2 = bf16[16,2,2,64,128]{4,3,2,1,0:T(8,128)(2,1)S(1)} async-done(((bf16[16,2,2,64,128]{4,3,2,1,0:T(8,128)(2,1)}), bf16[16,2,2,64,128]{4,3,2,1,0:T(8,128)(2,1)S(1)}, u32[]{:S(2)}, u32[]{:S(2)}) %all-to-all-start.2) | async-done | bytes 1048608 | tf_op jit(solution)/shard_map/all_to_all | solution.py:579
  175.4 0.2 reduce_sum.42
  175.6 0.6 slice_dynamic-update-slice_fusion.1
  176.2 0.6 slice_dynamic-update-slice_fusion
  176.8 11.0 %all-to-all-start.3 = ((bf16[128,2,64,128]{3,2,1,0:T(8,128)(2,1)}), bf16[128,2,64,128]{3,2,1,0:T(8,128)(2,1)}, u32[]{:S(2)}, u32[]{:S(2)}) async-start(bf16[128,2,64,128]{3,2,1,0:T(8,128)(2,1)} %slice_dynamic-update-slice_fusion), calls=%async_computation.3 | async-start | bytes 8388608 | tf_op jit(solution)/shard_map/all_to_all | solution.py:625
  187.9 0.0 copy-done.8
  187.9 3.4 %collective-permute-start.2 = (bf16[2,64,2048]{2,1,0:T(8,128)(2,1)S(1)}, bf16[2,64,2048]{2,1,0:T(8,128)(2,1)S(1)}, u32[]{:S(2)}, u32[]{:S(2)}) collective-permute-start(bf16[2,64,2048]{2,1,0:T(8,128)(2,1)S(1)} %copy-done.8), channel_id=1, source_target_pairs={{0,2},{2,4},{4,6},{6,8},{8,10},{10,12},{12,14},{14,16},{16,18},{18... | collective-permute-start | bytes 1572872 | tf_op jit(solution)/shard_map/ppermute | solution.py:551
  191.3 6.7 %collective-permute-start.3 = (bf16[2,64,2048]{2,1,0:T(8,128)(2,1)S(1)}, bf16[2,64,2048]{2,1,0:T(8,128)(2,1)S(1)}, u32[]{:S(2)}, u32[]{:S(2)}) collective-permute-start(bf16[2,64,2048]{2,1,0:T(8,128)(2,1)S(1)} %copy-done.7), channel_id=1, source_target_pairs={{2,0},{4,2},{6,4},{8,6},{10,8},{12,10},{14,12},{16,14},{18,16},{20... | collective-permute-start | bytes 1572872 | tf_op jit(solution)/shard_map/ppermute | solution.py:551
  198.0 0.1 convert_reduce_fusion.1.begin_ref
  198.1 0.2 convert_reduce_fusion
  198.2 0.1 select_reduce_fusion.order_ref
  198.4 10.1 %own_terms.1 = (bf16[128,2048]{1,0:T(8,128)(2,1)}, f32[2,128,2048]{2,1,0:T(8,128)}) custom-call(s32[96]{0:T(128)} %reshape.127.pick_ref, bf16[128,2048]{1,0:T(8,128)(2,1)} %query_ref.7, bf16[128,2048]{1,0:T(8,128)(2,1)} %grad_ref.7, bf16[128,2048]{1,0:T(8,128)(2,1)} %key_ref.5, bf16[128,2,64,128]{3,2,1,0:T(8,128)(2,1)} %all-to-all-done.far_ref.first_ref.last_ref, ...), custom_call_target="tpu_custom_call" | custom-call | flops 500000000 | bytes 16777216 | tf_op jit(solution)/shard_map/own_terms/pallas_call | solution.py:459
  208.5 83.4 %collective-permute-done.2.low_ref = bf16[2,64,2048]{2,1,0:T(8,128)(2,1)S(1)} collective-permute-done((bf16[2,64,2048]{2,1,0:T(8,128)(2,1)S(1)}, bf16[2,64,2048]{2,1,0:T(8,128)(2,1)S(1)}, u32[]{:S(2)}, u32[]{:S(2)}) %collective-permute-start.2) | collective-permute-done | bytes 524320 | tf_op jit(solution)/shard_map/ppermute | solution.py:551
  291.9 0.0 collective-permute-done.3.high_ref
  291.9 0.0 all-to-all-done.3.terms_ref
  291.9 1.6 copy-done
  293.5 5.4 %gather.1 = (bf16[128,2048]{1,0:T(8,128)(2,1)}, bf16[128,2048]{1,0:T(8,128)(2,1)}) custom-call(s32[128]{0:T(128)S(1)} %select_reduce_fusion.order_ref, s32[33]{0:T(128)S(1)} %convert_reduce_fusion.1.begin_ref, bf16[128,2,64,128]{3,2,1,0:T(8,128)(2,1)} %all-to-all-done.3.terms_ref, f32[2,128,2048]{2,1,0:T(8,128)S(1)} %copy-done, ...), custom_call_target="tpu_custom_call" | custom-call | flops 1000000 | bytes 9437184 | tf_op jit(solution)/shard_map/gather/pallas_call | solution.py:529
  (10 shorter events, 0.0 us)
Async XLA Ops:
  5.5 16.5 %copy-start.2 = (bf16[128,2048]{1,0:T(8,128)(2,1)S(1)}, bf16[128,2048]{1,0:T(8,128)(2,1)}, u32[]{:S(2)}) copy-start(bf16[128,2048]{1,0:T(8,128)(2,1)} %key_ref.5) | copy-start | bytes 1572868
  5.5 16.5 %copy-start.3 = (bf16[128,2048]{1,0:T(8,128)(2,1)S(1)}, bf16[128,2048]{1,0:T(8,128)(2,1)}, u32[]{:S(2)}) copy-start(bf16[128,2048]{1,0:T(8,128)(2,1)} %value_ref.3) | copy-start | bytes 1572868
  5.5 121.7 %all-to-all-start = ((bf16[128,2,64,128]{3,2,1,0:T(8,128)(2,1)}), bf16[128,2,64,128]{3,2,1,0:T(8,128)(2,1)}, u32[]{:S(2)}, u32[]{:S(2)}) async-start(bf16[128,2,64,128]{3,2,1,0:T(8,128)(2,1)} %pack.1), calls=%async_computation | async-start | bytes 8388608 | tf_op jit(solution)/shard_map/all_to_all | solution.py:609
  22.1 10.3 %copy-start.6 = (s32[256,16,3]{0,1,2:T(8,128)S(1)}, s32[256,16,3]{0,1,2:T(8,128)}, u32[]{:S(2)}) copy-start(s32[256,16,3]{0,1,2:T(8,128)} %param.13) | copy-start | bytes 147460
  22.2 105.0 %collective-permute-start = (bf16[2,64,2048]{2,1,0:T(8,128)(2,1)S(1)}, bf16[2,64,2048]{2,1,0:T(8,128)(2,1)S(1)}, u32[]{:S(2)}, u32[]{:S(2)}) collective-permute-start(bf16[2,64,2048]{2,1,0:T(8,128)(2,1)S(1)} %pad_maximum_fusion), channel_id=1, source_target_pairs={{0,2},{2,4},{4,6},{6,8},{8,10},{10,12},{12,14},{14,16},{16,18},{18... | collective-permute-start | bytes 1572872 | tf_op jit(solution)/shard_map/ppermute | solution.py:551
  25.7 101.6 %collective-permute-start.1 = (bf16[2,64,2048]{2,1,0:T(8,128)(2,1)S(1)}, bf16[2,64,2048]{2,1,0:T(8,128)(2,1)S(1)}, u32[]{:S(2)}, u32[]{:S(2)}) collective-permute-start(bf16[2,64,2048]{2,1,0:T(8,128)(2,1)S(1)} %pad_maximum_fusion.1), channel_id=1, source_target_pairs={{2,0},{4,2},{6,4},{8,6},{10,8},{12,10},{14,12},{16,14},{18,16},{20... | collective-permute-start | bytes 1572872 | tf_op jit(solution)/shard_map/ppermute | solution.py:551
  127.2 2.0 copy-start.4
  127.2 2.0 copy-start.5
  129.3 18.9 %all-to-all-start.1 = ((bf16[16,2,2,64,128]{4,3,2,1,0:T(8,128)(2,1)}), bf16[16,2,2,64,128]{4,3,2,1,0:T(8,128)(2,1)S(1)}, u32[]{:S(2)}, u32[]{:S(2)}) async-start(bf16[16,2,2,64,128]{4,3,2,1,0:T(8,128)(2,1)} %repeat_ends.1), calls=%async_computation.1 | async-start | bytes 2097152 | tf_op jit(solution)/shard_map/all_to_all | solution.py:579
  148.1 1.0 copy-start.1
  156.0 19.4 %all-to-all-start.2 = ((bf16[16,2,2,64,128]{4,3,2,1,0:T(8,128)(2,1)}), bf16[16,2,2,64,128]{4,3,2,1,0:T(8,128)(2,1)S(1)}, u32[]{:S(2)}, u32[]{:S(2)}) async-start(bf16[16,2,2,64,128]{4,3,2,1,0:T(8,128)(2,1)} %get-tuple-element.66), calls=%async_computation.2 | async-start | bytes 2097152 | tf_op jit(solution)/shard_map/all_to_all | solution.py:579
  176.8 11.0 %copy-start.8 = (bf16[2,64,2048]{2,1,0:T(8,128)(2,1)S(1)}, bf16[2,64,2048]{2,1,0:T(8,128)(2,1)}, u32[]{:S(2)}) copy-start(bf16[2,64,2048]{2,1,0:T(8,128)(2,1)} %get-tuple-element.68) | copy-start | bytes 1572868
  176.8 14.4 %copy-start.7 = (bf16[2,64,2048]{2,1,0:T(8,128)(2,1)S(1)}, bf16[2,64,2048]{2,1,0:T(8,128)(2,1)}, u32[]{:S(2)}) copy-start(bf16[2,64,2048]{2,1,0:T(8,128)(2,1)} %get-tuple-element.69) | copy-start | bytes 1572868
  176.8 115.1 %all-to-all-start.3 = ((bf16[128,2,64,128]{3,2,1,0:T(8,128)(2,1)}), bf16[128,2,64,128]{3,2,1,0:T(8,128)(2,1)}, u32[]{:S(2)}, u32[]{:S(2)}) async-start(bf16[128,2,64,128]{3,2,1,0:T(8,128)(2,1)} %slice_dynamic-update-slice_fusion), calls=%async_computation.3 | async-start | bytes 8388608 | tf_op jit(solution)/shard_map/all_to_all | solution.py:625
  187.9 104.0 %collective-permute-start.2 = (bf16[2,64,2048]{2,1,0:T(8,128)(2,1)S(1)}, bf16[2,64,2048]{2,1,0:T(8,128)(2,1)S(1)}, u32[]{:S(2)}, u32[]{:S(2)}) collective-permute-start(bf16[2,64,2048]{2,1,0:T(8,128)(2,1)S(1)} %copy-done.8), channel_id=1, source_target_pairs={{0,2},{2,4},{4,6},{6,8},{8,10},{10,12},{12,14},{14,16},{16,18},{18... | collective-permute-start | bytes 1572872 | tf_op jit(solution)/shard_map/ppermute | solution.py:551
  191.3 100.6 %collective-permute-start.3 = (bf16[2,64,2048]{2,1,0:T(8,128)(2,1)S(1)}, bf16[2,64,2048]{2,1,0:T(8,128)(2,1)S(1)}, u32[]{:S(2)}, u32[]{:S(2)}) collective-permute-start(bf16[2,64,2048]{2,1,0:T(8,128)(2,1)S(1)} %copy-done.7), channel_id=1, source_target_pairs={{2,0},{4,2},{6,4},{8,6},{10,8},{12,10},{14,12},{16,14},{18,16},{20... | collective-permute-start | bytes 1572872 | tf_op jit(solution)/shard_map/ppermute | solution.py:551
  291.9 1.6 copy-start
